TPU v7x, 32 devices: a whole 2x2x4 slice. The times are simulated.
32 devices in a mesh: space: 4 (over x, core), code: 4 (over z), clip: 2 (over y).
Axes of the slice: x: 2, y: 2, z: 4, core: 2. Of those that a mesh axis runs over, the one named last changes fastest.
Arguments:
- soft_weights: bfloat16 [2, 256, 32, 8192], P('clip', 'space', None, 'code'), may hold values from 0.00029945374 to 0.029907227
- codebook: bfloat16 [8192, 256], P('code'), may hold values from -6 to 6
- kernel_one: bfloat16 [3, 3, 256, 512], replicated, may hold values from -0.125 to 0.125
- kernel_two: bfloat16 [3, 3, 512, 512], replicated, may hold values from -0.09375 to 0.09375
- cotangent: bfloat16 [2, 256, 32, 512], P('clip', ('space', 'code')), may hold values from -6 to 6
Outputs:
- decoded: bfloat16 [2, 256, 32, 512], P('clip', ('space', 'code'))
- grad_one: float32 [3, 3, 256, 512], P(None, None, None, ('space', 'code', 'clip'))
- grad_two: float32 [3, 3, 512, 512], P(None, None, None, ('space', 'code', 'clip'))
- grad_codebook: float32 [8192, 256], P('code')
All inputs are finite; a program needn't handle non-finite values.
Results may differ from a plain program's by a relative error of at most 0.02.
Values may be sent and summed in bfloat16 or wider, within the bound.
No kernel may reach another device: no remote copies, remote signals or barrier semaphores. Data moves between devices by JAX's collectives and lax.ppermute only.
A program may use at most 192 MiB of HBM per device.

v0:
```python
import jax
import jax.numpy as jnp
from jax import lax
from jax.sharding import PartitionSpec as P


def with_halo(block, sides, width):
    for axis, dim in sides:
        count = lax.axis_size(axis)
        forward = [(i, i + 1) for i in range(count - 1)]
        backward = [(target, source) for source, target in forward]
        low = lax.ppermute(
            lax.slice_in_dim(block, block.shape[dim] - width, None, axis=dim), axis, forward
        )
        high = lax.ppermute(lax.slice_in_dim(block, 0, width, axis=dim), axis, backward)
        block = jnp.concatenate([low, block, high], axis=dim)
    return block


def extend(field):
    grown = with_halo(field, ((("space", "code"), 0),), 1)
    return jnp.pad(grown, ((0, 0), (1, 1), (0, 0)))


def taps_forward(padded, kernel):
    height = padded.shape[0] - 2
    breadth = padded.shape[1] - 2
    accum = jnp.zeros((height * breadth, kernel.shape[3]), jnp.float32)
    for first in range(3):
        for second in range(3):
            window = padded[first : first + height, second : second + breadth].reshape(
                height * breadth, -1
            )
            accum = accum + jnp.dot(
                window, kernel[first, second], preferred_element_type=jnp.float32
            )
    return accum.reshape(height, breadth, -1)


def taps_back(padded, kernel):
    height = padded.shape[0] - 2
    breadth = padded.shape[1] - 2
    accum = jnp.zeros((height * breadth, kernel.shape[2]), jnp.float32)
    for first in range(3):
        for second in range(3):
            window = padded[
                2 - first : 2 - first + height, 2 - second : 2 - second + breadth
            ].reshape(height * breadth, -1)
            accum = accum + jnp.dot(
                window, kernel[first, second].T, preferred_element_type=jnp.float32
            )
    return accum.reshape(height, breadth, -1)


def kernel_grad(padded, upstream):
    height = upstream.shape[0]
    breadth = upstream.shape[1]
    flat_up = upstream.reshape(height * breadth, -1)
    result = []
    for first in range(3):
        line = []
        for second in range(3):
            window = padded[first : first + height, second : second + breadth].reshape(
                height * breadth, -1
            )
            line.append(
                lax.dot_general(
                    window, flat_up, (((0,), (0,)), ((), ())), preferred_element_type=jnp.float32
                )
            )
        result.append(jnp.stack(line))
    return jnp.stack(result)


def on_device(soft_weights, codebook, kernel_one, kernel_two, cotangent):
    weights = soft_weights[0]
    upstream = cotangent[0]
    own_rows = upstream.shape[0]
    breadth = weights.shape[1]
    code_slice = weights.shape[2]
    partial_value = jnp.dot(
        weights.reshape(-1, code_slice), codebook, preferred_element_type=jnp.float32
    )
    partial_value = partial_value.reshape(weights.shape[0], breadth, -1)
    summed = lax.psum(partial_value, "code")
    owned = lax.dynamic_slice_in_dim(summed, lax.axis_index("code") * own_rows, own_rows, 0)
    embedded = owned.astype(jnp.bfloat16)
    embed_pad = extend(embedded)
    pre_one = taps_forward(embed_pad, kernel_one)
    hidden = jax.nn.silu(pre_one).astype(jnp.bfloat16)
    hidden_pad = extend(hidden)
    decoded = taps_forward(hidden_pad, kernel_two).astype(jnp.bfloat16)
    grad_hidden = taps_back(extend(upstream), kernel_two)
    sigma = jax.nn.sigmoid(pre_one)
    grad_pre = (grad_hidden * sigma * (1.0 + pre_one * (1.0 - sigma))).astype(jnp.bfloat16)
    grad_embedded = taps_back(extend(grad_pre), kernel_one).astype(jnp.bfloat16)
    piece = lax.all_gather(grad_embedded, "code", axis=0, tiled=True)
    code_terms = lax.dot_general(
        weights.reshape(-1, code_slice),
        piece.reshape(-1, piece.shape[2]),
        (((0,), (0,)), ((), ())),
        preferred_element_type=jnp.float32,
    )
    grad_codebook = lax.psum(code_terms.astype(jnp.bfloat16), ("space", "clip")).astype(jnp.float32)
    term_two = kernel_grad(hidden_pad, upstream)
    term_one = kernel_grad(embed_pad, grad_pre)
    grad_one, grad_two = (
        lax.psum_scatter(term_one, ("space", "code", "clip"), scatter_dimension=3, tiled=True),
        lax.psum_scatter(term_two, ("space", "code", "clip"), scatter_dimension=3, tiled=True),
    )
    return (decoded[None], grad_one, grad_two, grad_codebook)


def solution(mesh):
    in_specs = (
        P("clip", "space", None, "code"),
        P("code", None),
        P(),
        P(),
        P("clip", ("space", "code"), None, None),
    )
    out_specs = (
        P("clip", ("space", "code"), None, None),
        P(None, None, None, ("space", "code", "clip")),
        P(None, None, None, ("space", "code", "clip")),
        P("code", None),
    )
    return jax.shard_map(
        on_device, mesh=mesh, in_specs=in_specs, out_specs=out_specs, check_vma=False
    )
```

profile of v0, /device:TPU:9, one launch (start us, length us, event | category | flops | bytes accessed | tf_op | source)
XLA Modules:
  0.0 568.8 jit_solution(3390030245918410898)
XLA Ops:
  7.2 1.2 copy-done
  8.4 5.7 %fusion = f32[64,32,256]{2,1,0:T(8,128)S(1)} fusion(bf16[1,64,32,2048]{3,2,1,0:T(8,128)(2,1)} %param.5, bf16[2048,256]{1,0:T(8,128)(2,1)S(1)} %copy-done), kind=kOutput, calls=%fused_computation.1 | convolution fusion | flops 2147483648 | bytes 11534336 | tf_op jit(solution)/shard_map/dot_general | solution.py:81
  14.1 72.5 %all-reduce.14 = bf16[64,32,256]{2,1,0:T(8,128)(2,1)} all-reduce(f32[64,32,256]{2,1,0:T(8,128)S(1)} %fusion), channel_id=1, replica_groups=mesh['space'=4,'code'=4,'clip'=2] {'code'}, use_global_device_ids=true, to_apply=%region_0.0 | all-reduce | flops 524288 | bytes 3145728 | tf_op jit(solution)/shard_map/psum | solution.py:85
  86.6 1.1 dynamic-slice_convert_fusion
  87.8 5.2 collective-permute-start
  93.0 1.9 collective-permute-start.1
  95.0 3.4 collective-permute-start.4
  98.3 4.0 collective-permute-start.5
  105.5 1.5 convolution_bitcast_fusion.4
  107.3 0.5 fusion.113
  107.8 0.6 slice-done
  108.7 0.5 fusion.30
  109.3 0.5 convolution_add_fusion.6
  109.8 0.5 convolution_add_fusion.5
  110.2 0.5 convolution_add_fusion.4
  110.7 0.5 convolution_add_fusion.3
  111.2 0.5 fusion.12
  111.7 0.5 convolution_add_fusion.2
  112.1 0.5 convolution_add_fusion.1
  112.6 0.5 fusion.4
  113.1 0.5 multiply_convert_fusion.1
  113.7 0.7 fusion.115
  116.6 0.6 fusion.116
  117.3 4.9 collective-permute-start.2
  122.2 2.4 collective-permute-start.3
  124.6 6.1 %collective-permute-start.6 = (bf16[1,32,512]{2,1,0:T(8,128)(2,1)}, bf16[1,32,512]{2,1,0:T(8,128)(2,1)S(1)}, u32[]{:S(2)}, u32[]{:S(2)}) collective-permute-start(bf16[1,32,512]{2,1,0:T(8,128)(2,1)} %get-tuple-element.36), channel_id=1, source_target_pairs={{0,2},{2,4},{4,6},{6,8},{8,10},{10,12},{12,14},{14,16},{16,18},{18... | collective-permute-start | bytes 98312 | tf_op jit(solution)/shard_map/ppermute | solution.py:12
  130.7 2.1 collective-permute-start.7
  134.0 2.7 pad_maximum_fusion.1
  136.7 7.3 %copy.12 = f32[3,3,256,512]{2,1,0,3:T(4,128)} copy(f32[3,3,256,512]{3,2,1,0:T(8,128)} %pad_maximum_fusion.1) | data formatting | bytes 9437184 | tf_op jit(solution)/shard_map/stack | solution.py:72
  144.2 2.0 fusion.114
  146.4 0.5 fusion.112
  148.9 0.6 convolution_add_fusion.24
  150.5 1.1 fusion.9
  151.7 0.5 convolution_bitcast_fusion.7
  152.2 1.4 convolution_bitcast_fusion.1
  153.7 0.5 convolution_bitcast_fusion.3
  154.2 1.4 convolution_bitcast_fusion.2
  156.1 0.5 convolution_bitcast_fusion.6
  156.6 0.5 convolution_bitcast_fusion.8
  157.2 1.4 convolution_bitcast_fusion
  158.6 3.4 maximum_bitcast_fusion
  162.0 24.2 %all-gather.2.cloned.1.call-done = bf16[64,32,256]{2,1,0:T(8,128)(2,1)} async-done(((bf16[16,32,256]{2,1,0:T(8,128)(2,1)}), bf16[64,32,256]{2,1,0:T(8,128)(2,1)}) %all-gather.2.cloned.1.call-update) | async-done | bytes 1048592 | tf_op jit(solution)/shard_map/all_gather | solution.py:97
  186.2 7.0 %fusion.2 = bf16[2048,256]{0,1:T(8,128)(2,1)} fusion(bf16[2048,256]{1,0:T(8,128)(2,1)} %bitcast.297, bf16[2048,2048]{1,0:T(8,128)(2,1)} %bitcast.275), kind=kOutput, calls=%fused_computation.8 | convolution fusion | flops 2148007936 | bytes 10485760 | tf_op jit(solution)/shard_map/dot_general | solution.py:98
  193.5 2.3 maximum_bitcast_fusion.2
  195.9 0.5 copy-done.3
  196.3 1.0 copy-done.4
  197.3 4.7 pad_maximum_fusion
  202.0 13.8 %copy.13 = f32[3,3,512,512]{2,1,0,3:T(4,128)} copy(f32[3,3,512,512]{3,2,1,0:T(8,128)} %pad_maximum_fusion) | data formatting | bytes 18874368 | tf_op jit(solution)/shard_map/stack | solution.py:72
  215.9 1.7 fusion.32
  217.6 1.5 fusion.14
  219.1 1.5 convolution_add_fusion.13
  220.6 1.5 convolution_add_fusion.12
  222.1 1.6 convolution_add_fusion.11
  223.7 1.5 convolution_add_fusion.10
  225.2 1.5 convolution_add_fusion.9
  226.7 1.5 convolution_add_fusion.8
  228.2 2.4 fusion.7
  230.6 18.1 %all-reduce.11.cloned.1.call-done = bf16[2048,256]{0,1:T(8,128)(2,1)} async-done(((bf16[2048,256]{0,1:T(8,128)(2,1)}), bf16[2048,256]{0,1:T(8,128)(2,1)}) %all-reduce.11.cloned.1.call-update) | async-done | bytes 1048592 | tf_op jit(solution)/shard_map/psum | solution.py:104
  248.7 2.6 copy.16
  251.3 307.5 %all-reduce.13.cloned.1.call-done = (f32[3,3,256,512]{2,1,0,3:T(4,128)}, f32[3,3,512,512]{2,1,0,3:T(4,128)}) async-done(((f32[3,3,256,512]{2,1,0,3:T(4,128)}, f32[3,3,512,512]{2,1,0,3:T(4,128)}), (f32[3,3,256,512]{2,1,0,3:T(4,128)}, f32[3,3,512,512]{2,1,0,3:T(4,128)})) %all-reduce.13.cloned.1.call-update) | async-done | bytes 14155792
  558.7 1.0 constant_dynamic-slice_fusion.1
  559.7 1.1 constant_dynamic-slice_fusion
  560.8 0.8 copy.15
  561.6 0.7 copy.14
  (104 shorter events, 11.6 us)
Async XLA Ops:
  7.2 1.2 copy-start
  7.2 179.0 %all-gather.2.cloned.1.call-start = ((), (), s32[]{:S(2)}) async-start(), calls=%async_computation | async-start | bytes 1310720 | tf_op jit(solution)/shard_map/all_gather | solution.py:97
  14.1 80.8 %copy-start.2 = (bf16[1,16,32,512]{3,2,1,0:T(8,128)(2,1)S(1)}, bf16[1,16,32,512]{3,2,1,0:T(8,128)(2,1)}, u32[]{:S(2)}) copy-start(bf16[1,16,32,512]{3,2,1,0:T(8,128)(2,1)} %param.9) | copy-start | bytes 1572868
  86.6 16.1 %copy-start.5 = (bf16[3,3,256,512]{3,2,1,0:T(8,128)(2,1)S(1)}, bf16[3,3,256,512]{3,2,1,0:T(8,128)(2,1)}, u32[]{:S(2)}) copy-start(bf16[3,3,256,512]{3,2,1,0:T(8,128)(2,1)} %param.7) | copy-start | bytes 7077892
  87.8 14.5 %collective-permute-start = (bf16[1,32,256]{2,1,0:T(8,128)(2,1)S(1)}, bf16[1,32,256]{2,1,0:T(8,128)(2,1)S(1)}, u32[]{:S(2)}, u32[]{:S(2)}) collective-permute-start(bf16[1,32,256]{2,1,0:T(8,128)(2,1)S(1)} %get-tuple-element.54), channel_id=1, source_target_pairs={{0,2},{2,4},{4,6},{6,8},{8,10},{10,12},{12,14},{14,16},{16,18},{18... | collective-permute-start | bytes 49160 | tf_op jit(solution)/shard_map/ppermute | solution.py:12
  93.0 9.3 %collective-permute-start.1 = (bf16[1,32,256]{2,1,0:T(8,128)(2,1)S(1)}, bf16[1,32,256]{2,1,0:T(8,128)(2,1)S(1)}, u32[]{:S(2)}, u32[]{:S(2)}) collective-permute-start(bf16[1,32,256]{2,1,0:T(8,128)(2,1)S(1)} %get-tuple-element.55), channel_id=1, source_target_pairs={{2,0},{4,2},{6,4},{8,6},{10,8},{12,10},{14,12},{16,14},{18,16},{20... | collective-permute-start | bytes 49160 | tf_op jit(solution)/shard_map/ppermute | solution.py:15
  95.0 12.1 %collective-permute-start.4 = (bf16[1,32,512]{2,1,0:T(8,128)(2,1)S(1)}, bf16[1,32,512]{2,1,0:T(8,128)(2,1)S(1)}, u32[]{:S(2)}, u32[]{:S(2)}) collective-permute-start(bf16[1,32,512]{2,1,0:T(8,128)(2,1)S(1)} %get-tuple-element.40), channel_id=1, source_target_pairs={{0,2},{2,4},{4,6},{6,8},{8,10},{10,12},{12,14},{14,16},{16,18},{18... | collective-permute-start | bytes 98312 | tf_op jit(solution)/shard_map/ppermute | solution.py:12
  98.3 8.7 %collective-permute-start.5 = (bf16[1,32,512]{2,1,0:T(8,128)(2,1)S(1)}, bf16[1,32,512]{2,1,0:T(8,128)(2,1)S(1)}, u32[]{:S(2)}, u32[]{:S(2)}) collective-permute-start(bf16[1,32,512]{2,1,0:T(8,128)(2,1)S(1)} %get-tuple-element.41), channel_id=1, source_target_pairs={{2,0},{4,2},{6,4},{8,6},{10,8},{12,10},{14,12},{16,14},{18,16},{20... | collective-permute-start | bytes 98312 | tf_op jit(solution)/shard_map/ppermute | solution.py:15
  105.5 7.7 %copy-start.19 = (f32[512,512]{1,0:T(8,128)}, f32[512,512]{1,0:T(8,128)S(1)}, u32[]{:S(2)}) copy-start(f32[512,512]{1,0:T(8,128)S(1)} %fusion.6) | copy-start | bytes 3145732
  105.5 2.9 slice-start
  107.0 1.7 slice-start.1
  113.1 1.6 copy-start.22
  113.6 3.0 copy-start.6
  113.6 19.6 %copy-start.8 = (bf16[16,32,512]{2,1,0:T(8,128)(2,1)}, bf16[16,32,512]{2,1,0:T(8,128)(2,1)S(1)}, u32[]{:S(2)}) copy-start(bf16[16,32,512]{2,1,0:T(8,128)(2,1)S(1)} %get-tuple-element.14) | copy-start | bytes 1572868
  117.3 26.6 %collective-permute-start.2 = (bf16[1,32,512]{2,1,0:T(8,128)(2,1)}, bf16[1,32,512]{2,1,0:T(8,128)(2,1)S(1)}, u32[]{:S(2)}, u32[]{:S(2)}) collective-permute-start(bf16[1,32,512]{2,1,0:T(8,128)(2,1)} %get-tuple-element.44), channel_id=1, source_target_pairs={{0,2},{2,4},{4,6},{6,8},{8,10},{10,12},{12,14},{14,16},{16,18},{18... | collective-permute-start | bytes 98312 | tf_op jit(solution)/shard_map/ppermute | solution.py:12
  122.2 21.7 %collective-permute-start.3 = (bf16[1,32,512]{2,1,0:T(8,128)(2,1)}, bf16[1,32,512]{2,1,0:T(8,128)(2,1)S(1)}, u32[]{:S(2)}, u32[]{:S(2)}) collective-permute-start(bf16[1,32,512]{2,1,0:T(8,128)(2,1)} %get-tuple-element.45), channel_id=1, source_target_pairs={{2,0},{4,2},{6,4},{8,6},{10,8},{12,10},{14,12},{16,14},{18,16},{20... | collective-permute-start | bytes 98312 | tf_op jit(solution)/shard_map/ppermute | solution.py:15
  124.6 21.5 %collective-permute-start.6 = (bf16[1,32,512]{2,1,0:T(8,128)(2,1)}, bf16[1,32,512]{2,1,0:T(8,128)(2,1)S(1)}, u32[]{:S(2)}, u32[]{:S(2)}) collective-permute-start(bf16[1,32,512]{2,1,0:T(8,128)(2,1)} %get-tuple-element.36), channel_id=1, source_target_pairs={{0,2},{2,4},{4,6},{6,8},{8,10},{10,12},{12,14},{14,16},{16,18},{18... | collective-permute-start | bytes 98312 | tf_op jit(solution)/shard_map/ppermute | solution.py:12
  130.7 15.4 %collective-permute-start.7 = (bf16[1,32,512]{2,1,0:T(8,128)(2,1)}, bf16[1,32,512]{2,1,0:T(8,128)(2,1)S(1)}, u32[]{:S(2)}, u32[]{:S(2)}) collective-permute-start(bf16[1,32,512]{2,1,0:T(8,128)(2,1)} %get-tuple-element.37), channel_id=1, source_target_pairs={{2,0},{4,2},{6,4},{8,6},{10,8},{12,10},{14,12},{16,14},{18,16},{20... | collective-permute-start | bytes 98312 | tf_op jit(solution)/shard_map/ppermute | solution.py:15
  136.6 7.3 %copy-start.7 = (bf16[16,32,512]{2,1,0:T(8,128)(2,1)S(1)}, bf16[16,32,512]{2,1,0:T(8,128)(2,1)}, u32[]{:S(2)}) copy-start(bf16[16,32,512]{2,1,0:T(8,128)(2,1)} %copy-done.6) | copy-start | bytes 1572868
  144.2 2.0 copy-start.9
  147.4 1.2 copy-start.20
  147.4 1.5 copy-start.23
  151.6 97.1 %all-reduce.11.cloned.1.call-start = ((), (), s32[]{:S(2)}) async-start(), calls=%async_computation.1 | async-start | bytes 2097152 | tf_op jit(solution)/shard_map/psum | solution.py:104
  151.7 2.4 copy-start.17
  151.7 1.9 copy-start.11
  152.2 1.9 copy-start.10
  153.7 1.9 copy-start.12
  154.1 1.9 copy-start.13
  155.6 1.0 copy-start.16
  156.1 1.1 copy-start.14
  156.6 2.0 copy-start.24
  193.2 365.5 %all-reduce.13.cloned.1.call-start = ((), (), s32[]{:S(2)}) async-start(), calls=%async_computation.2 | async-start | bytes 37748736
  193.5 2.8 copy-start.3
  193.5 3.8 copy-start.4
  215.9 1.7 copy-start.15
  215.9 3.2 copy-start.18
  222.1 1.6 copy-start.21
  228.2 334.1 %copy-start.1 = (bf16[2048,256]{1,0:T(8,128)(2,1)S(1)}, bf16[2048,256]{1,0:T(8,128)(2,1)}, u32[]{:S(2)}) copy-start(bf16[2048,256]{1,0:T(8,128)(2,1)} %param.6) | copy-start | bytes 3145732
Sparse Core Ops, SparseCore 0:
  151.7 34.4 all-gather.1
  193.4 55.2 all-reduce.10
  255.1 303.5 all-reduce.12
where the time goes:
time: 572 us; the launch traced here: 569 us
  waiting for transfers between devices  350 us (61%)
  blocking collectives  72.5 us (13%)
  matrix products  49.2 us (9%)
  local copies, waits for them, and re-layouts  37.1 us (6%)
  starting transfers between devices  30.3 us (5%)
  other arithmetic  15.2 us (3%)
  between operations  14.6 us (3%)
    unnamed x4, waiting for transfers between devices  308 us
    psum x1, blocking collectives, on_device(): summed = lax.psum(partial_value, 'code')  72.5 us
    all_gather x1, waiting for transfers between devices, on_device(): piece = lax.all_gather(grad_embedded, 'code', axis=0, tiled=True)  24.2 us
    another operation x2, local copies, waits for them, and re-layouts, kernel_grad(): return jnp.stack(result)  21.1 us
    ppermute x4, starting transfers between devices, with_halo(): lax.ppermute(lax.slice_in_dim(block, block.shape[dim] - width, None, axis...  19.6 us
    psum x1, waiting for transfers between devices, on_device(): lax.psum(code_terms.astype(jnp.bfloat16), ('space', 'clip'))  18.1 us
    dot_general x18, matrix products, taps_forward(): jnp.dot(window, kernel[first, second], preferred_element_type=jnp.float32)  17.2 us
    another operation x6, other arithmetic, kernel_grad(): return jnp.stack(result)  13.6 us
  transfers between devices with their start and end apart: 11, of which 3 were waited for; matrix products, arithmetic and copies ran while one was open for 12% of the time, Pallas kernels for 0%

commit v1 on v0

v1 whole, which is shorter than its diff:
```python
import functools

import jax
import jax.numpy as jnp
from jax import lax
from jax.experimental import pallas as pl
from jax.experimental.pallas import tpu as pltpu
from jax.sharding import PartitionSpec as P

NARROW = jnp.bfloat16
WIDE = jnp.float32


def swap(value, axis, bits):
    return lax.ppermute(value, axis, [(i, i ^ bits) for i in range(lax.axis_size(axis))])


def plus(*terms):
    return sum(term.astype(WIDE) for term in terms).astype(NARROW)


def neighbours(field, width):
    axes = ("space", "code")
    count = lax.axis_size(axes)
    forward = [(i, i + 1) for i in range(count - 1)]
    backward = [(i + 1, i) for i in range(count - 1)]
    low = lax.ppermute(field[-width:], axes, forward)
    high = lax.ppermute(field[:width], axes, backward)
    return jnp.concatenate([low, field, high], axis=0)


def columns(field, offset):
    breadth = field.shape[1]
    if offset == 0:
        return field
    if offset < 0:
        return jnp.pad(field, ((0, 0), (1, 0), (0, 0)))[:, :breadth]
    return jnp.pad(field, ((0, 0), (0, 1), (0, 0)))[:, 1:]


def flat(field):
    return field.reshape(field.shape[0] * field.shape[1], field.shape[2])


def matmul(left, right):
    return jnp.dot(left, right, preferred_element_type=WIDE)


def taps_forward(field, kernel):
    height = field.shape[0] - 2
    wide = jnp.concatenate([columns(field, b - 1) for b in range(3)], axis=2)
    return sum(
        matmul(flat(wide[a : a + height]), kernel[a].reshape(-1, kernel.shape[3])) for a in range(3)
    )


def taps_back(field, turned):
    height = field.shape[0] - 2
    wide = jnp.concatenate([columns(field, 1 - b) for b in range(3)], axis=2)
    return sum(matmul(flat(wide[2 - a : 2 - a + height]), turned[a]) for a in range(3))


def turn(kernel):
    return kernel.transpose(0, 1, 3, 2).reshape(3, 3 * kernel.shape[3], kernel.shape[2])


def kernel_grad_body(
    breadth, pick, own_up, far_up, own_field, far_field, keep_a, send_a, keep_b, send_b, turned
):
    step = pl.program_id(0)
    cells = own_up.shape[0]
    half = pick.shape[0]
    lanes = own_field.shape[1] // 2
    parts = send_a.shape[0] + 1
    tall = half // parts

    @pl.when(step == 0)
    def _():
        for source, ref in enumerate((own_up, far_up)):
            across = lax.dot_general(
                pick[...], ref[...], (((1,), (1,)), ((), ())), preferred_element_type=WIDE
            )
            column = lax.broadcasted_iota(jnp.int32, across.shape, 1) % breadth
            after = jnp.where(column == breadth - 1, 0.0, pltpu.roll(across, cells - 1, 1))
            before = jnp.where(column == 0, 0.0, pltpu.roll(across, 1, 1))
            for b, value in enumerate((after, across, before)):
                turned[source, b * half : (b + 1) * half, :] = value.astype(NARROW)

    rows = pl.ds(pl.multiple_of(step * breadth, breadth), cells)
    total = matmul(turned[0], own_field[rows, :]) + matmul(turned[1], far_field[rows, :])
    total = total.astype(NARROW)
    short = tall // 2
    for b in range(3):
        for k in range(parts):
            base = b * half + k * tall
            block = total[base : base + tall]
            if k == 0:
                keep_a[0, b] = block[:, :lanes]
            else:
                send_a[k - 1, 0, b] = block[:, :lanes]
            keep_b[0, b, k] = block[:short, lanes:]
            send_b[0, b, k] = block[short:, lanes:]


def kernel_grad(pick, own_up, far_up, own_field, far_field, breadth, parts):
    half = pick.shape[0]
    cells = own_up.shape[0]
    inputs = own_field.shape[1]
    lanes = inputs // 2
    tall = half // parts
    whole = lambda array: pl.BlockSpec(array.shape, lambda a: (0, 0))
    operands = (pick, own_up, far_up, own_field, far_field)
    shapes = (
        ((3, 3, tall, lanes), (1, 3, tall, lanes), lambda a: (a, 0, 0, 0)),
        (
            (parts - 1, 3, 3, tall, lanes),
            (parts - 1, 1, 3, tall, lanes),
            lambda a: (0, a, 0, 0, 0),
        ),
        ((3, 3, parts, tall // 2, lanes), (1, 3, parts, tall // 2, lanes), lambda a: (a, 0, 0, 0, 0)),
        ((3, 3, parts, tall // 2, lanes), (1, 3, parts, tall // 2, lanes), lambda a: (a, 0, 0, 0, 0)),
    )
    return pl.pallas_call(
        functools.partial(kernel_grad_body, breadth),
        grid=(3,),
        in_specs=[whole(array) for array in operands],
        out_specs=[pl.BlockSpec(block, index) for _, block, index in shapes],
        out_shape=[jax.ShapeDtypeStruct(shape, NARROW) for shape, _, _ in shapes],
        scratch_shapes=[pltpu.VMEM((2, 3 * half, cells), NARROW)],
        compiler_params=pltpu.CompilerParams(vmem_limit_bytes=40 * 1024 * 1024),
        cost_estimate=pl.CostEstimate(
            flops=2 * 2 * 9 * half * cells * inputs,
            bytes_accessed=9 * half * inputs * 2 + 4 * cells * inputs * 2,
            transcendentals=0,
        ),
    )(*operands)


def spread(parts_of):
    keep_a, send_a, keep_b, send_b = parts_of
    parts = send_a.shape[0] + 1
    got = [swap(send_a[k - 1], "space", 2 * k) for k in range(1, parts)]
    from_clip = swap(send_b, "clip", 1)
    first = plus(keep_a, *got)
    short = first.shape[2] // 2
    first = plus(first[:, :, :short], swap(first[:, :, short:], "clip", 1))
    second = plus(keep_b, from_clip)
    got = [swap(second[:, :, k], "space", 2 * k) for k in range(1, parts)]
    second = plus(second[:, :, 0], *got)
    joined = jnp.concatenate([first, second], axis=3)
    grain = joined.shape[2] // 4
    piece = lambda k: joined[:, :, k * grain : (k + 1) * grain]
    middle = plus(piece(2), swap(piece(3), "code", 1))
    near = swap(piece(1), "code", 1)
    far = swap(middle, "code", 2)
    total = piece(0).astype(WIDE) + near.astype(WIDE) + far.astype(WIDE)
    return total.transpose(0, 1, 3, 2)


def own_channels(width):
    parts = lax.axis_size("space") // 2
    space = lax.axis_index("space")
    code = lax.axis_index("code")
    clip = lax.axis_index("clip")
    grain = width // (parts * 16)
    index = jnp.arange(width // 2)
    inner = index % grain
    d_code = (index // grain) % 4
    d_clip = (index // (grain * 4)) % 2
    d_space = index // (grain * 8)
    owner = ((space ^ (2 * d_space)) * 4 + (code ^ d_code)) * 2 + (clip ^ d_clip)
    channel = owner * grain + inner
    return (channel[:, None] == jnp.arange(width)[None, :]).astype(NARROW)


def sum_over_tiles(term):
    core = lax.axis_index("space") % 2
    half = term.shape[0] // 2
    mine = lax.dynamic_slice_in_dim(term, core * half, half, 0)
    other = lax.dynamic_slice_in_dim(term, (1 - core) * half, half, 0)
    mine = plus(mine, swap(other, "space", 1))
    stages = []
    bits = 2
    while bits < lax.axis_size("space"):
        stages.append(("space", bits))
        bits *= 2
    first, second = mine[: half // 2], mine[half // 2 :]
    for one, two in zip(stages + [("clip", 1)], [("clip", 1)] + stages):
        first, second = lax.optimization_barrier((first, second))
        got_one, got_two = swap(first, *one), swap(second, *two)
        first, second = plus(first, got_one), plus(second, got_two)
    mine = lax.optimization_barrier(jnp.concatenate([first, second], axis=0))
    other = swap(mine, "space", 1)
    low = jnp.where(core == 0, mine, other)
    high = jnp.where(core == 0, other, mine)
    return jnp.concatenate([low, high], axis=0).astype(WIDE)


def on_device(soft_weights, codebook, kernel_one, kernel_two, cotangent):
    weights = soft_weights[0]
    upstream = cotangent[0]
    own_rows, breadth, width = upstream.shape
    parts = lax.axis_size("space") // 2
    code = lax.axis_index("code")
    place = lax.axis_index("space") * 4 + code
    last = lax.axis_size("space") * 4 - 1

    def tile(k):
        return flat(lax.dynamic_slice_in_dim(weights, (code ^ k) * own_rows, own_rows, 0))

    partial = [matmul(tile(k), codebook) for k in (3, 2, 1, 0)][::-1]
    middle = plus(partial[2], swap(partial[3].astype(NARROW), "code", 1))
    near = swap(partial[1].astype(NARROW), "code", 1)
    far = swap(middle, "code", 2)
    embedded = plus(partial[0], near, far).reshape(own_rows, breadth, -1)

    pick = own_channels(width)
    far_upstream = swap(flat(upstream), "space", 1)
    grad_hidden = taps_back(neighbours(upstream, 2), turn(kernel_two))
    turned_one = turn(kernel_one)

    embed_pad = neighbours(embedded, 2)
    pre_one = taps_forward(embed_pad, kernel_one)
    row = lax.broadcasted_iota(jnp.int32, (own_rows + 2, breadth, 1), 0)
    inside = flat(((row > 0) | (place > 0)) & ((row <= own_rows) | (place < last)))
    sigma = jax.nn.sigmoid(pre_one)
    hidden = jnp.where(inside, pre_one * sigma, 0.0).astype(NARROW)
    grad_pre = jnp.where(
        inside, grad_hidden * sigma * (1.0 + pre_one * (1.0 - sigma)), 0.0
    ).astype(NARROW)
    grad_embedded = taps_back(grad_pre.reshape(own_rows + 2, breadth, -1), turned_one).astype(NARROW)

    across = swap(grad_embedded, "code", 2)
    beside = swap(grad_embedded, "code", 1)
    corner = swap(across, "code", 1)

    own_pre = grad_pre[breadth:-breadth]
    far_hidden = swap(hidden, "space", 1)
    far_pre = swap(own_pre, "space", 1)
    field = flat(embed_pad[1:-1])
    far_field = swap(field, "space", 1)
    grad_two = spread(
        kernel_grad(pick, flat(upstream), far_upstream, hidden, far_hidden, breadth, parts)
    )
    grad_one = spread(kernel_grad(pick, own_pre, far_pre, field, far_field, breadth, parts))
    decoded = taps_forward(hidden.reshape(own_rows + 2, breadth, -1), kernel_two).astype(NARROW)

    term = sum(
        lax.dot_general(tile(k), piece, (((0,), (0,)), ((), ())), preferred_element_type=WIDE)
        for k, piece in enumerate((grad_embedded, beside, across, corner))
    )
    grad_codebook = sum_over_tiles(term)
    return (decoded.reshape(upstream.shape)[None], grad_one, grad_two, grad_codebook)


def solution(mesh):
    in_specs = (
        P("clip", "space", None, "code"),
        P("code", None),
        P(),
        P(),
        P("clip", ("space", "code"), None, None),
    )
    out_specs = (
        P("clip", ("space", "code"), None, None),
        P(None, None, None, ("space", "code", "clip")),
        P(None, None, None, ("space", "code", "clip")),
        P("code", None),
    )
    return jax.shard_map(
        on_device, mesh=mesh, in_specs=in_specs, out_specs=out_specs, check_vma=False
    )
```

time: 572 us -> 186 us (0.33)
  the two profiles are of different devices: /device:TPU:9 before, /device:TPU:0 now
where the time goes in v1:
time: 186 us; the launch traced here: 185 us
  waiting for transfers between devices  57.7 us (31%)
  starting transfers between devices  52.5 us (28%)
  local copies, waits for them, and re-layouts  41.7 us (22%)
  matrix products  20.8 us (11%)
  Pallas kernels  6.22 us (3%)
  other arithmetic  5.13 us (3%)
    ppermute x30, waiting for transfers between devices, swap(): lax.ppermute(value, axis, [(i, i ^ bits) for i in range(lax.axis_size(axi...  54.3 us
    ppermute x30, starting transfers between devices, swap(): lax.ppermute(value, axis, [(i, i ^ bits) for i in range(lax.axis_size(axi...  44.3 us
    dot_general x16, matrix products, matmul(): return jnp.dot(left, right, preferred_element_type=WIDE)  17.8 us
    unnamed x48, local copies, waits for them, and re-layouts  16.7 us
    slice x2, local copies, waits for them, and re-layouts, taps_forward(): kernel[a].reshape(-1, kernel.shape[3])  7.82 us
    dynamic_slice x1, local copies, waits for them, and re-layouts, tile(): lax.dynamic_slice_in_dim(weights, (code ^ k) * own_rows, own_rows, 0)  6.83 us
    slice x2, local copies, waits for them, and re-layouts, taps_back(): turned[a]  6.23 us
    pallas_call x2, Pallas kernels, kernel_grad(): pl.pallas_call(functools.partial(kernel_grad_body, breadth), grid=(3,), i...  6.22 us
  transfers between devices with their start and end apart: 34, of which 14 were waited for; matrix products, arithmetic and copies ran while one was open for 28% of the time, Pallas kernels for 3%

profile of v1, /device:TPU:0, one launch (start us, length us, event | category | flops | bytes accessed | tf_op | source)
XLA Modules:
  0.0 185.3 jit_solution(6059526428135887078)
XLA Ops:
  0.7 6.8 %constant_dynamic-slice_fusion.3 = (bf16[1,16,32,2048]{3,2,1,0:T(8,128)(2,1)S(1)}, bf16[1,16,32,2048]{3,2,1,0:T(8,128)(2,1)}, bf16[1,16,32,2048]{3,2,1,0:T(8,128)(2,1)S(1)}, bf16[1,16,32,2048]{3,2,1,0:T(8,128)(2,1)}) fusion(bf16[1,64,32,2048]{3,2,1,0:T(8,128)(2,1)} %param.5, s32[]{:T(128)S(6)} %select_n.98, s32[]{:T(128)S(6)} %select_n.97, ...), kind=kLoop, calls=%fused_computation.109 | loop fusion | bytes 16777232 | tf_op jit(solution)/shard_map/dynamic_slice | solution.py:209
  7.5 1.9 %convolution_convert_fusion = bf16[512,256]{1,0:T(8,128)(2,1)} fusion(bf16[512,2048]{1,0:T(8,128)(2,1)S(1)} %bitcast.118, bf16[2048,256]{1,0:T(8,128)(2,1)S(1)} %copy-done), kind=kOutput, calls=%fused_computation.19 | convolution fusion | flops 537001984 | bytes 3407872 | tf_op jit(solution)/shard_map/dot_general | solution.py:46
  9.4 3.0 %collective-permute-start.1 = (bf16[512,256]{1,0:T(8,128)(2,1)}, bf16[512,256]{1,0:T(8,128)(2,1)}, u32[]{:S(2)}, u32[]{:S(2)}) collective-permute-start(bf16[512,256]{1,0:T(8,128)(2,1)} %convolution_convert_fusion), channel_id=1, source_target_pairs={{0,2},{2,0},{4,6},{6,4},{1,3},{3,1},{5,7},{7,5},{8,10},{10,8},{12,... | collective-permute-start | bytes 786440 | tf_op jit(solution)/shard_map/ppermute | solution.py:15
  12.5 1.4 convolution_convert_fusion.1
  14.6 3.9 %collective-permute-start.5 = (bf16[2,32,512]{2,1,0:T(8,128)(2,1)}, bf16[2,32,512]{2,1,0:T(8,128)(2,1)S(1)}, u32[]{:S(2)}, u32[]{:S(2)}) collective-permute-start(bf16[2,32,512]{2,1,0:T(8,128)(2,1)} %get-tuple-element.68), channel_id=1, source_target_pairs={{0,2},{2,4},{4,6},{6,8},{8,10},{10,12},{12,14},{14,16},{16,18},{18... | collective-permute-start | bytes 196616 | tf_op jit(solution)/shard_map/ppermute | solution.py:27
  18.5 1.3 collective-permute-start.6
  19.8 2.8 %collective-permute-start.16 = (bf16[512,512]{1,0:T(8,128)(2,1)S(1)}, bf16[512,512]{1,0:T(8,128)(2,1)S(1)}, u32[]{:S(2)}, u32[]{:S(2)}) collective-permute-start(bf16[512,512]{1,0:T(8,128)(2,1)S(1)} %bitcast.107), channel_id=1, source_target_pairs={{0,8},{8,0},{16,24},{24,16},{1,9},{9,1},{17,25},{25,17},{2,10},{10... | collective-permute-start | bytes 1572872 | tf_op jit(solution)/shard_map/ppermute | solution.py:15
  22.6 3.1 %fusion.33 = (bf16[1,3,256,512]{3,2,1,0:T(8,128)(2,1)}, bf16[1,3,256,512]{3,2,1,0:T(8,128)(2,1)}, bf16[1,3,256,512]{3,2,1,0:T(8,128)(2,1)S(1)}) fusion(bf16[3,3,256,512]{3,2,1,0:T(8,128)(2,1)} %param.7), kind=kLoop, calls=%fused_computation.128 | loop fusion | bytes 4718592 | tf_op jit(solution)/shard_map/slice | solution.py:53
  25.7 4.3 %copy.14 = bf16[3,3,256,512]{2,3,1,0:T(8,128)(2,1)} copy(bf16[3,3,256,512]{3,2,1,0:T(8,128)(2,1)} %param.7) | data formatting | bytes 4718592 | tf_op args[2]
  30.0 6.6 %copy.11 = bf16[3,3,512,512]{2,3,1,0:T(8,128)(2,1)} copy(bf16[3,3,512,512]{3,2,1,0:T(8,128)(2,1)} %param.8) | data formatting | bytes 9437184 | tf_op args[3]
  36.6 4.8 %fusion.31 = (bf16[1,3,512,512]{3,2,1,0:T(8,128)(2,1)}, bf16[1,3,512,512]{3,2,1,0:T(8,128)(2,1)}, bf16[1,3,512,512]{3,2,1,0:T(8,128)(2,1)}) fusion(bf16[3,3,512,512]{3,2,1,0:T(8,128)(2,1)} %param.8), kind=kLoop, calls=%fused_computation.126 | loop fusion | bytes 9437184 | tf_op jit(solution)/shard_map/slice | solution.py:53
  41.4 1.5 fusion.40
  42.9 4.8 %fusion.30 = (bf16[1,3,512,512]{3,2,1,0:T(8,128)(2,1)}, bf16[1,3,512,512]{3,2,1,0:T(8,128)(2,1)}, bf16[1,3,512,512]{3,2,1,0:T(8,128)(2,1)}) fusion(bf16[3,3,512,512]{3,2,1,0:T(8,128)(2,1)} %bitcast.117), kind=kLoop, calls=%fused_computation.125 | loop fusion | bytes 9437184 | tf_op jit(solution)/shard_map/slice | solution.py:60
  47.7 1.5 fusion.32
  50.8 0.9 copy-done.5
  51.7 1.8 add_convert_fusion.11
  53.5 1.0 collective-permute-start.2
  54.5 1.1 fusion.43
  55.6 12.5 %collective-permute-done.2 = bf16[512,256]{1,0:T(8,128)(2,1)S(1)} collective-permute-done((bf16[512,256]{1,0:T(8,128)(2,1)S(1)}, bf16[512,256]{1,0:T(8,128)(2,1)S(1)}, u32[]{:S(2)}, u32[]{:S(2)}) %collective-permute-start.2) | collective-permute-done | bytes 262176 | tf_op jit(solution)/shard_map/ppermute | solution.py:15
  68.2 1.6 collective-permute-start.3
  69.8 1.5 collective-permute-start.4
  71.3 1.1 fusion.44
  72.4 3.4 %collective-permute-done.4 = bf16[2,32,256]{2,1,0:T(8,128)(2,1)S(1)} collective-permute-done((bf16[2,32,256]{2,1,0:T(8,128)(2,1)S(1)}, bf16[2,32,256]{2,1,0:T(8,128)(2,1)S(1)}, u32[]{:S(2)}, u32[]{:S(2)}) %collective-permute-start.4) | collective-permute-done | bytes 32800 | tf_op jit(solution)/shard_map/ppermute | solution.py:28
  78.7 0.8 select_convert_fusion
  80.1 1.4 fusion.4
  85.5 1.8 collective-permute-start.25
  87.3 3.6 %collective-permute-start.26 = (bf16[512,256]{1,0:T(8,128)(2,1)S(1)}, bf16[512,256]{1,0:T(8,128)(2,1)S(1)}, u32[]{:S(2)}, u32[]{:S(2)}) collective-permute-start(bf16[512,256]{1,0:T(8,128)(2,1)S(1)} %fusion.6), channel_id=1, source_target_pairs={{0,4},{2,6},{4,0},{6,2},{1,5},{3,7},{5,1},{7,3},{8,12},{10,14},{12... | collective-permute-start | bytes 786440 | tf_op jit(solution)/shard_map/ppermute | solution.py:15
  91.0 1.8 collective-permute-start.17
  93.7 1.1 copy-done.17
  94.8 1.0 fusion.42
  96.2 1.0 convolution_add_fusion.7
  98.5 1.2 collective-permute-done.25
  99.8 2.3 %collective-permute-start.27 = (bf16[512,256]{1,0:T(8,128)(2,1)S(1)}, bf16[512,256]{1,0:T(8,128)(2,1)S(1)}, u32[]{:S(2)}, u32[]{:S(2)}) collective-permute-start(bf16[512,256]{1,0:T(8,128)(2,1)S(1)} %collective-permute-done.26), channel_id=1, source_target_pairs={{0,2},{2,0},{4,6},{6,4},{1,3},{3,1},{5,7},{7,5},{8,10},{10,8},{12,... | collective-permute-start | bytes 786440 | tf_op jit(solution)/shard_map/ppermute | solution.py:15
  102.1 0.8 convolution_add_fusion.2
  103.7 2.6 %shard_map.84 = (bf16[3,3,128,128]{3,2,1,0:T(8,128)(2,1)S(1)}, bf16[1,3,3,128,128]{4,3,2,1,0:T(8,128)(2,1)S(1)}, bf16[3,3,2,64,128]{4,3,2,1,0:T(8,128)(2,1)S(1)}, bf16[3,3,2,64,128]{4,3,2,1,0:T(8,128)(2,1)S(1)}) custom-call(bf16[256,512]{1,0:T(8,128)(2,1)S(1)} %fusion.8.pick, bf16[512,512]{1,0:T(8,128)(2,1)S(1)} %slice.260.own_up, ...), custom_call_target="tpu_custom_call" | custom-call | flops 1207959552 | bytes 2228224 | tf_op jit(solution)/shard_map/pallas_call | solution.py:123
  106.3 1.6 collective-permute-start.11
  108.9 1.2 collective-permute-start.28
  110.1 0.9 collective-permute-start.9
  111.0 3.6 %shard_map.85 = (bf16[3,3,128,256]{3,2,1,0:T(8,128)(2,1)S(1)}, bf16[1,3,3,128,256]{4,3,2,1,0:T(8,128)(2,1)S(1)}, bf16[3,3,2,64,256]{4,3,2,1,0:T(8,128)(2,1)S(1)}, bf16[3,3,2,64,256]{4,3,2,1,0:T(8,128)(2,1)S(1)}) custom-call(bf16[256,512]{1,0:T(8,128)(2,1)S(1)} %fusion.8.pick, bf16[512,512]{1,0:T(8,128)(2,1)S(1)} %bitcast.110, ...), custom_call_target="tpu_custom_call" | custom-call | flops 2415919104 | bytes 4456448 | tf_op jit(solution)/shard_map/pallas_call | solution.py:123
  114.6 1.6 collective-permute-start.20
  116.3 1.2 collective-permute-start.12
  117.5 1.6 collective-permute-done.9
  119.2 1.6 collective-permute-start.10
  120.8 1.6 collective-permute-done.12
  122.4 10.9 %collective-permute-done.10 = bf16[3,3,64,128]{3,2,1,0:T(8,128)(2,1)S(1)} collective-permute-done((bf16[3,3,64,128]{3,2,1,0:T(8,128)(2,1)S(1)}, bf16[3,3,64,128]{3,2,1,0:T(8,128)(2,1)S(1)}, u32[]{:S(2)}, u32[]{:S(2)}) %collective-permute-start.10) | collective-permute-done | bytes 147488 | tf_op jit(solution)/shard_map/ppermute | solution.py:15
  133.3 1.3 collective-permute-start.14
  134.6 1.8 fusion.5
  136.4 1.7 collective-permute-start.18
  138.2 3.5 %collective-permute-start.15 = (bf16[3,3,16,256]{3,2,1,0:T(8,128)(2,1)S(1)}, bf16[3,3,16,256]{3,2,1,0:T(8,128)(2,1)S(1)}, u32[]{:S(2)}, u32[]{:S(2)}) collective-permute-start(bf16[3,3,16,256]{3,2,1,0:T(8,128)(2,1)S(1)} %add_convert_fusion.14), channel_id=1, source_target_pairs={{0,4},{2,6},{4,0},{6,2},{1,5},{3,7},{5,1},{7,3},{8,12},{10,14},{12... | collective-permute-start | bytes 221192 | tf_op jit(solution)/shard_map/ppermute | solution.py:15
  142.7 1.6 collective-permute-start.30
  144.3 8.4 %collective-permute-done.18 = bf16[3,3,128,256]{3,2,1,0:T(8,128)(2,1)S(1)} collective-permute-done((bf16[3,3,128,256]{3,2,1,0:T(8,128)(2,1)S(1)}, bf16[3,3,128,256]{3,2,1,0:T(8,128)(2,1)S(1)}, u32[]{:S(2)}, u32[]{:S(2)}) %collective-permute-start.18) | collective-permute-done | bytes 589856 | tf_op jit(solution)/shard_map/ppermute | solution.py:15
  152.9 1.6 collective-permute-start.19
  154.5 2.5 %collective-permute-done.21 = bf16[3,3,64,256]{3,2,1,0:T(8,128)(2,1)S(1)} collective-permute-done((bf16[3,3,64,256]{3,2,1,0:T(8,128)(2,1)S(1)}, bf16[3,3,64,256]{3,2,1,0:T(8,128)(2,1)S(1)}, u32[]{:S(2)}, u32[]{:S(2)}) %collective-permute-start.21) | collective-permute-done | bytes 294944 | tf_op jit(solution)/shard_map/ppermute | solution.py:15
  157.0 1.3 collective-permute-start.29
  158.5 4.9 %collective-permute-done.29 = bf16[512,256]{1,0:T(8,128)(2,1)S(1)} collective-permute-done((bf16[512,256]{1,0:T(8,128)(2,1)S(1)}, bf16[512,256]{1,0:T(8,128)(2,1)S(1)}, u32[]{:S(2)}, u32[]{:S(2)}) %collective-permute-start.29) | collective-permute-done | bytes 262176 | tf_op jit(solution)/shard_map/ppermute | solution.py:15
  163.4 1.6 collective-permute-start.31
  165.1 1.5 collective-permute-start.32
  166.9 2.9 %collective-permute-done.31 = bf16[512,256]{1,0:T(8,128)(2,1)S(1)} collective-permute-done((bf16[512,256]{1,0:T(8,128)(2,1)S(1)}, bf16[512,256]{1,0:T(8,128)(2,1)S(1)}, u32[]{:S(2)}, u32[]{:S(2)}) %collective-permute-start.31) | collective-permute-done | bytes 262176 | tf_op jit(solution)/shard_map/ppermute | solution.py:15
  169.8 0.8 collective-permute-start.22
  170.7 0.8 collective-permute-done.32
  171.8 3.7 %collective-permute-start.24 = (bf16[3,3,16,512]{3,2,1,0:T(8,128)(2,1)S(1)}, bf16[3,3,16,512]{3,2,1,0:T(8,128)(2,1)S(1)}, u32[]{:S(2)}, u32[]{:S(2)}) collective-permute-start(bf16[3,3,16,512]{3,2,1,0:T(8,128)(2,1)S(1)} %add_convert_fusion.12), channel_id=1, source_target_pairs={{0,4},{2,6},{4,0},{6,2},{1,5},{3,7},{5,1},{7,3},{8,12},{10,14},{12... | collective-permute-start | bytes 442376 | tf_op jit(solution)/shard_map/ppermute | solution.py:15
  176.2 6.8 %collective-permute-done.24 = bf16[3,3,16,512]{3,2,1,0:T(8,128)(2,1)S(1)} collective-permute-done((bf16[3,3,16,512]{3,2,1,0:T(8,128)(2,1)S(1)}, bf16[3,3,16,512]{3,2,1,0:T(8,128)(2,1)S(1)}, u32[]{:S(2)}, u32[]{:S(2)}) %collective-permute-start.24) | collective-permute-done | bytes 147488 | tf_op jit(solution)/shard_map/ppermute | solution.py:15
  183.0 0.8 add_bitcast_fusion
  183.8 1.5 maximum_convert_fusion
  (131 shorter events, 17.5 us)
Async XLA Ops:
  0.6 6.9 %copy-start = (bf16[2048,256]{1,0:T(8,128)(2,1)S(1)}, bf16[2048,256]{1,0:T(8,128)(2,1)}, u32[]{:S(2)}) copy-start(bf16[2048,256]{1,0:T(8,128)(2,1)} %param.6) | copy-start | bytes 3145732
  7.5 1.9 %copy-start.3 = (bf16[1,16,32,2048]{3,2,1,0:T(8,128)(2,1)}, bf16[1,16,32,2048]{3,2,1,0:T(8,128)(2,1)S(1)}, u32[]{:S(2)}) copy-start(bf16[1,16,32,2048]{3,2,1,0:T(8,128)(2,1)S(1)} %get-tuple-element.30) | copy-start | bytes 6291460
  7.5 12.3 %copy-start.6 = (bf16[1,16,32,2048]{3,2,1,0:T(8,128)(2,1)}, bf16[1,16,32,2048]{3,2,1,0:T(8,128)(2,1)S(1)}, u32[]{:S(2)}) copy-start(bf16[1,16,32,2048]{3,2,1,0:T(8,128)(2,1)S(1)} %get-tuple-element.28) | copy-start | bytes 6291460
  9.4 41.3 %collective-permute-start.1 = (bf16[512,256]{1,0:T(8,128)(2,1)}, bf16[512,256]{1,0:T(8,128)(2,1)}, u32[]{:S(2)}, u32[]{:S(2)}) collective-permute-start(bf16[512,256]{1,0:T(8,128)(2,1)} %convolution_convert_fusion), channel_id=1, source_target_pairs={{0,2},{2,0},{4,6},{6,4},{1,3},{3,1},{5,7},{7,5},{8,10},{10,8},{12,... | collective-permute-start | bytes 786440 | tf_op jit(solution)/shard_map/ppermute | solution.py:15
  12.5 1.5 copy-start.2
  13.9 41.6 %collective-permute-start = (bf16[512,256]{1,0:T(8,128)(2,1)}, bf16[512,256]{1,0:T(8,128)(2,1)S(1)}, u32[]{:S(2)}, u32[]{:S(2)}) collective-permute-start(bf16[512,256]{1,0:T(8,128)(2,1)} %convolution_convert_fusion.1), channel_id=1, source_target_pairs={{0,2},{2,0},{4,6},{6,4},{1,3},{3,1},{5,7},{7,5},{8,10},{10,8},{12,... | collective-permute-start | bytes 786440 | tf_op jit(solution)/shard_map/ppermute | solution.py:15
  14.6 34.9 %collective-permute-start.5 = (bf16[2,32,512]{2,1,0:T(8,128)(2,1)}, bf16[2,32,512]{2,1,0:T(8,128)(2,1)S(1)}, u32[]{:S(2)}, u32[]{:S(2)}) collective-permute-start(bf16[2,32,512]{2,1,0:T(8,128)(2,1)} %get-tuple-element.68), channel_id=1, source_target_pairs={{0,2},{2,4},{4,6},{6,8},{8,10},{10,12},{12,14},{14,16},{16,18},{18... | collective-permute-start | bytes 196616 | tf_op jit(solution)/shard_map/ppermute | solution.py:27
  18.5 31.0 %collective-permute-start.6 = (bf16[2,32,512]{2,1,0:T(8,128)(2,1)}, bf16[2,32,512]{2,1,0:T(8,128)(2,1)S(1)}, u32[]{:S(2)}, u32[]{:S(2)}) collective-permute-start(bf16[2,32,512]{2,1,0:T(8,128)(2,1)} %get-tuple-element.69), channel_id=1, source_target_pairs={{2,0},{4,2},{6,4},{8,6},{10,8},{12,10},{14,12},{16,14},{18,16},{20... | collective-permute-start | bytes 196616 | tf_op jit(solution)/shard_map/ppermute | solution.py:28
  19.8 91.2 %collective-permute-start.16 = (bf16[512,512]{1,0:T(8,128)(2,1)S(1)}, bf16[512,512]{1,0:T(8,128)(2,1)S(1)}, u32[]{:S(2)}, u32[]{:S(2)}) collective-permute-start(bf16[512,512]{1,0:T(8,128)(2,1)S(1)} %bitcast.107), channel_id=1, source_target_pairs={{0,8},{8,0},{16,24},{24,16},{1,9},{9,1},{17,25},{25,17},{2,10},{10... | collective-permute-start | bytes 1572872 | tf_op jit(solution)/shard_map/ppermute | solution.py:15
  36.6 4.8 %copy-start.8 = (bf16[1,16,32,2048]{3,2,1,0:T(8,128)(2,1)S(1)}, bf16[1,16,32,2048]{3,2,1,0:T(8,128)(2,1)}, u32[]{:S(2)}) copy-start(bf16[1,16,32,2048]{3,2,1,0:T(8,128)(2,1)} %get-tuple-element.29) | copy-start | bytes 6291460
  42.9 4.8 %copy-start.10 = (bf16[3,3,256,512]{2,3,1,0:T(8,128)(2,1)S(1)}, bf16[3,3,256,512]{2,3,1,0:T(8,128)(2,1)}, u32[]{:S(2)}) copy-start(bf16[3,3,256,512]{2,3,1,0:T(8,128)(2,1)} %copy.14) | copy-start | bytes 7077892
  50.1 1.6 copy-start.5
  51.7 2.8 %copy-start.20 = (bf16[1,3,512,512]{3,2,1,0:T(8,128)(2,1)S(1)}, bf16[1,3,512,512]{3,2,1,0:T(8,128)(2,1)}, u32[]{:S(2)}) copy-start(bf16[1,3,512,512]{3,2,1,0:T(8,128)(2,1)} %get-tuple-element.34) | copy-start | bytes 4718596
  53.5 14.6 %collective-permute-start.2 = (bf16[512,256]{1,0:T(8,128)(2,1)S(1)}, bf16[512,256]{1,0:T(8,128)(2,1)S(1)}, u32[]{:S(2)}, u32[]{:S(2)}) collective-permute-start(bf16[512,256]{1,0:T(8,128)(2,1)S(1)} %add_convert_fusion.11), channel_id=1, source_target_pairs={{0,4},{2,6},{4,0},{6,2},{1,5},{3,7},{5,1},{7,3},{8,12},{10,14},{12... | collective-permute-start | bytes 786440 | tf_op jit(solution)/shard_map/ppermute | solution.py:15
  54.5 13.6 %copy-start.22 = (f32[512,256]{1,0:T(8,128)S(1)}, f32[512,256]{1,0:T(8,128)}, u32[]{:S(2)}) copy-start(f32[512,256]{1,0:T(8,128)} %fusion.40) | copy-start | bytes 1572868
  54.5 16.8 %copy-start.19 = (bf16[1,3,512,512]{3,2,1,0:T(8,128)(2,1)S(1)}, bf16[1,3,512,512]{3,2,1,0:T(8,128)(2,1)}, u32[]{:S(2)}) copy-start(bf16[1,3,512,512]{3,2,1,0:T(8,128)(2,1)} %get-tuple-element.33) | copy-start | bytes 4718596
  68.2 4.2 %collective-permute-start.3 = (bf16[2,32,256]{2,1,0:T(8,128)(2,1)S(1)}, bf16[2,32,256]{2,1,0:T(8,128)(2,1)S(1)}, u32[]{:S(2)}, u32[]{:S(2)}) collective-permute-start(bf16[2,32,256]{2,1,0:T(8,128)(2,1)S(1)} %bitcast.156), channel_id=1, source_target_pairs={{0,2},{2,4},{4,6},{6,8},{8,10},{10,12},{12,14},{14,16},{16,18},{18... | collective-permute-start | bytes 98312 | tf_op jit(solution)/shard_map/ppermute | solution.py:27
  69.8 6.0 %collective-permute-start.4 = (bf16[2,32,256]{2,1,0:T(8,128)(2,1)S(1)}, bf16[2,32,256]{2,1,0:T(8,128)(2,1)S(1)}, u32[]{:S(2)}, u32[]{:S(2)}) collective-permute-start(bf16[2,32,256]{2,1,0:T(8,128)(2,1)S(1)} %bitcast.155), channel_id=1, source_target_pairs={{2,0},{4,2},{6,4},{8,6},{10,8},{12,10},{14,12},{16,14},{18,16},{20... | collective-permute-start | bytes 98312 | tf_op jit(solution)/shard_map/ppermute | solution.py:28
  76.5 1.1 copy-start.13
  77.6 1.1 copy-start.21
  78.7 1.4 copy-start.18
  82.0 1.1 copy-start.12
  82.6 1.2 copy-start.14
  83.8 1.1 copy-start.11
  85.5 14.2 %collective-permute-start.25 = (bf16[512,256]{1,0:T(8,128)(2,1)S(1)}, bf16[512,256]{1,0:T(8,128)(2,1)S(1)}, u32[]{:S(2)}, u32[]{:S(2)}) collective-permute-start(bf16[512,256]{1,0:T(8,128)(2,1)S(1)} %fusion.6), channel_id=1, source_target_pairs={{0,2},{2,0},{4,6},{6,4},{1,3},{3,1},{5,7},{7,5},{8,10},{10,8},{12,... | collective-permute-start | bytes 786440 | tf_op jit(solution)/shard_map/ppermute | solution.py:15
  87.3 12.5 %collective-permute-start.26 = (bf16[512,256]{1,0:T(8,128)(2,1)S(1)}, bf16[512,256]{1,0:T(8,128)(2,1)S(1)}, u32[]{:S(2)}, u32[]{:S(2)}) collective-permute-start(bf16[512,256]{1,0:T(8,128)(2,1)S(1)} %fusion.6), channel_id=1, source_target_pairs={{0,4},{2,6},{4,0},{6,2},{1,5},{3,7},{5,1},{7,3},{8,12},{10,14},{12... | collective-permute-start | bytes 786440 | tf_op jit(solution)/shard_map/ppermute | solution.py:15
  91.0 20.0 %collective-permute-start.17 = (bf16[576,512]{1,0:T(8,128)(2,1)S(1)}, bf16[576,512]{1,0:T(8,128)(2,1)S(1)}, u32[]{:S(2)}, u32[]{:S(2)}) collective-permute-start(bf16[576,512]{1,0:T(8,128)(2,1)S(1)} %get-tuple-element.76.own_field), channel_id=1, source_target_pairs={{0,8},{8,0},{16,24},{24,16},{1,9},{9,1},{17,25},{25,17},{2,10},{10... | collective-permute-start | bytes 1769480 | tf_op jit(solution)/shard_map/ppermute | solution.py:15
  92.8 10.9 %collective-permute-start.7 = (bf16[512,512]{1,0:T(8,128)(2,1)S(1)}, bf16[512,512]{1,0:T(8,128)(2,1)S(1)}, u32[]{:S(2)}, u32[]{:S(2)}) collective-permute-start(bf16[512,512]{1,0:T(8,128)(2,1)S(1)} %slice.260.own_up), channel_id=1, source_target_pairs={{0,8},{8,0},{16,24},{24,16},{1,9},{9,1},{17,25},{25,17},{2,10},{10... | collective-permute-start | bytes 1572872 | tf_op jit(solution)/shard_map/ppermute | solution.py:15
  93.4 1.4 copy-start.17
  94.8 1.4 copy-start.16
  96.2 1.6 copy-start.9
  97.8 4.3 %copy-start.7 = (bf16[1,16,32,2048]{3,2,1,0:T(8,128)(2,1)S(1)}, bf16[1,16,32,2048]{3,2,1,0:T(8,128)(2,1)}, u32[]{:S(2)}) copy-start(bf16[1,16,32,2048]{3,2,1,0:T(8,128)(2,1)} %copy-done.6) | copy-start | bytes 6291460
  99.7 4.0 %collective-permute-start.8 = (bf16[576,256]{1,0:T(8,128)(2,1)S(1)}, bf16[576,256]{1,0:T(8,128)(2,1)S(1)}, u32[]{:S(2)}, u32[]{:S(2)}) collective-permute-start(bf16[576,256]{1,0:T(8,128)(2,1)S(1)} %bitcast.113), channel_id=1, source_target_pairs={{0,8},{8,0},{16,24},{24,16},{1,9},{9,1},{17,25},{25,17},{2,10},{10... | collective-permute-start | bytes 884744 | tf_op jit(solution)/shard_map/ppermute | solution.py:15
  99.8 8.2 %collective-permute-start.27 = (bf16[512,256]{1,0:T(8,128)(2,1)S(1)}, bf16[512,256]{1,0:T(8,128)(2,1)S(1)}, u32[]{:S(2)}, u32[]{:S(2)}) collective-permute-start(bf16[512,256]{1,0:T(8,128)(2,1)S(1)} %collective-permute-done.26), channel_id=1, source_target_pairs={{0,2},{2,0},{4,6},{6,4},{1,3},{3,1},{5,7},{7,5},{8,10},{10,8},{12,... | collective-permute-start | bytes 786440 | tf_op jit(solution)/shard_map/ppermute | solution.py:15
  103.7 4.4 %copy-start.4 = (bf16[1,16,32,2048]{3,2,1,0:T(8,128)(2,1)S(1)}, bf16[1,16,32,2048]{3,2,1,0:T(8,128)(2,1)}, u32[]{:S(2)}) copy-start(bf16[1,16,32,2048]{3,2,1,0:T(8,128)(2,1)} %copy-done.3) | copy-start | bytes 6291460
  106.3 9.9 %collective-permute-start.11 = (bf16[3,3,2,64,128]{4,3,2,1,0:T(8,128)(2,1)S(1)}, bf16[3,3,2,64,128]{4,3,2,1,0:T(8,128)(2,1)S(1)}, u32[]{:S(2)}, u32[]{:S(2)}) collective-permute-start(bf16[3,3,2,64,128]{4,3,2,1,0:T(8,128)(2,1)S(1)} %get-tuple-element.19), channel_id=1, source_target_pairs={{0,1},{1,0},{2,3},{3,2},{4,5},{5,4},{6,7},{7,6},{8,9},{9,8},{10,11... | collective-permute-start | bytes 884744 | tf_op jit(solution)/shard_map/ppermute | solution.py:15
  108.9 33.6 %collective-permute-start.28 = (f32[1024,256]{1,0:T(8,128)S(1)}, f32[1024,256]{1,0:T(8,128)S(1)}, u32[]{:S(2)}, u32[]{:S(2)}) collective-permute-start(f32[1024,256]{1,0:T(8,128)S(1)} %constant_dynamic-slice_fusion), channel_id=1, source_target_pairs={{0,8},{8,0},{16,24},{24,16},{1,9},{9,1},{17,25},{25,17},{2,10},{10... | collective-permute-start | bytes 3145736 | tf_op jit(solution)/shard_map/ppermute | solution.py:15
  110.1 9.0 %collective-permute-start.9 = (bf16[3,3,128,128]{3,2,1,0:T(8,128)(2,1)S(1)}, bf16[3,3,128,128]{3,2,1,0:T(8,128)(2,1)S(1)}, u32[]{:S(2)}, u32[]{:S(2)}) collective-permute-start(bf16[3,3,128,128]{3,2,1,0:T(8,128)(2,1)S(1)} %bitcast.116), channel_id=1, source_target_pairs={{0,16},{8,24},{16,0},{24,8},{1,17},{9,25},{17,1},{25,9},{2,18},{10... | collective-permute-start | bytes 884744 | tf_op jit(solution)/shard_map/ppermute | solution.py:15
  114.6 27.0 %collective-permute-start.20 = (bf16[3,3,2,64,256]{4,3,2,1,0:T(8,128)(2,1)S(1)}, bf16[3,3,2,64,256]{4,3,2,1,0:T(8,128)(2,1)S(1)}, u32[]{:S(2)}, u32[]{:S(2)}) collective-permute-start(bf16[3,3,2,64,256]{4,3,2,1,0:T(8,128)(2,1)S(1)} %get-tuple-element.23), channel_id=1, source_target_pairs={{0,1},{1,0},{2,3},{3,2},{4,5},{5,4},{6,7},{7,6},{8,9},{9,8},{10,11... | collective-permute-start | bytes 1769480 | tf_op jit(solution)/shard_map/ppermute | solution.py:15
  116.2 18.4 %copy-start.15 = (bf16[1,3,512,512]{3,2,1,0:T(8,128)(2,1)S(1)}, bf16[1,3,512,512]{3,2,1,0:T(8,128)(2,1)}, u32[]{:S(2)}) copy-start(bf16[1,3,512,512]{3,2,1,0:T(8,128)(2,1)} %get-tuple-element.35) | copy-start | bytes 4718596
  116.3 6.0 %collective-permute-start.12 = (bf16[3,3,64,128]{3,2,1,0:T(8,128)(2,1)S(1)}, bf16[3,3,64,128]{3,2,1,0:T(8,128)(2,1)S(1)}, u32[]{:S(2)}, u32[]{:S(2)}) collective-permute-start(bf16[3,3,64,128]{3,2,1,0:T(8,128)(2,1)S(1)} %slice_bitcast_fusion.2), channel_id=1, source_target_pairs={{0,16},{8,24},{16,0},{24,8},{1,17},{9,25},{17,1},{25,9},{2,18},{10... | collective-permute-start | bytes 442376 | tf_op jit(solution)/shard_map/ppermute | solution.py:15
  119.2 14.1 %collective-permute-start.10 = (bf16[3,3,64,128]{3,2,1,0:T(8,128)(2,1)S(1)}, bf16[3,3,64,128]{3,2,1,0:T(8,128)(2,1)S(1)}, u32[]{:S(2)}, u32[]{:S(2)}) collective-permute-start(bf16[3,3,64,128]{3,2,1,0:T(8,128)(2,1)S(1)} %slice.263), channel_id=1, source_target_pairs={{0,1},{1,0},{2,3},{3,2},{4,5},{5,4},{6,7},{7,6},{8,9},{9,8},{10,11... | collective-permute-start | bytes 442376 | tf_op jit(solution)/shard_map/ppermute | solution.py:15
  133.3 4.8 %collective-permute-start.14 = (bf16[3,3,16,256]{3,2,1,0:T(8,128)(2,1)S(1)}, bf16[3,3,16,256]{3,2,1,0:T(8,128)(2,1)S(1)}, u32[]{:S(2)}, u32[]{:S(2)}) collective-permute-start(bf16[3,3,16,256]{3,2,1,0:T(8,128)(2,1)S(1)} %get-tuple-element.73), channel_id=1, source_target_pairs={{0,2},{2,0},{4,6},{6,4},{1,3},{3,1},{5,7},{7,5},{8,10},{10,8},{12,... | collective-permute-start | bytes 221192 | tf_op jit(solution)/shard_map/ppermute | solution.py:15
  136.4 16.3 %collective-permute-start.18 = (bf16[3,3,128,256]{3,2,1,0:T(8,128)(2,1)S(1)}, bf16[3,3,128,256]{3,2,1,0:T(8,128)(2,1)S(1)}, u32[]{:S(2)}, u32[]{:S(2)}) collective-permute-start(bf16[3,3,128,256]{3,2,1,0:T(8,128)(2,1)S(1)} %bitcast.115), channel_id=1, source_target_pairs={{0,16},{8,24},{16,0},{24,8},{1,17},{9,25},{17,1},{25,9},{2,18},{10... | collective-permute-start | bytes 1769480 | tf_op jit(solution)/shard_map/ppermute | solution.py:15
  138.1 37.4 %collective-permute-start.13 = (bf16[3,3,16,256]{3,2,1,0:T(8,128)(2,1)S(1)}, bf16[3,3,16,256]{3,2,1,0:T(8,128)(2,1)S(1)}, u32[]{:S(2)}, u32[]{:S(2)}) collective-permute-start(bf16[3,3,16,256]{3,2,1,0:T(8,128)(2,1)S(1)} %get-tuple-element.72), channel_id=1, source_target_pairs={{0,2},{2,0},{4,6},{6,4},{1,3},{3,1},{5,7},{7,5},{8,10},{10,8},{12,... | collective-permute-start | bytes 221192 | tf_op jit(solution)/shard_map/ppermute | solution.py:15
  138.2 37.4 %collective-permute-start.15 = (bf16[3,3,16,256]{3,2,1,0:T(8,128)(2,1)S(1)}, bf16[3,3,16,256]{3,2,1,0:T(8,128)(2,1)S(1)}, u32[]{:S(2)}, u32[]{:S(2)}) collective-permute-start(bf16[3,3,16,256]{3,2,1,0:T(8,128)(2,1)S(1)} %add_convert_fusion.14), channel_id=1, source_target_pairs={{0,4},{2,6},{4,0},{6,2},{1,5},{3,7},{5,1},{7,3},{8,12},{10,14},{12... | collective-permute-start | bytes 221192 | tf_op jit(solution)/shard_map/ppermute | solution.py:15
  141.9 15.1 %collective-permute-start.21 = (bf16[3,3,64,256]{3,2,1,0:T(8,128)(2,1)S(1)}, bf16[3,3,64,256]{3,2,1,0:T(8,128)(2,1)S(1)}, u32[]{:S(2)}, u32[]{:S(2)}) collective-permute-start(bf16[3,3,64,256]{3,2,1,0:T(8,128)(2,1)S(1)} %slice_bitcast_fusion), channel_id=1, source_target_pairs={{0,16},{8,24},{16,0},{24,8},{1,17},{9,25},{17,1},{25,9},{2,18},{10... | collective-permute-start | bytes 884744 | tf_op jit(solution)/shard_map/ppermute | solution.py:15
  142.7 15.7 %collective-permute-start.30 = (bf16[512,256]{1,0:T(8,128)(2,1)S(1)}, bf16[512,256]{1,0:T(8,128)(2,1)S(1)}, u32[]{:S(2)}, u32[]{:S(2)}) collective-permute-start(bf16[512,256]{1,0:T(8,128)(2,1)S(1)} %get-tuple-element.25), channel_id=1, source_target_pairs={{0,1},{1,0},{2,3},{3,2},{4,5},{5,4},{6,7},{7,6},{8,9},{9,8},{10,11... | collective-permute-start | bytes 786440 | tf_op jit(solution)/shard_map/ppermute | solution.py:15
  152.9 12.1 %collective-permute-start.19 = (bf16[3,3,64,256]{3,2,1,0:T(8,128)(2,1)S(1)}, bf16[3,3,64,256]{3,2,1,0:T(8,128)(2,1)S(1)}, u32[]{:S(2)}, u32[]{:S(2)}) collective-permute-start(bf16[3,3,64,256]{3,2,1,0:T(8,128)(2,1)S(1)} %slice.273), channel_id=1, source_target_pairs={{0,1},{1,0},{2,3},{3,2},{4,5},{5,4},{6,7},{7,6},{8,9},{9,8},{10,11... | collective-permute-start | bytes 884744 | tf_op jit(solution)/shard_map/ppermute | solution.py:15
  157.0 6.4 %collective-permute-start.29 = (bf16[512,256]{1,0:T(8,128)(2,1)S(1)}, bf16[512,256]{1,0:T(8,128)(2,1)S(1)}, u32[]{:S(2)}, u32[]{:S(2)}) collective-permute-start(bf16[512,256]{1,0:T(8,128)(2,1)S(1)} %get-tuple-element.24), channel_id=1, source_target_pairs={{0,16},{8,24},{16,0},{24,8},{1,17},{9,25},{17,1},{25,9},{2,18},{10... | collective-permute-start | bytes 786440 | tf_op jit(solution)/shard_map/ppermute | solution.py:15
  163.4 6.4 %collective-permute-start.31 = (bf16[512,256]{1,0:T(8,128)(2,1)S(1)}, bf16[512,256]{1,0:T(8,128)(2,1)S(1)}, u32[]{:S(2)}, u32[]{:S(2)}) collective-permute-start(bf16[512,256]{1,0:T(8,128)(2,1)S(1)} %add_convert_fusion.9), channel_id=1, source_target_pairs={{0,1},{1,0},{2,3},{3,2},{4,5},{5,4},{6,7},{7,6},{8,9},{9,8},{10,11... | collective-permute-start | bytes 786440 | tf_op jit(solution)/shard_map/ppermute | solution.py:15
  165.1 6.4 %collective-permute-start.32 = (bf16[512,256]{1,0:T(8,128)(2,1)S(1)}, bf16[512,256]{1,0:T(8,128)(2,1)S(1)}, u32[]{:S(2)}, u32[]{:S(2)}) collective-permute-start(bf16[512,256]{1,0:T(8,128)(2,1)S(1)} %add_convert_fusion.8), channel_id=1, source_target_pairs={{0,16},{8,24},{16,0},{24,8},{1,17},{9,25},{17,1},{25,9},{2,18},{10... | collective-permute-start | bytes 786440 | tf_op jit(solution)/shard_map/ppermute | solution.py:15
  166.6 5.2 %collective-permute-start.23 = (bf16[3,3,16,512]{3,2,1,0:T(8,128)(2,1)S(1)}, bf16[3,3,16,512]{3,2,1,0:T(8,128)(2,1)S(1)}, u32[]{:S(2)}, u32[]{:S(2)}) collective-permute-start(bf16[3,3,16,512]{3,2,1,0:T(8,128)(2,1)S(1)} %get-tuple-element.63), channel_id=1, source_target_pairs={{0,2},{2,0},{4,6},{6,4},{1,3},{3,1},{5,7},{7,5},{8,10},{10,8},{12,... | collective-permute-start | bytes 442376 | tf_op jit(solution)/shard_map/ppermute | solution.py:15
  169.8 6.4 %collective-permute-start.22 = (bf16[3,3,16,512]{3,2,1,0:T(8,128)(2,1)S(1)}, bf16[3,3,16,512]{3,2,1,0:T(8,128)(2,1)S(1)}, u32[]{:S(2)}, u32[]{:S(2)}) collective-permute-start(bf16[3,3,16,512]{3,2,1,0:T(8,128)(2,1)S(1)} %get-tuple-element.62), channel_id=1, source_target_pairs={{0,2},{2,0},{4,6},{6,4},{1,3},{3,1},{5,7},{7,5},{8,10},{10,8},{12,... | collective-permute-start | bytes 442376 | tf_op jit(solution)/shard_map/ppermute | solution.py:15
  171.6 12.1 %collective-permute-start.33 = (bf16[1024,256]{1,0:T(8,128)(2,1)S(1)}, bf16[1024,256]{1,0:T(8,128)(2,1)S(1)}, u32[]{:S(2)}, u32[]{:S(2)}) collective-permute-start(bf16[1024,256]{1,0:T(8,128)(2,1)S(1)} %pad_maximum_fusion.5), channel_id=1, source_target_pairs={{0,8},{8,0},{16,24},{24,16},{1,9},{9,1},{17,25},{25,17},{2,10},{10... | collective-permute-start | bytes 1572872 | tf_op jit(solution)/shard_map/ppermute | solution.py:15
  171.8 11.2 %collective-permute-start.24 = (bf16[3,3,16,512]{3,2,1,0:T(8,128)(2,1)S(1)}, bf16[3,3,16,512]{3,2,1,0:T(8,128)(2,1)S(1)}, u32[]{:S(2)}, u32[]{:S(2)}) collective-permute-start(bf16[3,3,16,512]{3,2,1,0:T(8,128)(2,1)S(1)} %add_convert_fusion.12), channel_id=1, source_target_pairs={{0,4},{2,6},{4,0},{6,2},{1,5},{3,7},{5,1},{7,3},{8,12},{10,14},{12... | collective-permute-start | bytes 442376 | tf_op jit(solution)/shard_map/ppermute | solution.py:15
  183.8 1.6 copy-start.1

commit v2 on v0

v2 whole, which is shorter than its diff:
```python
import functools

import jax
import jax.numpy as jnp
from jax import lax
from jax.experimental import pallas as pl
from jax.experimental.pallas import tpu as pltpu
from jax.sharding import PartitionSpec as P

NARROW = jnp.bfloat16
WIDE = jnp.float32
COST = 8
SMALL, LARGE, WHOLE = 16 * 1024 * 1024, 24 * 1024 * 1024, 56 * 1024 * 1024


def swap(value, axis, bits, name):
    with jax.named_scope(name):
        return lax.ppermute(value, axis, [(i, i ^ bits) for i in range(lax.axis_size(axis))])


def after(value, *others):
    return lax.optimization_barrier((value, *others))[0]


def plus(*terms):
    return sum(term.astype(WIDE) for term in terms).astype(NARROW)


def edges(top, bottom, name):
    axes = ("space", "code")
    count = lax.axis_size(axes)
    forward = [(i, i + 1) for i in range(count - 1)]
    backward = [(i + 1, i) for i in range(count - 1)]
    with jax.named_scope(name):
        low = lax.ppermute(bottom, axes, forward)
        high = lax.ppermute(top, axes, backward)
    return low, high


def matmul(left, right):
    return jnp.dot(left, right, preferred_element_type=WIDE)


def matmul_turned(left, right):
    return lax.dot_general(left, right, (((1,), (1,)), ((), ())), preferred_element_type=WIDE)


def step_columns(value, offset, breadth):
    if offset == 0:
        return value
    count = value.shape[0]
    column = lax.broadcasted_iota(jnp.int32, value.shape, 0) % breadth
    moved = pltpu.roll(value, (-offset) % count, 0)
    return jnp.where(column == (0 if offset < 0 else breadth - 1), 0.0, moved)


def call(body, operands, outs, flops, scratch=(), limit=SMALL, spaces=None):
    local = pl.BlockSpec(memory_space=pltpu.VMEM)
    return pl.pallas_call(
        body,
        in_specs=[pl.BlockSpec(memory_space=space) for space in spaces] if spaces else [local] * len(operands),
        out_specs=[local] * len(outs),
        out_shape=[jax.ShapeDtypeStruct(shape, dtype) for shape, dtype in outs],
        scratch_shapes=list(scratch),
        compiler_params=pltpu.CompilerParams(vmem_limit_bytes=limit),
        cost_estimate=pl.CostEstimate(flops=flops // COST, bytes_accessed=1, transcendentals=0),
    )(*operands)


def fuse(*tasks):
    spans = [(len(operands), len(outs), len(scratch)) for _, operands, outs, scratch in tasks]
    counts = [sum(span[k] for span in spans) for k in range(3)]

    def body(*refs):
        at = [0, counts[0], counts[0] + counts[1]]
        for (task, *_), span in zip(tasks, spans):
            picked = []
            for k in range(3):
                picked += refs[at[k] : at[k] + span[k]]
                at[k] += span[k]
            task(*picked)

    operands = [operand for task in tasks for operand in task[1]]
    results = list(
        call(
            body,
            operands,
            [out for task in tasks for out in task[2]],
            8 * 10**8,
            [item for task in tasks for item in task[3]],
            spaces=[pltpu.SMEM if item.dtype == jnp.int32 else pltpu.VMEM for item in operands],
        )
    )
    return [[results.pop(0) for _ in range(span[1])] for span in spans]


def lookup_body(count, edge, order, weights, codebook, *refs):
    outs, total = refs[:-1], refs[-1]
    shard, step = pl.program_id(0), pl.program_id(1)
    last = pl.num_programs(1) - 1
    term = matmul(weights[...], codebook[...])

    @pl.when(step == 0)
    def _():
        total[...] = term

    @pl.when(step > 0)
    def _():
        total[...] += term

    for k in range(count):

        @pl.when((step == last) & (shard == k))
        def _():
            if len(outs) == 1:
                ends, inner = outs[0].at[: 2 * edge], outs[0].at[2 * edge :]
            else:
                ends, inner = outs[2 * k], outs[2 * k + 1]
            ends[:edge] = total[:edge].astype(NARROW)
            ends[edge:] = total[-edge:].astype(NARROW)
            inner[...] = total[edge:-edge].astype(NARROW)


def lookup(places, info, weights, codebook, cells, edge, split):
    codes, inner = codebook.shape
    count = len(places)
    first = places[0]
    rows = [cells] if count == 1 else [2 * edge, cells - 2 * edge] * count
    return pl.pallas_call(
        functools.partial(lookup_body, count, edge),
        grid_spec=pltpu.PrefetchScalarGridSpec(
            num_scalar_prefetch=1,
            grid=(count, split),
            in_specs=[
                pl.BlockSpec((cells, codes // split), lambda i, j, order: (order[first + i], j)),
                pl.BlockSpec((codes // split, inner), lambda i, j, order: (j, 0)),
            ],
            out_specs=[pl.BlockSpec((height, inner), lambda i, j, order: (0, 0)) for height in rows],
            scratch_shapes=[pltpu.VMEM((cells, inner), WIDE)],
        ),
        out_shape=[jax.ShapeDtypeStruct((height, inner), NARROW) for height in rows],
        compiler_params=pltpu.CompilerParams(vmem_limit_bytes=WHOLE),
        cost_estimate=pl.CostEstimate(
            flops=2 * count * cells * codebook.size // COST, bytes_accessed=1, transcendentals=0
        ),
    )(info, weights, codebook)


def upstream_body(breadth, own, low, high, kernel, out, padded):
    edge = low.shape[0]
    cells = own.shape[0]
    tall = out.shape[0]
    padded[:edge] = low[...]
    padded[edge : edge + cells] = own[...]
    padded[edge + cells :] = high[...]
    for b in (1, 0, 2):
        total = sum(
            matmul_turned(padded[(2 - a) * breadth : (2 - a) * breadth + tall], kernel[a, b])
            for a in range(3)
        )
        total = step_columns(total, 1 - b, breadth)
        out[...] = total if b == 1 else out[...] + total


def upstream_back(own, low, high, kernel, breadth):
    cells, width = own.shape
    return call(
        functools.partial(upstream_body, breadth),
        (own, low, high, kernel),
        [((cells + 2 * breadth, kernel.shape[2]), WIDE)],
        2 * cells * kernel.size,
        [pltpu.VMEM((cells + 2 * low.shape[0], width), NARROW)],
    )[0]


def head_body(
    breadth, info, low, top, inner, bottom, high, kernel, grad_hidden, hidden, own_pre, field, grad, padded, grad_pre
):
    cells = grad.shape[0]
    tall = hidden.shape[0]
    at = 0
    for part in (low, top, inner, bottom, high):
        padded[at : at + part.shape[0]] = part[...]
        at += part.shape[0]
    field[...] = padded[breadth : breadth + tall]
    pre = sum(
        step_columns(
            sum(matmul(padded[a * breadth : a * breadth + tall], kernel[a, b]) for a in range(3)),
            b - 1,
            breadth,
        )
        for b in (1, 0, 2)
    )
    row = lax.broadcasted_iota(jnp.int32, pre.shape, 0)
    inside = ((row >= breadth) | (info[4] > 0)) & ((row < tall - breadth) | (info[5] > 0))
    sigma = 1.0 / (1.0 + jnp.exp(-pre))
    hidden[...] = jnp.where(inside, pre * sigma, 0.0).astype(NARROW)
    slope = grad_hidden[...] * (sigma * (1.0 + pre * (1.0 - sigma)))
    grad_pre[...] = jnp.where(inside, slope, 0.0).astype(NARROW)
    own_pre[...] = grad_pre[breadth : breadth + cells]
    total = sum(
        step_columns(
            sum(
                matmul_turned(
                    grad_pre[(2 - a) * breadth : (2 - a) * breadth + cells], kernel[a, b]
                )
                for a in range(3)
            ),
            1 - b,
            breadth,
        )
        for b in (1, 0, 2)
    )
    grad[...] = total.astype(NARROW)


def head(info, parts, kernel, grad_hidden, breadth):
    inputs = parts[0].shape[1]
    tall, width = grad_hidden.shape
    cells = tall - 2 * breadth
    return call(
        functools.partial(head_body, breadth),
        (info, *parts, kernel, grad_hidden),
        [((tall, width), NARROW), ((cells, width), NARROW), ((tall, inputs), NARROW), ((cells, inputs), NARROW)],
        4 * cells * kernel.size,
        [pltpu.VMEM((tall + 2 * breadth, inputs), NARROW), pltpu.VMEM((tall, width), NARROW)],
        spaces=(pltpu.SMEM,) + (pltpu.VMEM,) * 7,
    )


def decode_body(breadth, hidden, kernel, out):
    cells = out.shape[0]
    total = sum(
        step_columns(
            sum(matmul(hidden[a * breadth : a * breadth + cells], kernel[a, b]) for a in range(3)),
            b - 1,
            breadth,
        )
        for b in (1, 0, 2)
    )
    out[...] = total.astype(NARROW)


def decode(hidden, kernel, breadth):
    tall = hidden.shape[0]
    return call(
        functools.partial(decode_body, breadth),
        (hidden, kernel),
        [((tall - 2 * breadth, kernel.shape[3]), NARROW)],
        2 * (tall - 2 * breadth) * kernel.size,
    )[0]


def term_of(info, place, weights, field):
    cells = field.shape[0]
    rows = pl.ds(pl.multiple_of(info[place] * cells, cells), cells)
    return lax.dot_general(
        weights[rows, :], field[...], (((0,), (0,)), ((), ())), preferred_element_type=WIDE
    )


def book_start_body(info, weights, own, beside, across, out):
    out[...] = term_of(info, 3, weights, own)
    out[...] += term_of(info, 2, weights, beside)
    out[...] += term_of(info, 1, weights, across)


def book_end_body(info, weights, corner, base, mine, other, total):
    total[...] = base[...] + term_of(info, 0, weights, corner)
    half = mine.shape[0]
    core = info[6]
    mine[...] = total[pl.ds(pl.multiple_of(core * half, half), half), :].astype(NARROW)
    other[...] = total[pl.ds(pl.multiple_of((1 - core) * half, half), half), :].astype(NARROW)


def book_start(info, weights, own, beside, across):
    shape = (weights.shape[1], own.shape[1])
    return call(
        book_start_body,
        (info, weights, own, beside, across),
        [(shape, WIDE)],
        6 * weights.shape[1] * own.size,
        spaces=(pltpu.SMEM,) + (pltpu.VMEM,) * 4,
    )[0]


def book_end(info, weights, corner, base):
    half = (base.shape[0] // 2, base.shape[1])
    return (
        book_end_body,
        (info, weights, corner, base),
        [(half, NARROW), (half, NARROW)],
        [pltpu.VMEM(base.shape, WIDE)],
    )


def halves_body(mine, got, first, second):
    half = first.shape[0]
    first[...] = plus(mine[:half], got[:half])
    second[...] = plus(mine[half:], got[half:])


def halves(mine, got):
    half = (mine.shape[0] // 2, mine.shape[1])
    return halves_body, (mine, got), [(half, NARROW), (half, NARROW)], []


def pair_body(first, got_first, second, got_second, *outs):
    half = first.shape[0]
    if len(outs) == 2:
        outs[0][...] = plus(first[...], got_first[...])
        outs[1][...] = plus(second[...], got_second[...])
    else:
        outs[0][:half] = plus(first[...], got_first[...])
        outs[0][half:] = plus(second[...], got_second[...])


def pair(first, got_first, second, got_second, joined):
    rows, lanes = first.shape
    outs = [((2 * rows, lanes), NARROW)] if joined else [((rows, lanes), NARROW)] * 2
    return pair_body, (first, got_first, second, got_second), outs, []


def kernel_grad_part(breadth, at, pick, own_up, far_up, own_field, far_field, outs, turned):
    keep_a, send_a, keep_b, send_b = outs
    cells = own_up.shape[0]
    half = pick.shape[0]
    lanes = own_field.shape[1] // 2
    parts = send_a.shape[0] + 1
    tall = half // parts
    short = tall // 2
    for source, ref in enumerate((own_up, far_up)):
        across = matmul_turned(pick[...], ref[...])
        column = lax.broadcasted_iota(jnp.int32, across.shape, 1) % breadth
        later = jnp.where(column == breadth - 1, 0.0, pltpu.roll(across, cells - 1, 1))
        sooner = jnp.where(column == 0, 0.0, pltpu.roll(across, 1, 1))
        for b, value in enumerate((later, across, sooner)):
            turned[source, b * half : (b + 1) * half, :] = value.astype(NARROW)

    @pl.loop(0, 3)
    def _(a):
        rows = pl.ds(pl.multiple_of(a * breadth, breadth), cells)
        total = matmul(turned[0], own_field[rows, :]) + matmul(turned[1], far_field[rows, :])
        total = total.astype(NARROW)
        for b in range(3):
            for k in range(parts):
                base = b * half + k * tall
                block = total[base : base + tall]
                if k == 0:
                    keep_a[a, b, :, at : at + lanes] = block[:, :lanes]
                else:
                    send_a[k - 1, a, b, :, at : at + lanes] = block[:, :lanes]
                keep_b[a, b, k, :, at : at + lanes] = block[:short, lanes:]
                send_b[a, b, k, :, at : at + lanes] = block[short:, lanes:]


def kernel_grads_body(breadth, pick, *refs):
    outs, turned = refs[8:12], refs[-1]
    kernel_grad_part(breadth, 0, pick, *refs[:4], outs, turned)
    kernel_grad_part(breadth, refs[2].shape[1] // 2, pick, *refs[4:8], outs, turned)


def kernel_grads(pick, two, one, breadth, parts):
    half = pick.shape[0]
    cells = two[0].shape[0]
    tall = half // parts
    lanes = (two[2].shape[1] + one[2].shape[1]) // 2
    shapes = [
        (3, 3, tall, lanes),
        (parts - 1, 3, 3, tall, lanes),
        (3, 3, parts, tall // 2, lanes),
        (3, 3, parts, tall // 2, lanes),
    ]
    return call(
        functools.partial(kernel_grads_body, breadth),
        (pick, *two, *one),
        [(shape, NARROW) for shape in shapes],
        36 * half * (two[2].size + one[2].size),
        [pltpu.VMEM((2, 3 * half, cells), NARROW)],
        limit=LARGE,
    )


def own_channels(width):
    parts = lax.axis_size("space") // 2
    space = lax.axis_index("space")
    code = lax.axis_index("code")
    clip = lax.axis_index("clip")
    grain = width // (parts * 16)
    index = jnp.arange(width // 2)
    inner = index % grain
    d_code = (index // grain) % 4
    d_clip = (index // (grain * 4)) % 2
    d_space = index // (grain * 8)
    owner = ((space ^ (2 * d_space)) * 4 + (code ^ d_code)) * 2 + (clip ^ d_clip)
    channel = owner * grain + inner
    return (channel[:, None] == jnp.arange(width)[None, :]).astype(NARROW)


def turn_body(keep_a, keep_b, got_b, *refs):
    keep_first, send_first, keep_second, send_second = refs[-4:]
    got_a = refs[:-4]
    short = keep_first.shape[2]
    for a in range(3):
        for b in range(3):
            total = plus(keep_a[a, b], *[got[a, b] for got in got_a])
            keep_first[a, b] = total[:short]
            send_first[a, b] = total[short:]
            total = plus(keep_b[a, b], got_b[a, b])
            keep_second[a, b] = total[0]
            for k in range(1, total.shape[0]):
                send_second[k - 1, a, b] = total[k]


def along_body(keep_first, got_first, keep_second, *refs):
    outs = refs[-4:] if refs[-1].shape[2] * 4 == keep_first.shape[2] else refs[-1:]
    got_second = refs[: -len(outs)]
    lanes = keep_first.shape[3]
    grain = keep_first.shape[2] // len(outs)
    for a in range(3):
        for b in range(3):
            first = plus(keep_first[a, b], got_first[a, b])
            second = plus(keep_second[a, b], *[got[a, b] for got in got_second])
            for k, out in enumerate(outs):
                out[a, b, :, :lanes] = first[k * grain : (k + 1) * grain]
                out[a, b, :, lanes:] = second[k * grain : (k + 1) * grain]


class Spread:
    def __init__(self, parts_of, name):
        self.keep_a, send_a, self.keep_b, send_b = parts_of
        self.name = name
        self.parts = send_a.shape[0] + 1
        self.got_a = [swap(send_a[k - 1], "space", 2 * k, name + "_a1") for k in range(1, self.parts)]
        self.got_b = swap(send_b, "clip", 1, name + "_b1")

    def turn(self):
        tall, lanes = self.keep_a.shape[2:]
        shape = (3, 3, tall // 2, lanes)
        outs = [(shape, NARROW)] * 3 + [((self.parts - 1,) + shape, NARROW)]
        return turn_body, (self.keep_a, self.keep_b, self.got_b, *self.got_a), outs, []

    def turned(self, outs):
        self.first, send_first, self.second, send_second = outs
        self.got_a = swap(send_first, "clip", 1, self.name + "_a2")
        self.got_b = [
            swap(send_second[k - 1], "space", 2 * k, self.name + "_b2") for k in range(1, self.parts)
        ]

    def along(self):
        rows, lanes = self.first.shape[2:]
        outs = [((3, 3, rows, 2 * lanes), NARROW)]
        if rows % 64 == 0:
            outs = [((3, 3, rows // 4, 2 * lanes), NARROW)] * 4
        return along_body, (self.first, self.got_a, self.second, *self.got_b), outs, []

    def sent(self, outs):
        if len(outs) == 1:
            grain = outs[0].shape[2] // 4
            outs = [outs[0][:, :, k * grain : (k + 1) * grain] for k in range(4)]
        self.last = outs[0]
        self.got = [swap(outs[k], "code", k, self.name + "_z") for k in (2, 1, 3)]

    def done(self, split):
        total = sum(got.astype(WIDE) for got in self.got) + self.last.astype(WIDE)
        total = total.transpose(0, 1, 3, 2)
        half = total.shape[2] // 2
        one = jnp.concatenate([total[:, :, split:half], total[:, :, half + split :]], axis=2)
        two = jnp.concatenate([total[:, :, :split], total[:, :, half : half + split]], axis=2)
        return one, two


def on_device(soft_weights, codebook, kernel_one, kernel_two, cotangent):
    weights = soft_weights[0]
    weights = weights.reshape(-1, weights.shape[2])
    own_rows, breadth, width = cotangent.shape[1:]
    upstream = cotangent[0]
    cells = own_rows * breadth
    own_up = upstream.reshape(cells, width)
    parts = lax.axis_size("space") // 2
    code = lax.axis_index("code")
    space = lax.axis_index("space")
    place = space * 4 + code
    last = lax.axis_size("space") * 4 - 1
    flat = lambda field: field.reshape(-1, field.shape[2])
    info = jnp.stack([code ^ 3, code ^ 2, code ^ 1, code, place, last - place, space % 2, 0])
    info = info.astype(jnp.int32)

    edge = 2 * breadth
    (third,) = lookup((0,), info, weights, codebook, cells, edge, 2)
    from_pair = swap(third, "code", 1, "look_z1")
    upstream = after(own_up, third)
    cot_low, cot_high = edges(upstream[:edge], upstream[-edge:], "cot_edge")
    shards = lookup((1, 2, 3), info, weights, after(codebook, third), cells, edge, 1)
    pick = after(own_channels(width), shards[0])
    (second_ends, second, beside_ends, beside, own_ends, own), pick, cot_low, cot_high = (
        lax.optimization_barrier((shards, pick, cot_low, cot_high))
    )
    middle_ends = plus(second_ends, from_pair[: 2 * edge])
    far_ends = swap(middle_ends, "code", 2, "look_ends")
    near_ends = swap(beside_ends, "code", 1, "look_near_ends")
    middle = plus(after(second, middle_ends), from_pair[2 * edge :])
    far = swap(middle, "code", 2, "look_z2")
    near = swap(after(beside, middle), "code", 1, "look_near")
    grad_hidden = upstream_back(after(own_up, middle), cot_low, cot_high, kernel_two, breadth)
    far_up = swap(after(own_up, middle), "space", 1, "cot_core")
    own_ends, own, grad_hidden, far_up = lax.optimization_barrier(
        (own_ends, own, grad_hidden, far_up)
    )
    part = lambda k: slice(k * edge, (k + 1) * edge)
    top, bottom = [
        plus(own_ends[part(k)], near_ends[part(k)], far_ends[part(k)]) for k in range(2)
    ]
    low, high = edges(top, bottom, "embed_edge")
    inner = plus(after(own, top, bottom), near, far)
    hidden, own_pre, field, grad_embedded = head(
        info, (low, top, inner, bottom, high), kernel_one, grad_hidden, breadth
    )

    across = swap(grad_embedded, "code", 2, "ge_z2")
    beside = swap(grad_embedded, "code", 1, "ge_z1")
    far_hidden = swap(hidden, "space", 1, "hidden_core")
    far_pre = swap(own_pre, "space", 1, "pre_core")
    far_field = swap(field, "space", 1, "field_core")
    grads = kernel_grads(
        pick,
        (own_up, far_up, hidden, far_hidden),
        (own_pre, far_pre, field, far_field),
        breadth,
        parts,
    )
    across, beside = after((across, beside), grads[0])
    grads = Spread(grads, "grads")
    corner = swap(across, "code", 1, "ge_z3")
    term = book_start(info, weights, grad_embedded, beside, across)
    ((mine, other),) = fuse(book_end(info, weights, corner, term))
    got = swap(other, "space", 1, "book_core")
    ((first, second),) = fuse(halves(mine, got))

    stages = []
    bits = 2
    while bits < lax.axis_size("space"):
        stages.append(("space", bits))
        bits *= 2
    ways = list(zip(stages + [("clip", 1)], [("clip", 1)] + stages))
    for k, (way, back) in enumerate(ways):
        got_first, got_second = swap(first, *way, "book_a"), swap(second, *back, "book_b")
        task = pair(first, got_first, second, got_second, k == len(ways) - 1)
        if k == 0:
            outs, (first, second) = fuse(grads.turn(), task)
            grads.turned(outs)
        elif k < len(ways) - 1:
            ((first, second),) = fuse(task)
        else:
            decoded = decode(after(hidden, first, second), kernel_two, breadth)
            task = (task[0], (after(first, decoded),) + task[1][1:]) + task[2:]
            outs, (mine,) = fuse(grads.along(), task)
            grads.sent(outs)
    other = swap(mine, "space", 1, "book_back")
    core = space % 2
    low = jnp.where(core == 0, mine, other)
    high = jnp.where(core == 0, other, mine)
    grad_codebook = jnp.concatenate([low, high], axis=0).astype(WIDE)
    grad_one, grad_two = grads.done(width // 2)
    return (decoded.reshape(cotangent.shape), grad_one, grad_two, grad_codebook)


def solution(mesh):
    in_specs = (
        P("clip", "space", None, "code"),
        P("code", None),
        P(),
        P(),
        P("clip", ("space", "code"), None, None),
    )
    out_specs = (
        P("clip", ("space", "code"), None, None),
        P(None, None, None, ("space", "code", "clip")),
        P(None, None, None, ("space", "code", "clip")),
        P("code", None),
    )
    return jax.shard_map(
        on_device, mesh=mesh, in_specs=in_specs, out_specs=out_specs, check_vma=False
    )
```

time: 572 us -> 135 us (0.24)
  the two profiles are of different devices: /device:TPU:9 before, /device:TPU:0 now
where the time goes in v2:
time: 135 us
  starting transfers between devices  50.3 us (37%)
  waiting for transfers between devices  45.5 us (34%)
  Pallas kernels  32.3 us (24%)
  other arithmetic  5.16 us (4%)
    ppermute x25, waiting for transfers between devices, swap(): lax.ppermute(value, axis, [(i, i ^ bits) for i in range(lax.axis_size(axi...  42.2 us
    ppermute x25, starting transfers between devices, swap(): lax.ppermute(value, axis, [(i, i ^ bits) for i in range(lax.axis_size(axi...  40.8 us
    pallas_call x9, Pallas kernels, call(): pl.pallas_call(body, in_specs=[pl.BlockSpec(memory_space=space) for space...  21.4 us
    pallas_call x2, Pallas kernels, lookup(): pl.pallas_call(functools.partial(lookup_body, count, edge), grid_spec=plt...  11 us
    ppermute x2, starting transfers between devices, edges(): low = lax.ppermute(bottom, axes, forward)  6.69 us
    ppermute x2, waiting for transfers between devices, edges(): high = lax.ppermute(top, axes, backward)  3.34 us
    ppermute x2, starting transfers between devices, edges(): high = lax.ppermute(top, axes, backward)  2.76 us
  transfers between devices with their start and end apart: 29, of which 14 were waited for; matrix products, arithmetic and copies ran while one was open for 1% of the time, Pallas kernels for 17%

profile of v2, /device:TPU:0, one launch (start us, length us, event | category | flops | bytes accessed | tf_op | source)
XLA Modules:
  0.0 135.0 jit_solution(11713762231200566399)
XLA Ops:
  0.6 0.6 stack.31.order.info.refs_0_
  1.3 3.9 %shard_map.84 = bf16[512,256]{1,0:T(8,128)(2,1)} custom-call(s32[8]{0:T(128)} %stack.31.order.info.refs_0_, bf16[2048,2048]{1,0:T(8,128)(2,1)} %bitcast.14, bf16[2048,256]{1,0:T(8,128)(2,1)} %codebook.2), custom_call_target="tpu_custom_call" | custom-call | flops 67108864 | bytes 1 | tf_op jit(solution)/shard_map/pallas_call | solution.py:129
  5.1 3.0 %collective-permute-start.2 = (bf16[512,256]{1,0:T(8,128)(2,1)}, bf16[512,256]{1,0:T(8,128)(2,1)S(1)}, u32[]{:S(2)}, u32[]{:S(2)}) collective-permute-start(bf16[512,256]{1,0:T(8,128)(2,1)} %shard_map.84), channel_id=1, source_target_pairs={{0,2},{2,0},{4,6},{6,4},{1,3},{3,1},{5,7},{7,5},{8,10},{10,8},{12,... | collective-permute-start | bytes 786440 | tf_op jit(solution)/shard_map/look_z1/ppermute | solution.py:18
  8.2 1.9 %collective-permute-start = (bf16[64,512]{1,0:T(8,128)(2,1)S(1)}, bf16[64,512]{1,0:T(8,128)(2,1)S(1)}, u32[]{:S(2)}, u32[]{:S(2)}) collective-permute-start(bf16[64,512]{1,0:T(8,128)(2,1)S(1)} %get-tuple-element.113), channel_id=1, source_target_pairs={{0,2},{2,4},{4,6},{6,8},{8,10},{10,12},{12,14},{14,16},{16,18},{18... | collective-permute-start | bytes 196616 | tf_op jit(solution)/shard_map/cot_edge/ppermute | solution.py:35
  10.1 1.3 collective-permute-start.1
  11.4 0.1 fusion.pick
  11.5 0.0 slice-start.3
  11.6 7.1 %shard_map.85 = (bf16[128,256]{1,0:T(8,128)(2,1)}, bf16[384,256]{1,0:T(8,128)(2,1)}, bf16[128,256]{1,0:T(8,128)(2,1)}, bf16[384,256]{1,0:T(8,128)(2,1)}, bf16[12...) custom-call(s32[8]{0:T(128)} %stack.31.order.info.refs_0_, bf16[2048,2048]{1,0:T(8,128)(2,1)} %bitcast.15, ...), custom_call_target="tpu_custom_call" | custom-call | flops 201326592 | bytes 1 | tf_op jit(solution)/shard_map/pallas_call | solution.py:129
  18.7 0.9 add_convert_fusion.2
  19.5 1.0 add_convert_fusion.1
  20.6 3.8 %collective-permute-start.3 = (bf16[512,512]{1,0:T(8,128)(2,1)S(1)}, bf16[512,512]{1,0:T(8,128)(2,1)S(1)}, u32[]{:S(2)}, u32[]{:S(2)}) collective-permute-start(bf16[512,512]{1,0:T(8,128)(2,1)S(1)} %bitcast.23), channel_id=1, source_target_pairs={{0,8},{8,0},{16,24},{24,16},{1,9},{9,1},{17,25},{25,17},{2,10},{10... | collective-permute-start | bytes 1572872 | tf_op jit(solution)/shard_map/cot_core/ppermute | solution.py:18
  24.3 0.1 collective-permute-start.4
  24.5 2.2 %collective-permute-start.5 = (bf16[128,256]{1,0:T(8,128)(2,1)S(1)}, bf16[128,256]{1,0:T(8,128)(2,1)S(1)}, u32[]{:S(2)}, u32[]{:S(2)}) collective-permute-start(bf16[128,256]{1,0:T(8,128)(2,1)S(1)} %add_convert_fusion.2), channel_id=1, source_target_pairs={{0,4},{2,6},{4,0},{6,2},{1,5},{3,7},{5,1},{7,3},{8,12},{10,14},{12... | collective-permute-start | bytes 196616 | tf_op jit(solution)/shard_map/look_ends/ppermute | solution.py:18
  26.7 0.7 collective-permute-start.8
  27.4 1.9 %collective-permute-start.7 = (bf16[384,256]{1,0:T(8,128)(2,1)}, bf16[384,256]{1,0:T(8,128)(2,1)S(1)}, u32[]{:S(2)}, u32[]{:S(2)}) collective-permute-start(bf16[384,256]{1,0:T(8,128)(2,1)} %get-tuple-element.79), channel_id=1, source_target_pairs={{0,2},{2,0},{4,6},{6,4},{1,3},{3,1},{5,7},{7,5},{8,10},{10,8},{12,... | collective-permute-start | bytes 589832 | tf_op jit(solution)/shard_map/look_near/ppermute | solution.py:18
  29.3 2.9 %shard_map.86.grad_hidden = f32[576,512]{1,0:T(8,128)S(1)} custom-call(bf16[512,512]{1,0:T(8,128)(2,1)S(1)} %bitcast.24, bf16[64,512]{1,0:T(8,128)(2,1)S(1)} %collective-permute-done.low, bf16[64,512]{1,0:T(8,128)(2,1)S(1)} %collective-permute-done.1.high, bf16[3,3,512,512]{3,2,1,0:T(8,128)(2,1)S(1)} %bitcast.21), custom_call_target="tpu_custom_call" | custom-call | flops 301989888 | bytes 1 | tf_op jit(solution)/shard_map/pallas_call | solution.py:59
  32.3 4.8 %collective-permute-start.6 = (bf16[64,256]{1,0:T(8,128)(2,1)S(1)}, bf16[64,256]{1,0:T(8,128)(2,1)S(1)}, u32[]{:S(2)}, u32[]{:S(2)}) collective-permute-start(bf16[64,256]{1,0:T(8,128)(2,1)S(1)} %get-tuple-element.119.bottom), channel_id=1, source_target_pairs={{0,2},{2,4},{4,6},{6,8},{8,10},{10,12},{12,14},{14,16},{16,18},{18... | collective-permute-start | bytes 98312 | tf_op jit(solution)/shard_map/embed_edge/ppermute | solution.py:35
  37.1 1.5 %collective-permute-start.9 = (bf16[64,256]{1,0:T(8,128)(2,1)S(1)}, bf16[64,256]{1,0:T(8,128)(2,1)S(1)}, u32[]{:S(2)}, u32[]{:S(2)}) collective-permute-start(bf16[64,256]{1,0:T(8,128)(2,1)S(1)} %get-tuple-element.118.top), channel_id=1, source_target_pairs={{2,0},{4,2},{6,4},{8,6},{10,8},{12,10},{14,12},{16,14},{18,16},{20... | collective-permute-start | bytes 98312 | tf_op jit(solution)/shard_map/embed_edge/ppermute | solution.py:36
  38.6 0.9 collective-permute-done.8
  39.5 0.1 add_convert_fusion.inner
  39.6 3.3 %collective-permute-done.9.high = bf16[64,256]{1,0:T(8,128)(2,1)S(1)} collective-permute-done((bf16[64,256]{1,0:T(8,128)(2,1)S(1)}, bf16[64,256]{1,0:T(8,128)(2,1)S(1)}, u32[]{:S(2)}, u32[]{:S(2)}) %collective-permute-start.9) | collective-permute-done | bytes 32800 | tf_op jit(solution)/shard_map/embed_edge/ppermute | solution.py:36
  42.9 4.1 %shard_map.87 = (bf16[576,512]{1,0:T(8,128)(2,1)S(1)}, bf16[512,512]{1,0:T(8,128)(2,1)S(1)}, bf16[576,256]{1,0:T(8,128)(2,1)S(1)}, bf16[512,256]{1,0:T(8,128)(2,1)S(1)}) custom-call(s32[8]{0:T(128)S(1)} %copy-done.2, bf16[64,256]{1,0:T(8,128)(2,1)S(1)} %collective-permute-done.6.low, bf16[64,256]{1,0:T(8,128)(2,1)S(1)} %get-tuple-element.118.top, ...), custom_call_target="tpu_custom_call" | custom-call | flops 301989888 | bytes 1 | tf_op jit(solution)/shard_map/pallas_call | solution.py:59
  47.1 0.3 collective-permute-start.10
  47.4 0.3 collective-permute-start.11
  47.7 0.2 collective-permute-start.12
  47.9 4.5 %collective-permute-start.15 = (bf16[512,256]{1,0:T(8,128)(2,1)S(1)}, bf16[512,256]{1,0:T(8,128)(2,1)S(1)}, u32[]{:S(2)}, u32[]{:S(2)}) collective-permute-start(bf16[512,256]{1,0:T(8,128)(2,1)S(1)} %get-tuple-element.90.own), channel_id=1, source_target_pairs={{0,4},{2,6},{4,0},{6,2},{1,5},{3,7},{5,1},{7,3},{8,12},{10,14},{12... | collective-permute-start | bytes 786440 | tf_op jit(solution)/shard_map/ge_z2/ppermute | solution.py:18
  52.4 5.0 %collective-permute-start.16 = (bf16[512,256]{1,0:T(8,128)(2,1)S(1)}, bf16[512,256]{1,0:T(8,128)(2,1)S(1)}, u32[]{:S(2)}, u32[]{:S(2)}) collective-permute-start(bf16[512,256]{1,0:T(8,128)(2,1)S(1)} %get-tuple-element.90.own), channel_id=1, source_target_pairs={{0,2},{2,0},{4,6},{6,4},{1,3},{3,1},{5,7},{7,5},{8,10},{10,8},{12,... | collective-permute-start | bytes 786440 | tf_op jit(solution)/shard_map/ge_z1/ppermute | solution.py:18
  57.4 5.9 %shard_map.88 = (bf16[3,3,128,384]{3,2,1,0:T(8,128)(2,1)S(1)}, bf16[1,3,3,128,384]{4,3,2,1,0:T(8,128)(2,1)S(1)}, bf16[3,3,2,64,384]{4,3,2,1,0:T(8,128)(2,1)S(1)}, bf16[3,3,2,64,384]{4,3,2,1,0:T(8,128)(2,1)S(1)}) custom-call(bf16[256,512]{1,0:T(8,128)(2,1)S(1)} %fusion.pick, bf16[512,512]{1,0:T(8,128)(2,1)S(1)} %bitcast.25, ...), custom_call_target="tpu_custom_call" | custom-call | flops 509607936 | bytes 1 | tf_op jit(solution)/shard_map/pallas_call | solution.py:59
  63.3 1.3 collective-permute-done.15.across
  64.6 0.1 collective-permute-done.16.beside
  64.7 1.6 %collective-permute-start.17 = (bf16[512,256]{1,0:T(8,128)(2,1)S(1)}, bf16[512,256]{1,0:T(8,128)(2,1)S(1)}, u32[]{:S(2)}, u32[]{:S(2)}) collective-permute-start(bf16[512,256]{1,0:T(8,128)(2,1)S(1)} %collective-permute-done.15.across), channel_id=1, source_target_pairs={{0,2},{2,0},{4,6},{6,4},{1,3},{3,1},{5,7},{7,5},{8,10},{10,8},{12,... | collective-permute-start | bytes 786440 | tf_op jit(solution)/shard_map/ge_z3/ppermute | solution.py:18
  66.3 1.5 %collective-permute-start.13 = (bf16[3,3,2,64,384]{4,3,2,1,0:T(8,128)(2,1)S(1)}, bf16[3,3,2,64,384]{4,3,2,1,0:T(8,128)(2,1)S(1)}, u32[]{:S(2)}, u32[]{:S(2)}) collective-permute-start(bf16[3,3,2,64,384]{4,3,2,1,0:T(8,128)(2,1)S(1)} %get-tuple-element.88), channel_id=1, source_target_pairs={{0,1},{1,0},{2,3},{3,2},{4,5},{5,4},{6,7},{7,6},{8,9},{9,8},{10,11... | collective-permute-start | bytes 2654216 | tf_op jit(solution)/shard_map/grads_b1/ppermute | solution.py:18
  67.8 1.8 %collective-permute-start.14 = (bf16[3,3,128,384]{3,2,1,0:T(8,128)(2,1)S(1)}, bf16[3,3,128,384]{3,2,1,0:T(8,128)(2,1)S(1)}, u32[]{:S(2)}, u32[]{:S(2)}) collective-permute-start(bf16[3,3,128,384]{3,2,1,0:T(8,128)(2,1)S(1)} %bitcast.26), channel_id=1, source_target_pairs={{0,16},{8,24},{16,0},{24,8},{1,17},{9,25},{17,1},{25,9},{2,18},{10... | collective-permute-start | bytes 2654216 | tf_op jit(solution)/shard_map/grads_a1/ppermute | solution.py:18
  69.6 2.5 %shard_map.89.refs_3_ = f32[2048,256]{1,0:T(8,128)S(1)} custom-call(s32[8]{0:T(128)S(1)} %copy-done.2, bf16[2048,2048]{1,0:T(8,128)(2,1)S(1)} %bitcast.18, bf16[512,256]{1,0:T(8,128)(2,1)S(1)} %get-tuple-element.90.own, bf16[512,256]{1,0:T(8,128)(2,1)S(1)} %collective-permute-done.16.beside, bf16[512,256]{1,0:T(8,128)(2,1)S(1)} %collective-permute-done.15.across), custom_call_target="tpu_custom_call" | custom-call | flops 201326592 | bytes 1 | tf_op jit(solution)/shard_map/pallas_call | solution.py:59
  72.2 0.1 collective-permute-done.17.refs_2_
  72.3 1.5 %shard_map.90 = (bf16[1024,256]{1,0:T(8,128)(2,1)S(1)}, bf16[1024,256]{1,0:T(8,128)(2,1)S(1)}) custom-call(s32[8]{0:T(128)S(1)} %copy-done.2, bf16[2048,2048]{1,0:T(8,128)(2,1)S(1)} %bitcast.19, bf16[512,256]{1,0:T(8,128)(2,1)S(1)} %collective-permute-done.17.refs_2_, f32[2048,256]{1,0:T(8,128)S(1)} %shard_map.89.refs_3_), custom_call_target="tpu_custom_call" | custom-call | flops 100000000 | bytes 1 | tf_op jit(solution)/shard_map/pallas_call | solution.py:59
  73.8 0.1 collective-permute-start.18
  73.9 1.9 %collective-permute-done.18.refs_1_ = bf16[1024,256]{1,0:T(8,128)(2,1)S(1)} collective-permute-done((bf16[1024,256]{1,0:T(8,128)(2,1)S(1)}, bf16[1024,256]{1,0:T(8,128)(2,1)S(1)}, u32[]{:S(2)}, u32[]{:S(2)}) %collective-permute-start.18) | collective-permute-done | bytes 524320 | tf_op jit(solution)/shard_map/book_core/ppermute | solution.py:18
  75.7 0.1 shard_map.91
  75.9 3.4 %collective-permute-start.19 = (bf16[512,256]{1,0:T(8,128)(2,1)S(1)}, bf16[512,256]{1,0:T(8,128)(2,1)S(1)}, u32[]{:S(2)}, u32[]{:S(2)}) collective-permute-start(bf16[512,256]{1,0:T(8,128)(2,1)S(1)} %get-tuple-element.95.refs_4_), channel_id=1, source_target_pairs={{0,16},{8,24},{16,0},{24,8},{1,17},{9,25},{17,1},{25,9},{2,18},{10... | collective-permute-start | bytes 786440 | tf_op jit(solution)/shard_map/book_a/ppermute | solution.py:18
  79.3 1.5 %collective-permute-start.20 = (bf16[512,256]{1,0:T(8,128)(2,1)S(1)}, bf16[512,256]{1,0:T(8,128)(2,1)S(1)}, u32[]{:S(2)}, u32[]{:S(2)}) collective-permute-start(bf16[512,256]{1,0:T(8,128)(2,1)S(1)} %get-tuple-element.96.refs_6_), channel_id=1, source_target_pairs={{0,1},{1,0},{2,3},{3,2},{4,5},{5,4},{6,7},{7,6},{8,9},{9,8},{10,11... | collective-permute-start | bytes 786440 | tf_op jit(solution)/shard_map/book_b/ppermute | solution.py:18
  80.8 8.1 %collective-permute-done.13.refs_2_ = bf16[3,3,2,64,384]{4,3,2,1,0:T(8,128)(2,1)S(1)} collective-permute-done((bf16[3,3,2,64,384]{4,3,2,1,0:T(8,128)(2,1)S(1)}, bf16[3,3,2,64,384]{4,3,2,1,0:T(8,128)(2,1)S(1)}, u32[]{:S(2)}, u32[]{:S(2)}) %collective-permute-start.13) | collective-permute-done | bytes 884768 | tf_op jit(solution)/shard_map/grads_b1/ppermute | solution.py:18
  88.9 1.5 %collective-permute-done.14.refs_3_ = bf16[3,3,128,384]{3,2,1,0:T(8,128)(2,1)S(1)} collective-permute-done((bf16[3,3,128,384]{3,2,1,0:T(8,128)(2,1)S(1)}, bf16[3,3,128,384]{3,2,1,0:T(8,128)(2,1)S(1)}, u32[]{:S(2)}, u32[]{:S(2)}) %collective-permute-start.14) | collective-permute-done | bytes 884768 | tf_op jit(solution)/shard_map/grads_a1/ppermute | solution.py:18
  90.4 4.0 %collective-permute-done.19.refs_5_ = bf16[512,256]{1,0:T(8,128)(2,1)S(1)} collective-permute-done((bf16[512,256]{1,0:T(8,128)(2,1)S(1)}, bf16[512,256]{1,0:T(8,128)(2,1)S(1)}, u32[]{:S(2)}, u32[]{:S(2)}) %collective-permute-start.19) | collective-permute-done | bytes 262176 | tf_op jit(solution)/shard_map/book_a/ppermute | solution.py:18
  94.3 0.5 shard_map.92
  94.9 0.6 collective-permute-start.21
  95.5 1.7 %collective-permute-start.22 = (bf16[3,3,64,384]{3,2,1,0:T(8,128)(2,1)S(1)}, bf16[3,3,64,384]{3,2,1,0:T(8,128)(2,1)S(1)}, u32[]{:S(2)}, u32[]{:S(2)}) collective-permute-start(bf16[3,3,64,384]{3,2,1,0:T(8,128)(2,1)S(1)} %bitcast.27), channel_id=1, source_target_pairs={{0,16},{8,24},{16,0},{24,8},{1,17},{9,25},{17,1},{25,9},{2,18},{10... | collective-permute-start | bytes 1327112 | tf_op jit(solution)/shard_map/grads_b2/ppermute | solution.py:18
  97.2 1.5 %collective-permute-start.23 = (bf16[512,256]{1,0:T(8,128)(2,1)S(1)}, bf16[512,256]{1,0:T(8,128)(2,1)S(1)}, u32[]{:S(2)}, u32[]{:S(2)}) collective-permute-start(bf16[512,256]{1,0:T(8,128)(2,1)S(1)} %get-tuple-element.104.refs_4_), channel_id=1, source_target_pairs={{0,1},{1,0},{2,3},{3,2},{4,5},{5,4},{6,7},{7,6},{8,9},{9,8},{10,11... | collective-permute-start | bytes 786440 | tf_op jit(solution)/shard_map/book_a/ppermute | solution.py:18
  98.7 0.3 collective-permute-start.24
  99.0 3.4 %shard_map.93 = bf16[512,512]{1,0:T(8,128)(2,1)} custom-call(bf16[576,512]{1,0:T(8,128)(2,1)S(1)} %get-tuple-element.99.refs_2_.hidden, bf16[3,3,512,512]{3,2,1,0:T(8,128)(2,1)S(1)} %bitcast.21), custom_call_target="tpu_custom_call" | custom-call | flops 301989888 | bytes 1 | tf_op jit(solution)/shard_map/pallas_call | solution.py:59
  102.4 8.7 %collective-permute-done.23.refs_5_ = bf16[512,256]{1,0:T(8,128)(2,1)S(1)} collective-permute-done((bf16[512,256]{1,0:T(8,128)(2,1)S(1)}, bf16[512,256]{1,0:T(8,128)(2,1)S(1)}, u32[]{:S(2)}, u32[]{:S(2)}) %collective-permute-start.23) | collective-permute-done | bytes 262176 | tf_op jit(solution)/shard_map/book_a/ppermute | solution.py:18
  111.1 0.2 collective-permute-done.24.refs_7_
  111.3 0.3 shard_map.94
  111.7 4.1 %collective-permute-start.27 = (bf16[3,3,16,768]{3,2,1,0:T(8,128)(2,1)S(1)}, bf16[3,3,16,768]{3,2,1,0:T(8,128)(2,1)S(1)}, u32[]{:S(2)}, u32[]{:S(2)}) collective-permute-start(bf16[3,3,16,768]{3,2,1,0:T(8,128)(2,1)S(1)} %get-tuple-element.107), channel_id=1, source_target_pairs={{0,6},{2,4},{4,2},{6,0},{1,7},{3,5},{5,3},{7,1},{8,14},{10,12},{12... | collective-permute-start | bytes 663560 | tf_op jit(solution)/shard_map/grads_z/ppermute | solution.py:18
  115.8 0.2 collective-permute-start.26
  116.0 0.5 collective-permute-start.25
  116.4 5.8 %collective-permute-done.27 = bf16[3,3,16,768]{3,2,1,0:T(8,128)(2,1)S(1)} collective-permute-done((bf16[3,3,16,768]{3,2,1,0:T(8,128)(2,1)S(1)}, bf16[3,3,16,768]{3,2,1,0:T(8,128)(2,1)S(1)}, u32[]{:S(2)}, u32[]{:S(2)}) %collective-permute-start.27) | collective-permute-done | bytes 221216 | tf_op jit(solution)/shard_map/grads_z/ppermute | solution.py:18
  122.2 2.5 %collective-permute-done.26 = bf16[3,3,16,768]{3,2,1,0:T(8,128)(2,1)S(1)} collective-permute-done((bf16[3,3,16,768]{3,2,1,0:T(8,128)(2,1)S(1)}, bf16[3,3,16,768]{3,2,1,0:T(8,128)(2,1)S(1)}, u32[]{:S(2)}, u32[]{:S(2)}) %collective-permute-start.26) | collective-permute-done | bytes 221216 | tf_op jit(solution)/shard_map/grads_z/ppermute | solution.py:18
  124.8 7.0 %collective-permute-done.25 = bf16[3,3,16,768]{3,2,1,0:T(8,128)(2,1)S(1)} collective-permute-done((bf16[3,3,16,768]{3,2,1,0:T(8,128)(2,1)S(1)}, bf16[3,3,16,768]{3,2,1,0:T(8,128)(2,1)S(1)}, u32[]{:S(2)}, u32[]{:S(2)}) %collective-permute-start.25) | collective-permute-done | bytes 221216 | tf_op jit(solution)/shard_map/grads_z/ppermute | solution.py:18
  131.8 0.1 add_bitcast_fusion
  131.9 0.7 pad_maximum_fusion.1
  132.7 0.7 pad_maximum_fusion
  133.4 0.1 broadcast_select_fusion.1
  133.5 1.5 %maximum_convert_fusion = f32[2048,256]{1,0:T(8,128)} fusion(bf16[1024,256]{1,0:T(8,128)(2,1)S(1)} %get-tuple-element.111, bf16[1024,256]{1,0:T(8,128)(2,1)S(1)} %get-tuple-element.110), kind=kLoop, calls=%fused_computation | loop fusion | flops 2097152 | bytes 3145728 | tf_op jit(solution)/shard_map/convert_element_type | solution.py:563
  (40 shorter events, 0.2 us)
Async XLA Ops:
  1.3 6.9 %copy-start = (bf16[1,16,32,512]{3,2,1,0:T(8,128)(2,1)S(1)}, bf16[1,16,32,512]{3,2,1,0:T(8,128)(2,1)}, u32[]{:S(2)}) copy-start(bf16[1,16,32,512]{3,2,1,0:T(8,128)(2,1)} %param.9) | copy-start | bytes 1572868
  5.1 13.5 %collective-permute-start.2 = (bf16[512,256]{1,0:T(8,128)(2,1)}, bf16[512,256]{1,0:T(8,128)(2,1)S(1)}, u32[]{:S(2)}, u32[]{:S(2)}) collective-permute-start(bf16[512,256]{1,0:T(8,128)(2,1)} %shard_map.84), channel_id=1, source_target_pairs={{0,2},{2,0},{4,6},{6,4},{1,3},{3,1},{5,7},{7,5},{8,10},{10,8},{12,... | collective-permute-start | bytes 786440 | tf_op jit(solution)/shard_map/look_z1/ppermute | solution.py:18
  8.2 10.5 %collective-permute-start = (bf16[64,512]{1,0:T(8,128)(2,1)S(1)}, bf16[64,512]{1,0:T(8,128)(2,1)S(1)}, u32[]{:S(2)}, u32[]{:S(2)}) collective-permute-start(bf16[64,512]{1,0:T(8,128)(2,1)S(1)} %get-tuple-element.113), channel_id=1, source_target_pairs={{0,2},{2,4},{4,6},{6,8},{8,10},{10,12},{12,14},{14,16},{16,18},{18... | collective-permute-start | bytes 196616 | tf_op jit(solution)/shard_map/cot_edge/ppermute | solution.py:35
  10.1 8.6 %collective-permute-start.1 = (bf16[64,512]{1,0:T(8,128)(2,1)S(1)}, bf16[64,512]{1,0:T(8,128)(2,1)S(1)}, u32[]{:S(2)}, u32[]{:S(2)}) collective-permute-start(bf16[64,512]{1,0:T(8,128)(2,1)S(1)} %get-tuple-element.112), channel_id=1, source_target_pairs={{2,0},{4,2},{6,4},{8,6},{10,8},{12,10},{14,12},{16,14},{18,16},{20... | collective-permute-start | bytes 196616 | tf_op jit(solution)/shard_map/cot_edge/ppermute | solution.py:36
  11.4 17.9 %slice-start.2 = ((s8[4718592]{0:T(1024)(128)(4,1)}), s8[4194304]{0:T(1024)(128)(4,1)S(1)}, s32[]{:S(2)}) async-start(s8[4718592]{0:T(1024)(128)(4,1)} %bitcast.20), calls=%async_computation.2 | async-start | bytes 8388608
  11.5 17.7 %slice-start.3 = ((s8[4718592]{0:T(1024)(128)(4,1)}), s8[524288]{0:T(1024)(128)(4,1)S(1)}, s32[]{:S(2)}) async-start(s8[4718592]{0:T(1024)(128)(4,1)} %bitcast.20), calls=%async_computation.3 | async-start | bytes 1048576
  20.5 11.8 %copy-start.4 = (bf16[128,256]{1,0:T(8,128)(2,1)S(1)}, bf16[128,256]{1,0:T(8,128)(2,1)}, u32[]{:S(2)}) copy-start(bf16[128,256]{1,0:T(8,128)(2,1)} %get-tuple-element.74) | copy-start | bytes 196612
  20.5 19.0 %copy-start.3 = (bf16[384,256]{1,0:T(8,128)(2,1)S(1)}, bf16[384,256]{1,0:T(8,128)(2,1)}, u32[]{:S(2)}) copy-start(bf16[384,256]{1,0:T(8,128)(2,1)} %get-tuple-element.77) | copy-start | bytes 589828
  20.5 22.4 %copy-start.2 = (s32[8]{0:T(128)S(1)}, s32[8]{0:T(128)}, u32[]{:S(2)}) copy-start(s32[8]{0:T(128)} %stack.31.order.info.refs_0_) | copy-start | bytes 100
  20.6 11.7 %collective-permute-start.3 = (bf16[512,512]{1,0:T(8,128)(2,1)S(1)}, bf16[512,512]{1,0:T(8,128)(2,1)S(1)}, u32[]{:S(2)}, u32[]{:S(2)}) collective-permute-start(bf16[512,512]{1,0:T(8,128)(2,1)S(1)} %bitcast.23), channel_id=1, source_target_pairs={{0,8},{8,0},{16,24},{24,16},{1,9},{9,1},{17,25},{25,17},{2,10},{10... | collective-permute-start | bytes 1572872 | tf_op jit(solution)/shard_map/cot_core/ppermute | solution.py:18
  24.3 7.9 %collective-permute-start.4 = (bf16[128,256]{1,0:T(8,128)(2,1)}, bf16[128,256]{1,0:T(8,128)(2,1)S(1)}, u32[]{:S(2)}, u32[]{:S(2)}) collective-permute-start(bf16[128,256]{1,0:T(8,128)(2,1)} %get-tuple-element.75), channel_id=1, source_target_pairs={{0,2},{2,0},{4,6},{6,4},{1,3},{3,1},{5,7},{7,5},{8,10},{10,8},{12,... | collective-permute-start | bytes 196616 | tf_op jit(solution)/shard_map/look_near_ends/ppermute | solution.py:18
  24.5 7.8 %collective-permute-start.5 = (bf16[128,256]{1,0:T(8,128)(2,1)S(1)}, bf16[128,256]{1,0:T(8,128)(2,1)S(1)}, u32[]{:S(2)}, u32[]{:S(2)}) collective-permute-start(bf16[128,256]{1,0:T(8,128)(2,1)S(1)} %add_convert_fusion.2), channel_id=1, source_target_pairs={{0,4},{2,6},{4,0},{6,2},{1,5},{3,7},{5,1},{7,3},{8,12},{10,14},{12... | collective-permute-start | bytes 196616 | tf_op jit(solution)/shard_map/look_ends/ppermute | solution.py:18
  26.7 12.8 %collective-permute-start.8 = (bf16[384,256]{1,0:T(8,128)(2,1)S(1)}, bf16[384,256]{1,0:T(8,128)(2,1)S(1)}, u32[]{:S(2)}, u32[]{:S(2)}) collective-permute-start(bf16[384,256]{1,0:T(8,128)(2,1)S(1)} %add_convert_fusion.1), channel_id=1, source_target_pairs={{0,4},{2,6},{4,0},{6,2},{1,5},{3,7},{5,1},{7,3},{8,12},{10,14},{12... | collective-permute-start | bytes 589832 | tf_op jit(solution)/shard_map/look_z2/ppermute | solution.py:18
  27.4 12.1 %collective-permute-start.7 = (bf16[384,256]{1,0:T(8,128)(2,1)}, bf16[384,256]{1,0:T(8,128)(2,1)S(1)}, u32[]{:S(2)}, u32[]{:S(2)}) collective-permute-start(bf16[384,256]{1,0:T(8,128)(2,1)} %get-tuple-element.79), channel_id=1, source_target_pairs={{0,2},{2,0},{4,6},{6,4},{1,3},{3,1},{5,7},{7,5},{8,10},{10,8},{12,... | collective-permute-start | bytes 589832 | tf_op jit(solution)/shard_map/look_near/ppermute | solution.py:18
  29.3 13.6 %copy-start.1 = (bf16[3,3,256,512]{3,2,1,0:T(8,128)(2,1)S(1)}, bf16[3,3,256,512]{3,2,1,0:T(8,128)(2,1)}, u32[]{:S(2)}) copy-start(bf16[3,3,256,512]{3,2,1,0:T(8,128)(2,1)} %kernel.4) | copy-start | bytes 7077892
  29.3 40.3 %slice-start = ((s8[8388608]{0:T(1024)(128)(4,1)}), s8[4194304]{0:T(1024)(128)(4,1)S(1)}, s32[]{:S(2)}) async-start(s8[8388608]{0:T(1024)(128)(4,1)} %bitcast.16), calls=%async_computation | async-start | bytes 8388608
  32.3 7.3 %collective-permute-start.6 = (bf16[64,256]{1,0:T(8,128)(2,1)S(1)}, bf16[64,256]{1,0:T(8,128)(2,1)S(1)}, u32[]{:S(2)}, u32[]{:S(2)}) collective-permute-start(bf16[64,256]{1,0:T(8,128)(2,1)S(1)} %get-tuple-element.119.bottom), channel_id=1, source_target_pairs={{0,2},{2,4},{4,6},{6,8},{8,10},{10,12},{12,14},{14,16},{16,18},{18... | collective-permute-start | bytes 98312 | tf_op jit(solution)/shard_map/embed_edge/ppermute | solution.py:35
  37.1 5.8 %collective-permute-start.9 = (bf16[64,256]{1,0:T(8,128)(2,1)S(1)}, bf16[64,256]{1,0:T(8,128)(2,1)S(1)}, u32[]{:S(2)}, u32[]{:S(2)}) collective-permute-start(bf16[64,256]{1,0:T(8,128)(2,1)S(1)} %get-tuple-element.118.top), channel_id=1, source_target_pairs={{2,0},{4,2},{6,4},{8,6},{10,8},{12,10},{14,12},{16,14},{18,16},{20... | collective-permute-start | bytes 98312 | tf_op jit(solution)/shard_map/embed_edge/ppermute | solution.py:36
  39.6 30.1 %slice-start.1 = ((s8[8388608]{0:T(1024)(128)(4,1)}), s8[4194304]{0:T(1024)(128)(4,1)S(1)}, s32[]{:S(2)}) async-start(s8[8388608]{0:T(1024)(128)(4,1)} %bitcast.16), calls=%async_computation.1 | async-start | bytes 8388608
  47.1 10.3 %collective-permute-start.10 = (bf16[576,512]{1,0:T(8,128)(2,1)S(1)}, bf16[576,512]{1,0:T(8,128)(2,1)S(1)}, u32[]{:S(2)}, u32[]{:S(2)}) collective-permute-start(bf16[576,512]{1,0:T(8,128)(2,1)S(1)} %get-tuple-element.99.refs_2_.hidden), channel_id=1, source_target_pairs={{0,8},{8,0},{16,24},{24,16},{1,9},{9,1},{17,25},{25,17},{2,10},{10... | collective-permute-start | bytes 1769480 | tf_op jit(solution)/shard_map/hidden_core/ppermute | solution.py:18
  47.4 10.0 %collective-permute-start.11 = (bf16[512,512]{1,0:T(8,128)(2,1)S(1)}, bf16[512,512]{1,0:T(8,128)(2,1)S(1)}, u32[]{:S(2)}, u32[]{:S(2)}) collective-permute-start(bf16[512,512]{1,0:T(8,128)(2,1)S(1)} %get-tuple-element.84.refs_4_), channel_id=1, source_target_pairs={{0,8},{8,0},{16,24},{24,16},{1,9},{9,1},{17,25},{25,17},{2,10},{10... | collective-permute-start | bytes 1572872 | tf_op jit(solution)/shard_map/pre_core/ppermute | solution.py:18
  47.7 9.7 %collective-permute-start.12 = (bf16[576,256]{1,0:T(8,128)(2,1)S(1)}, bf16[576,256]{1,0:T(8,128)(2,1)S(1)}, u32[]{:S(2)}, u32[]{:S(2)}) collective-permute-start(bf16[576,256]{1,0:T(8,128)(2,1)S(1)} %get-tuple-element.85.refs_6_), channel_id=1, source_target_pairs={{0,8},{8,0},{16,24},{24,16},{1,9},{9,1},{17,25},{25,17},{2,10},{10... | collective-permute-start | bytes 884744 | tf_op jit(solution)/shard_map/field_core/ppermute | solution.py:18
  47.9 16.8 %collective-permute-start.15 = (bf16[512,256]{1,0:T(8,128)(2,1)S(1)}, bf16[512,256]{1,0:T(8,128)(2,1)S(1)}, u32[]{:S(2)}, u32[]{:S(2)}) collective-permute-start(bf16[512,256]{1,0:T(8,128)(2,1)S(1)} %get-tuple-element.90.own), channel_id=1, source_target_pairs={{0,4},{2,6},{4,0},{6,2},{1,5},{3,7},{5,1},{7,3},{8,12},{10,14},{12... | collective-permute-start | bytes 786440 | tf_op jit(solution)/shard_map/ge_z2/ppermute | solution.py:18
  52.4 12.3 %collective-permute-start.16 = (bf16[512,256]{1,0:T(8,128)(2,1)S(1)}, bf16[512,256]{1,0:T(8,128)(2,1)S(1)}, u32[]{:S(2)}, u32[]{:S(2)}) collective-permute-start(bf16[512,256]{1,0:T(8,128)(2,1)S(1)} %get-tuple-element.90.own), channel_id=1, source_target_pairs={{0,2},{2,0},{4,6},{6,4},{1,3},{3,1},{5,7},{7,5},{8,10},{10,8},{12,... | collective-permute-start | bytes 786440 | tf_op jit(solution)/shard_map/ge_z1/ppermute | solution.py:18
  64.7 7.6 %collective-permute-start.17 = (bf16[512,256]{1,0:T(8,128)(2,1)S(1)}, bf16[512,256]{1,0:T(8,128)(2,1)S(1)}, u32[]{:S(2)}, u32[]{:S(2)}) collective-permute-start(bf16[512,256]{1,0:T(8,128)(2,1)S(1)} %collective-permute-done.15.across), channel_id=1, source_target_pairs={{0,2},{2,0},{4,6},{6,4},{1,3},{3,1},{5,7},{7,5},{8,10},{10,8},{12,... | collective-permute-start | bytes 786440 | tf_op jit(solution)/shard_map/ge_z3/ppermute | solution.py:18
  66.3 22.6 %collective-permute-start.13 = (bf16[3,3,2,64,384]{4,3,2,1,0:T(8,128)(2,1)S(1)}, bf16[3,3,2,64,384]{4,3,2,1,0:T(8,128)(2,1)S(1)}, u32[]{:S(2)}, u32[]{:S(2)}) collective-permute-start(bf16[3,3,2,64,384]{4,3,2,1,0:T(8,128)(2,1)S(1)} %get-tuple-element.88), channel_id=1, source_target_pairs={{0,1},{1,0},{2,3},{3,2},{4,5},{5,4},{6,7},{7,6},{8,9},{9,8},{10,11... | collective-permute-start | bytes 2654216 | tf_op jit(solution)/shard_map/grads_b1/ppermute | solution.py:18
  67.8 22.6 %collective-permute-start.14 = (bf16[3,3,128,384]{3,2,1,0:T(8,128)(2,1)S(1)}, bf16[3,3,128,384]{3,2,1,0:T(8,128)(2,1)S(1)}, u32[]{:S(2)}, u32[]{:S(2)}) collective-permute-start(bf16[3,3,128,384]{3,2,1,0:T(8,128)(2,1)S(1)} %bitcast.26), channel_id=1, source_target_pairs={{0,16},{8,24},{16,0},{24,8},{1,17},{9,25},{17,1},{25,9},{2,18},{10... | collective-permute-start | bytes 2654216 | tf_op jit(solution)/shard_map/grads_a1/ppermute | solution.py:18
  73.8 2.0 %collective-permute-start.18 = (bf16[1024,256]{1,0:T(8,128)(2,1)S(1)}, bf16[1024,256]{1,0:T(8,128)(2,1)S(1)}, u32[]{:S(2)}, u32[]{:S(2)}) collective-permute-start(bf16[1024,256]{1,0:T(8,128)(2,1)S(1)} %get-tuple-element.94), channel_id=1, source_target_pairs={{0,8},{8,0},{16,24},{24,16},{1,9},{9,1},{17,25},{25,17},{2,10},{10... | collective-permute-start | bytes 1572872 | tf_op jit(solution)/shard_map/book_core/ppermute | solution.py:18
  75.9 18.5 %collective-permute-start.19 = (bf16[512,256]{1,0:T(8,128)(2,1)S(1)}, bf16[512,256]{1,0:T(8,128)(2,1)S(1)}, u32[]{:S(2)}, u32[]{:S(2)}) collective-permute-start(bf16[512,256]{1,0:T(8,128)(2,1)S(1)} %get-tuple-element.95.refs_4_), channel_id=1, source_target_pairs={{0,16},{8,24},{16,0},{24,8},{1,17},{9,25},{17,1},{25,9},{2,18},{10... | collective-permute-start | bytes 786440 | tf_op jit(solution)/shard_map/book_a/ppermute | solution.py:18
  79.3 15.1 %collective-permute-start.20 = (bf16[512,256]{1,0:T(8,128)(2,1)S(1)}, bf16[512,256]{1,0:T(8,128)(2,1)S(1)}, u32[]{:S(2)}, u32[]{:S(2)}) collective-permute-start(bf16[512,256]{1,0:T(8,128)(2,1)S(1)} %get-tuple-element.96.refs_6_), channel_id=1, source_target_pairs={{0,1},{1,0},{2,3},{3,2},{4,5},{5,4},{6,7},{7,6},{8,9},{9,8},{10,11... | collective-permute-start | bytes 786440 | tf_op jit(solution)/shard_map/book_b/ppermute | solution.py:18
  94.9 16.4 %collective-permute-start.21 = (bf16[3,3,64,384]{3,2,1,0:T(8,128)(2,1)S(1)}, bf16[3,3,64,384]{3,2,1,0:T(8,128)(2,1)S(1)}, u32[]{:S(2)}, u32[]{:S(2)}) collective-permute-start(bf16[3,3,64,384]{3,2,1,0:T(8,128)(2,1)S(1)} %get-tuple-element.101), channel_id=1, source_target_pairs={{0,1},{1,0},{2,3},{3,2},{4,5},{5,4},{6,7},{7,6},{8,9},{9,8},{10,11... | collective-permute-start | bytes 1327112 | tf_op jit(solution)/shard_map/grads_a2/ppermute | solution.py:18
  95.5 15.9 %collective-permute-start.22 = (bf16[3,3,64,384]{3,2,1,0:T(8,128)(2,1)S(1)}, bf16[3,3,64,384]{3,2,1,0:T(8,128)(2,1)S(1)}, u32[]{:S(2)}, u32[]{:S(2)}) collective-permute-start(bf16[3,3,64,384]{3,2,1,0:T(8,128)(2,1)S(1)} %bitcast.27), channel_id=1, source_target_pairs={{0,16},{8,24},{16,0},{24,8},{1,17},{9,25},{17,1},{25,9},{2,18},{10... | collective-permute-start | bytes 1327112 | tf_op jit(solution)/shard_map/grads_b2/ppermute | solution.py:18
  97.2 13.9 %collective-permute-start.23 = (bf16[512,256]{1,0:T(8,128)(2,1)S(1)}, bf16[512,256]{1,0:T(8,128)(2,1)S(1)}, u32[]{:S(2)}, u32[]{:S(2)}) collective-permute-start(bf16[512,256]{1,0:T(8,128)(2,1)S(1)} %get-tuple-element.104.refs_4_), channel_id=1, source_target_pairs={{0,1},{1,0},{2,3},{3,2},{4,5},{5,4},{6,7},{7,6},{8,9},{9,8},{10,11... | collective-permute-start | bytes 786440 | tf_op jit(solution)/shard_map/book_a/ppermute | solution.py:18
  98.7 12.6 %collective-permute-start.24 = (bf16[512,256]{1,0:T(8,128)(2,1)S(1)}, bf16[512,256]{1,0:T(8,128)(2,1)S(1)}, u32[]{:S(2)}, u32[]{:S(2)}) collective-permute-start(bf16[512,256]{1,0:T(8,128)(2,1)S(1)} %get-tuple-element.98.refs_6_), channel_id=1, source_target_pairs={{0,16},{8,24},{16,0},{24,8},{1,17},{9,25},{17,1},{25,9},{2,18},{10... | collective-permute-start | bytes 786440 | tf_op jit(solution)/shard_map/book_b/ppermute | solution.py:18
  111.7 10.6 %collective-permute-start.27 = (bf16[3,3,16,768]{3,2,1,0:T(8,128)(2,1)S(1)}, bf16[3,3,16,768]{3,2,1,0:T(8,128)(2,1)S(1)}, u32[]{:S(2)}, u32[]{:S(2)}) collective-permute-start(bf16[3,3,16,768]{3,2,1,0:T(8,128)(2,1)S(1)} %get-tuple-element.107), channel_id=1, source_target_pairs={{0,6},{2,4},{4,2},{6,0},{1,7},{3,5},{5,3},{7,1},{8,14},{10,12},{12... | collective-permute-start | bytes 663560 | tf_op jit(solution)/shard_map/grads_z/ppermute | solution.py:18
  115.8 9.0 %collective-permute-start.26 = (bf16[3,3,16,768]{3,2,1,0:T(8,128)(2,1)S(1)}, bf16[3,3,16,768]{3,2,1,0:T(8,128)(2,1)S(1)}, u32[]{:S(2)}, u32[]{:S(2)}) collective-permute-start(bf16[3,3,16,768]{3,2,1,0:T(8,128)(2,1)S(1)} %get-tuple-element.106), channel_id=1, source_target_pairs={{0,2},{2,0},{4,6},{6,4},{1,3},{3,1},{5,7},{7,5},{8,10},{10,8},{12,... | collective-permute-start | bytes 663560 | tf_op jit(solution)/shard_map/grads_z/ppermute | solution.py:18
  116.0 15.8 %collective-permute-start.25 = (bf16[3,3,16,768]{3,2,1,0:T(8,128)(2,1)S(1)}, bf16[3,3,16,768]{3,2,1,0:T(8,128)(2,1)S(1)}, u32[]{:S(2)}, u32[]{:S(2)}) collective-permute-start(bf16[3,3,16,768]{3,2,1,0:T(8,128)(2,1)S(1)} %get-tuple-element.105), channel_id=1, source_target_pairs={{0,4},{2,6},{4,0},{6,2},{1,5},{3,7},{5,1},{7,3},{8,12},{10,14},{12... | collective-permute-start | bytes 663560 | tf_op jit(solution)/shard_map/grads_z/ppermute | solution.py:18
  116.4 17.0 %collective-permute-start.28 = (bf16[1024,256]{1,0:T(8,128)(2,1)S(1)}, bf16[1024,256]{1,0:T(8,128)(2,1)S(1)}, u32[]{:S(2)}, u32[]{:S(2)}) collective-permute-start(bf16[1024,256]{1,0:T(8,128)(2,1)S(1)} %get-tuple-element.109), channel_id=1, source_target_pairs={{0,8},{8,0},{16,24},{24,16},{1,9},{9,1},{17,25},{25,17},{2,10},{10... | collective-permute-start | bytes 1572872 | tf_op jit(solution)/shard_map/book_back/ppermute | solution.py:18

commit v3 on v2

--- a/solution.py
+++ b/solution.py
@@ -545,17 +545,19 @@
     ways = list(zip(stages + [("clip", 1)], [("clip", 1)] + stages))
     for k, (way, back) in enumerate(ways):
         got_first, got_second = swap(first, *way, "book_a"), swap(second, *back, "book_b")
-        task = pair(first, got_first, second, got_second, k == len(ways) - 1)
         if k == 0:
-            outs, (first, second) = fuse(grads.turn(), task)
+            (outs,) = fuse(grads.turn())
             grads.turned(outs)
-        elif k < len(ways) - 1:
-            ((first, second),) = fuse(task)
-        else:
+            (outs,) = fuse(grads.along())
+            grads.sent(outs)
+            first = after(first, grads.last)
+        elif k == len(ways) - 1:
             decoded = decode(after(hidden, first, second), kernel_two, breadth)
-            task = (task[0], (after(first, decoded),) + task[1][1:]) + task[2:]
-            outs, (mine,) = fuse(grads.along(), task)
-            grads.sent(outs)
+            first = after(first, decoded)
+        (outs,) = fuse(pair(first, got_first, second, got_second, k == len(ways) - 1))
+        if k < len(ways) - 1:
+            first, second = outs
+    (mine,) = outs
     other = swap(mine, "space", 1, "book_back")
     core = space % 2
     low = jnp.where(core == 0, mine, other)

time: 135 us -> 125 us (0.926)
  the two profiles are of different devices: /device:TPU:0 before, /device:TPU:9 now
where the time goes in v3:
time: 125 us; the launch traced here: 124 us
  waiting for transfers between devices  42.4 us (34%)
  starting transfers between devices  40 us (32%)
  Pallas kernels  32.5 us (26%)
  other arithmetic  5.17 us (4%)
  local copies, waits for them, and re-layouts  3.11 us (2%)
    ppermute x25, waiting for transfers between devices, swap(): lax.ppermute(value, axis, [(i, i ^ bits) for i in range(lax.axis_size(axi...  39.3 us
    ppermute x25, starting transfers between devices, swap(): lax.ppermute(value, axis, [(i, i ^ bits) for i in range(lax.axis_size(axi...  28.2 us
    pallas_call x11, Pallas kernels, call(): pl.pallas_call(body, in_specs=[pl.BlockSpec(memory_space=space) for space...  21.6 us
    pallas_call x2, Pallas kernels, lookup(): pl.pallas_call(functools.partial(lookup_body, count, edge), grid_spec=plt...  11 us
    ppermute x2, starting transfers between devices, edges(): low = lax.ppermute(bottom, axes, forward)  6.42 us
    ppermute x2, starting transfers between devices, edges(): high = lax.ppermute(top, axes, backward)  5.46 us
    ppermute x2, waiting for transfers between devices, edges(): high = lax.ppermute(top, axes, backward)  3.07 us
  transfers between devices with their start and end apart: 29, of which 12 were waited for; matrix products, arithmetic and copies ran while one was open for 1% of the time, Pallas kernels for 15%

profile of v3, /device:TPU:9, one launch (start us, length us, event | category | flops | bytes accessed | tf_op | source)
XLA Modules:
  0.0 124.2 jit_solution(1901440401378419769)
XLA Ops:
  0.6 0.7 stack.31.order.info.refs_0_
  1.3 3.9 %shard_map.84 = bf16[512,256]{1,0:T(8,128)(2,1)} custom-call(s32[8]{0:T(128)} %stack.31.order.info.refs_0_, bf16[2048,2048]{1,0:T(8,128)(2,1)} %bitcast.14, bf16[2048,256]{1,0:T(8,128)(2,1)} %codebook.2), custom_call_target="tpu_custom_call" | custom-call | flops 67108864 | bytes 1 | tf_op jit(solution)/shard_map/pallas_call | solution.py:129
  5.2 4.5 %collective-permute-start = (bf16[64,512]{1,0:T(8,128)(2,1)S(1)}, bf16[64,512]{1,0:T(8,128)(2,1)S(1)}, u32[]{:S(2)}, u32[]{:S(2)}) collective-permute-start(bf16[64,512]{1,0:T(8,128)(2,1)S(1)} %get-tuple-element.113), channel_id=1, source_target_pairs={{0,2},{2,4},{4,6},{6,8},{8,10},{10,12},{12,14},{14,16},{16,18},{18... | collective-permute-start | bytes 196616 | tf_op jit(solution)/shard_map/cot_edge/ppermute | solution.py:35
  9.7 1.9 %collective-permute-start.1 = (bf16[64,512]{1,0:T(8,128)(2,1)S(1)}, bf16[64,512]{1,0:T(8,128)(2,1)S(1)}, u32[]{:S(2)}, u32[]{:S(2)}) collective-permute-start(bf16[64,512]{1,0:T(8,128)(2,1)S(1)} %get-tuple-element.112), channel_id=1, source_target_pairs={{2,0},{4,2},{6,4},{8,6},{10,8},{12,10},{14,12},{16,14},{18,16},{20... | collective-permute-start | bytes 196616 | tf_op jit(solution)/shard_map/cot_edge/ppermute | solution.py:36
  11.7 0.0 slice-start.2
  11.7 0.1 fusion.pick
  11.8 0.0 slice-start.3
  11.8 7.1 %shard_map.85 = (bf16[128,256]{1,0:T(8,128)(2,1)}, bf16[384,256]{1,0:T(8,128)(2,1)}, bf16[128,256]{1,0:T(8,128)(2,1)}, bf16[384,256]{1,0:T(8,128)(2,1)}, bf16[12...) custom-call(s32[8]{0:T(128)} %stack.31.order.info.refs_0_, bf16[2048,2048]{1,0:T(8,128)(2,1)} %bitcast.15, ...), custom_call_target="tpu_custom_call" | custom-call | flops 201326592 | bytes 1 | tf_op jit(solution)/shard_map/pallas_call | solution.py:129
  18.9 0.9 add_convert_fusion.2
  19.8 1.0 add_convert_fusion.1
  20.8 1.3 %collective-permute-start.3 = (bf16[512,512]{1,0:T(8,128)(2,1)S(1)}, bf16[512,512]{1,0:T(8,128)(2,1)S(1)}, u32[]{:S(2)}, u32[]{:S(2)}) collective-permute-start(bf16[512,512]{1,0:T(8,128)(2,1)S(1)} %bitcast.23), channel_id=1, source_target_pairs={{0,8},{8,0},{16,24},{24,16},{1,9},{9,1},{17,25},{25,17},{2,10},{10... | collective-permute-start | bytes 1572872 | tf_op jit(solution)/shard_map/cot_core/ppermute | solution.py:18
  22.1 1.2 %collective-permute-start.4 = (bf16[128,256]{1,0:T(8,128)(2,1)}, bf16[128,256]{1,0:T(8,128)(2,1)S(1)}, u32[]{:S(2)}, u32[]{:S(2)}) collective-permute-start(bf16[128,256]{1,0:T(8,128)(2,1)} %get-tuple-element.75), channel_id=1, source_target_pairs={{0,2},{2,0},{4,6},{6,4},{1,3},{3,1},{5,7},{7,5},{8,10},{10,8},{12,... | collective-permute-start | bytes 196616 | tf_op jit(solution)/shard_map/look_near_ends/ppermute | solution.py:18
  23.4 1.7 %collective-permute-start.5 = (bf16[128,256]{1,0:T(8,128)(2,1)S(1)}, bf16[128,256]{1,0:T(8,128)(2,1)S(1)}, u32[]{:S(2)}, u32[]{:S(2)}) collective-permute-start(bf16[128,256]{1,0:T(8,128)(2,1)S(1)} %add_convert_fusion.2), channel_id=1, source_target_pairs={{0,4},{2,6},{4,0},{6,2},{1,5},{3,7},{5,1},{7,3},{8,12},{10,14},{12... | collective-permute-start | bytes 196616 | tf_op jit(solution)/shard_map/look_ends/ppermute | solution.py:18
  25.0 0.7 collective-permute-start.8
  25.7 0.2 collective-permute-start.7
  26.0 3.0 %shard_map.86.grad_hidden = f32[576,512]{1,0:T(8,128)S(1)} custom-call(bf16[512,512]{1,0:T(8,128)(2,1)S(1)} %bitcast.24, bf16[64,512]{1,0:T(8,128)(2,1)S(1)} %collective-permute-done.low, bf16[64,512]{1,0:T(8,128)(2,1)S(1)} %collective-permute-done.1.high, bf16[3,3,512,512]{3,2,1,0:T(8,128)(2,1)S(1)} %bitcast.21), custom_call_target="tpu_custom_call" | custom-call | flops 301989888 | bytes 1 | tf_op jit(solution)/shard_map/pallas_call | solution.py:59
  29.0 3.2 %collective-permute-done.5 = bf16[128,256]{1,0:T(8,128)(2,1)S(1)} collective-permute-done((bf16[128,256]{1,0:T(8,128)(2,1)S(1)}, bf16[128,256]{1,0:T(8,128)(2,1)S(1)}, u32[]{:S(2)}, u32[]{:S(2)}) %collective-permute-start.5) | collective-permute-done | bytes 65568 | tf_op jit(solution)/shard_map/look_ends/ppermute | solution.py:18
  32.2 1.9 %collective-permute-start.6 = (bf16[64,256]{1,0:T(8,128)(2,1)S(1)}, bf16[64,256]{1,0:T(8,128)(2,1)S(1)}, u32[]{:S(2)}, u32[]{:S(2)}) collective-permute-start(bf16[64,256]{1,0:T(8,128)(2,1)S(1)} %get-tuple-element.119.bottom), channel_id=1, source_target_pairs={{0,2},{2,4},{4,6},{6,8},{8,10},{10,12},{12,14},{14,16},{16,18},{18... | collective-permute-start | bytes 98312 | tf_op jit(solution)/shard_map/embed_edge/ppermute | solution.py:35
  34.2 3.5 %collective-permute-start.9 = (bf16[64,256]{1,0:T(8,128)(2,1)S(1)}, bf16[64,256]{1,0:T(8,128)(2,1)S(1)}, u32[]{:S(2)}, u32[]{:S(2)}) collective-permute-start(bf16[64,256]{1,0:T(8,128)(2,1)S(1)} %get-tuple-element.118.top), channel_id=1, source_target_pairs={{2,0},{4,2},{6,4},{8,6},{10,8},{12,10},{14,12},{16,14},{18,16},{20... | collective-permute-start | bytes 98312 | tf_op jit(solution)/shard_map/embed_edge/ppermute | solution.py:36
  37.7 0.1 add_convert_fusion.inner
  37.8 0.0 slice-start.1
  37.8 3.1 %collective-permute-done.9.high = bf16[64,256]{1,0:T(8,128)(2,1)S(1)} collective-permute-done((bf16[64,256]{1,0:T(8,128)(2,1)S(1)}, bf16[64,256]{1,0:T(8,128)(2,1)S(1)}, u32[]{:S(2)}, u32[]{:S(2)}) %collective-permute-start.9) | collective-permute-done | bytes 32800 | tf_op jit(solution)/shard_map/embed_edge/ppermute | solution.py:36
  40.9 4.2 %shard_map.87 = (bf16[576,512]{1,0:T(8,128)(2,1)S(1)}, bf16[512,512]{1,0:T(8,128)(2,1)S(1)}, bf16[576,256]{1,0:T(8,128)(2,1)S(1)}, bf16[512,256]{1,0:T(8,128)(2,1)S(1)}) custom-call(s32[8]{0:T(128)S(1)} %copy-done.3, bf16[64,256]{1,0:T(8,128)(2,1)S(1)} %collective-permute-done.6.low, bf16[64,256]{1,0:T(8,128)(2,1)S(1)} %get-tuple-element.118.top, ...), custom_call_target="tpu_custom_call" | custom-call | flops 301989888 | bytes 1 | tf_op jit(solution)/shard_map/pallas_call | solution.py:59
  45.1 1.9 %collective-permute-start.12 = (bf16[576,512]{1,0:T(8,128)(2,1)S(1)}, bf16[576,512]{1,0:T(8,128)(2,1)S(1)}, u32[]{:S(2)}, u32[]{:S(2)}) collective-permute-start(bf16[576,512]{1,0:T(8,128)(2,1)S(1)} %get-tuple-element.105.refs_2_.hidden), channel_id=1, source_target_pairs={{0,8},{8,0},{16,24},{24,16},{1,9},{9,1},{17,25},{25,17},{2,10},{10... | collective-permute-start | bytes 1769480 | tf_op jit(solution)/shard_map/hidden_core/ppermute | solution.py:18
  47.0 0.1 collective-permute-start.13
  47.1 0.4 collective-permute-start.14
  47.5 2.3 %collective-permute-done.14.refs_7_ = bf16[576,256]{1,0:T(8,128)(2,1)S(1)} collective-permute-done((bf16[576,256]{1,0:T(8,128)(2,1)S(1)}, bf16[576,256]{1,0:T(8,128)(2,1)S(1)}, u32[]{:S(2)}, u32[]{:S(2)}) %collective-permute-start.14) | collective-permute-done | bytes 294944 | tf_op jit(solution)/shard_map/field_core/ppermute | solution.py:18
  49.8 5.9 %shard_map.88 = (bf16[3,3,128,384]{3,2,1,0:T(8,128)(2,1)S(1)}, bf16[1,3,3,128,384]{4,3,2,1,0:T(8,128)(2,1)S(1)}, bf16[3,3,2,64,384]{4,3,2,1,0:T(8,128)(2,1)S(1)}, bf16[3,3,2,64,384]{4,3,2,1,0:T(8,128)(2,1)S(1)}) custom-call(bf16[256,512]{1,0:T(8,128)(2,1)S(1)} %fusion.pick, bf16[512,512]{1,0:T(8,128)(2,1)S(1)} %bitcast.25, ...), custom_call_target="tpu_custom_call" | custom-call | flops 509607936 | bytes 1 | tf_op jit(solution)/shard_map/pallas_call | solution.py:59
  55.7 1.3 %collective-permute-start.17 = (bf16[3,3,2,64,384]{4,3,2,1,0:T(8,128)(2,1)S(1)}, bf16[3,3,2,64,384]{4,3,2,1,0:T(8,128)(2,1)S(1)}, u32[]{:S(2)}, u32[]{:S(2)}) collective-permute-start(bf16[3,3,2,64,384]{4,3,2,1,0:T(8,128)(2,1)S(1)} %get-tuple-element.94), channel_id=1, source_target_pairs={{0,1},{1,0},{2,3},{3,2},{4,5},{5,4},{6,7},{7,6},{8,9},{9,8},{10,11... | collective-permute-start | bytes 2654216 | tf_op jit(solution)/shard_map/grads_b1/ppermute | solution.py:18
  57.0 1.0 collective-permute-start.18
  58.0 6.2 %collective-permute-start.10 = (bf16[512,256]{1,0:T(8,128)(2,1)S(1)}, bf16[512,256]{1,0:T(8,128)(2,1)S(1)}, u32[]{:S(2)}, u32[]{:S(2)}) collective-permute-start(bf16[512,256]{1,0:T(8,128)(2,1)S(1)} %get-tuple-element.82.own), channel_id=1, source_target_pairs={{0,4},{2,6},{4,0},{6,2},{1,5},{3,7},{5,1},{7,3},{8,12},{10,14},{12... | collective-permute-start | bytes 786440 | tf_op jit(solution)/shard_map/ge_z2/ppermute | solution.py:18
  64.2 9.4 %collective-permute-done.10.across = bf16[512,256]{1,0:T(8,128)(2,1)S(1)} collective-permute-done((bf16[512,256]{1,0:T(8,128)(2,1)S(1)}, bf16[512,256]{1,0:T(8,128)(2,1)S(1)}, u32[]{:S(2)}, u32[]{:S(2)}) %collective-permute-start.10) | collective-permute-done | bytes 262176 | tf_op jit(solution)/shard_map/ge_z2/ppermute | solution.py:18
  73.6 2.4 %collective-permute-start.15 = (bf16[512,256]{1,0:T(8,128)(2,1)S(1)}, bf16[512,256]{1,0:T(8,128)(2,1)S(1)}, u32[]{:S(2)}, u32[]{:S(2)}) collective-permute-start(bf16[512,256]{1,0:T(8,128)(2,1)S(1)} %collective-permute-done.10.across), channel_id=1, source_target_pairs={{0,2},{2,0},{4,6},{6,4},{1,3},{3,1},{5,7},{7,5},{8,10},{10,8},{12,... | collective-permute-start | bytes 786440 | tf_op jit(solution)/shard_map/ge_z3/ppermute | solution.py:18
  76.0 2.6 %shard_map.89.refs_3_ = f32[2048,256]{1,0:T(8,128)S(1)} custom-call(s32[8]{0:T(128)S(1)} %copy-done.3, bf16[2048,2048]{1,0:T(8,128)(2,1)S(1)} %bitcast.18, bf16[512,256]{1,0:T(8,128)(2,1)S(1)} %get-tuple-element.82.own, bf16[512,256]{1,0:T(8,128)(2,1)S(1)} %collective-permute-done.11.beside, bf16[512,256]{1,0:T(8,128)(2,1)S(1)} %collective-permute-done.10.across), custom_call_target="tpu_custom_call" | custom-call | flops 201326592 | bytes 1 | tf_op jit(solution)/shard_map/pallas_call | solution.py:59
  78.6 2.5 %collective-permute-done.15.refs_2_ = bf16[512,256]{1,0:T(8,128)(2,1)S(1)} collective-permute-done((bf16[512,256]{1,0:T(8,128)(2,1)S(1)}, bf16[512,256]{1,0:T(8,128)(2,1)S(1)}, u32[]{:S(2)}, u32[]{:S(2)}) %collective-permute-start.15) | collective-permute-done | bytes 262176 | tf_op jit(solution)/shard_map/ge_z3/ppermute | solution.py:18
  81.1 1.5 %shard_map.90 = (bf16[1024,256]{1,0:T(8,128)(2,1)S(1)}, bf16[1024,256]{1,0:T(8,128)(2,1)S(1)}) custom-call(s32[8]{0:T(128)S(1)} %copy-done.3, bf16[2048,2048]{1,0:T(8,128)(2,1)S(1)} %bitcast.19, bf16[512,256]{1,0:T(8,128)(2,1)S(1)} %collective-permute-done.15.refs_2_, f32[2048,256]{1,0:T(8,128)S(1)} %shard_map.89.refs_3_), custom_call_target="tpu_custom_call" | custom-call | flops 100000000 | bytes 1 | tf_op jit(solution)/shard_map/pallas_call | solution.py:59
  82.6 2.3 %collective-permute-start.16 = (bf16[1024,256]{1,0:T(8,128)(2,1)S(1)}, bf16[1024,256]{1,0:T(8,128)(2,1)S(1)}, u32[]{:S(2)}, u32[]{:S(2)}) collective-permute-start(bf16[1024,256]{1,0:T(8,128)(2,1)S(1)} %get-tuple-element.91), channel_id=1, source_target_pairs={{0,8},{8,0},{16,24},{24,16},{1,9},{9,1},{17,25},{25,17},{2,10},{10... | collective-permute-start | bytes 1572872 | tf_op jit(solution)/shard_map/book_core/ppermute | solution.py:18
  84.9 0.4 shard_map.92
  85.3 0.3 collective-permute-start.19
  85.6 0.8 collective-permute-done.16.refs_1_
  86.4 0.1 shard_map.91
  86.5 0.7 collective-permute-start.21
  87.3 1.2 collective-permute-start.22
  88.5 8.6 %collective-permute-done.19.refs_1_ = bf16[3,3,64,384]{3,2,1,0:T(8,128)(2,1)S(1)} collective-permute-done((bf16[3,3,64,384]{3,2,1,0:T(8,128)(2,1)S(1)}, bf16[3,3,64,384]{3,2,1,0:T(8,128)(2,1)S(1)}, u32[]{:S(2)}, u32[]{:S(2)}) %collective-permute-start.19) | collective-permute-done | bytes 442400 | tf_op jit(solution)/shard_map/grads_a2/ppermute | solution.py:18
  97.2 0.2 shard_map.93
  97.4 2.8 %collective-permute-start.23 = (bf16[3,3,16,768]{3,2,1,0:T(8,128)(2,1)S(1)}, bf16[3,3,16,768]{3,2,1,0:T(8,128)(2,1)S(1)}, u32[]{:S(2)}, u32[]{:S(2)}) collective-permute-start(bf16[3,3,16,768]{3,2,1,0:T(8,128)(2,1)S(1)} %get-tuple-element.106), channel_id=1, source_target_pairs={{0,4},{2,6},{4,0},{6,2},{1,5},{3,7},{5,1},{7,3},{8,12},{10,14},{12... | collective-permute-start | bytes 663560 | tf_op jit(solution)/shard_map/grads_z/ppermute | solution.py:18
  100.2 0.4 collective-permute-start.24
  100.5 2.1 %collective-permute-done.21.refs_1_ = bf16[512,256]{1,0:T(8,128)(2,1)S(1)} collective-permute-done((bf16[512,256]{1,0:T(8,128)(2,1)S(1)}, bf16[512,256]{1,0:T(8,128)(2,1)S(1)}, u32[]{:S(2)}, u32[]{:S(2)}) %collective-permute-start.21) | collective-permute-done | bytes 262176 | tf_op jit(solution)/shard_map/book_a/ppermute | solution.py:18
  102.7 0.1 collective-permute-done.22.refs_3_
  102.8 0.1 shard_map.94
  102.9 1.2 collective-permute-start.26
  104.1 0.1 collective-permute-start.27
  104.2 2.3 %copy-done = bf16[3,3,512,512]{3,2,1,0:T(8,128)(2,1)S(1)} copy-done((bf16[3,3,512,512]{3,2,1,0:T(8,128)(2,1)S(1)}, bf16[3,3,512,512]{3,2,1,0:T(8,128)(2,1)}, u32[]{:S(2)}) %copy-start) | copy-done | bytes 4718616
  106.6 3.4 %shard_map.95 = bf16[512,512]{1,0:T(8,128)(2,1)} custom-call(bf16[576,512]{1,0:T(8,128)(2,1)S(1)} %get-tuple-element.105.refs_2_.hidden, bf16[3,3,512,512]{3,2,1,0:T(8,128)(2,1)S(1)} %copy-done), custom_call_target="tpu_custom_call" | custom-call | flops 301989888 | bytes 1 | tf_op jit(solution)/shard_map/pallas_call | solution.py:59
  110.0 1.4 %collective-permute-done.23 = bf16[3,3,16,768]{3,2,1,0:T(8,128)(2,1)S(1)} collective-permute-done((bf16[3,3,16,768]{3,2,1,0:T(8,128)(2,1)S(1)}, bf16[3,3,16,768]{3,2,1,0:T(8,128)(2,1)S(1)}, u32[]{:S(2)}, u32[]{:S(2)}) %collective-permute-start.23) | collective-permute-done | bytes 221216 | tf_op jit(solution)/shard_map/grads_z/ppermute | solution.py:18
  111.4 8.8 %collective-permute-done.25 = bf16[3,3,16,768]{3,2,1,0:T(8,128)(2,1)S(1)} collective-permute-done((bf16[3,3,16,768]{3,2,1,0:T(8,128)(2,1)S(1)}, bf16[3,3,16,768]{3,2,1,0:T(8,128)(2,1)S(1)}, u32[]{:S(2)}, u32[]{:S(2)}) %collective-permute-start.25) | collective-permute-done | bytes 221216 | tf_op jit(solution)/shard_map/grads_z/ppermute | solution.py:18
  120.2 0.1 add_bitcast_fusion
  120.3 0.1 shard_map.96
  120.4 0.6 collective-permute-start.28
  121.1 0.7 pad_maximum_fusion.1
  121.8 0.7 pad_maximum_fusion
  122.5 0.1 collective-permute-done.28
  122.6 0.1 broadcast_select_fusion.1
  122.7 1.5 %maximum_convert_fusion = f32[2048,256]{1,0:T(8,128)} fusion(bf16[1024,256]{1,0:T(8,128)(2,1)S(1)} %get-tuple-element.111, bf16[1024,256]{1,0:T(8,128)(2,1)S(1)} %get-tuple-element.110), kind=kLoop, calls=%fused_computation | loop fusion | flops 2097152 | bytes 3145728 | tf_op jit(solution)/shard_map/convert_element_type | solution.py:565
  (44 shorter events, 0.2 us)
Async XLA Ops:
  1.3 3.9 %copy-start.1 = (bf16[1,16,32,512]{3,2,1,0:T(8,128)(2,1)S(1)}, bf16[1,16,32,512]{3,2,1,0:T(8,128)(2,1)}, u32[]{:S(2)}) copy-start(bf16[1,16,32,512]{3,2,1,0:T(8,128)(2,1)} %param.9) | copy-start | bytes 1572868
  5.2 13.7 %collective-permute-start.2 = (bf16[512,256]{1,0:T(8,128)(2,1)}, bf16[512,256]{1,0:T(8,128)(2,1)S(1)}, u32[]{:S(2)}, u32[]{:S(2)}) collective-permute-start(bf16[512,256]{1,0:T(8,128)(2,1)} %shard_map.84), channel_id=1, source_target_pairs={{0,2},{2,0},{4,6},{6,4},{1,3},{3,1},{5,7},{7,5},{8,10},{10,8},{12,... | collective-permute-start | bytes 786440 | tf_op jit(solution)/shard_map/look_z1/ppermute | solution.py:18
  5.2 13.7 %collective-permute-start = (bf16[64,512]{1,0:T(8,128)(2,1)S(1)}, bf16[64,512]{1,0:T(8,128)(2,1)S(1)}, u32[]{:S(2)}, u32[]{:S(2)}) collective-permute-start(bf16[64,512]{1,0:T(8,128)(2,1)S(1)} %get-tuple-element.113), channel_id=1, source_target_pairs={{0,2},{2,4},{4,6},{6,8},{8,10},{10,12},{12,14},{14,16},{16,18},{18... | collective-permute-start | bytes 196616 | tf_op jit(solution)/shard_map/cot_edge/ppermute | solution.py:35
  9.7 9.2 %collective-permute-start.1 = (bf16[64,512]{1,0:T(8,128)(2,1)S(1)}, bf16[64,512]{1,0:T(8,128)(2,1)S(1)}, u32[]{:S(2)}, u32[]{:S(2)}) collective-permute-start(bf16[64,512]{1,0:T(8,128)(2,1)S(1)} %get-tuple-element.112), channel_id=1, source_target_pairs={{2,0},{4,2},{6,4},{8,6},{10,8},{12,10},{14,12},{16,14},{18,16},{20... | collective-permute-start | bytes 196616 | tf_op jit(solution)/shard_map/cot_edge/ppermute | solution.py:36
  11.7 14.3 %slice-start.2 = ((s8[4718592]{0:T(1024)(128)(4,1)}), s8[4194304]{0:T(1024)(128)(4,1)S(1)}, s32[]{:S(2)}) async-start(s8[4718592]{0:T(1024)(128)(4,1)} %bitcast.20), calls=%async_computation.2 | async-start | bytes 8388608
  11.8 14.2 %slice-start.3 = ((s8[4718592]{0:T(1024)(128)(4,1)}), s8[524288]{0:T(1024)(128)(4,1)S(1)}, s32[]{:S(2)}) async-start(s8[4718592]{0:T(1024)(128)(4,1)} %bitcast.20), calls=%async_computation.3 | async-start | bytes 1048576
  20.8 11.4 %copy-start.5 = (bf16[128,256]{1,0:T(8,128)(2,1)S(1)}, bf16[128,256]{1,0:T(8,128)(2,1)}, u32[]{:S(2)}) copy-start(bf16[128,256]{1,0:T(8,128)(2,1)} %get-tuple-element.74) | copy-start | bytes 196612
  20.8 16.9 %copy-start.4 = (bf16[384,256]{1,0:T(8,128)(2,1)S(1)}, bf16[384,256]{1,0:T(8,128)(2,1)}, u32[]{:S(2)}) copy-start(bf16[384,256]{1,0:T(8,128)(2,1)} %get-tuple-element.77) | copy-start | bytes 589828
  20.8 20.1 %copy-start.3 = (s32[8]{0:T(128)S(1)}, s32[8]{0:T(128)}, u32[]{:S(2)}) copy-start(s32[8]{0:T(128)} %stack.31.order.info.refs_0_) | copy-start | bytes 100
  20.8 8.1 %collective-permute-start.3 = (bf16[512,512]{1,0:T(8,128)(2,1)S(1)}, bf16[512,512]{1,0:T(8,128)(2,1)S(1)}, u32[]{:S(2)}, u32[]{:S(2)}) collective-permute-start(bf16[512,512]{1,0:T(8,128)(2,1)S(1)} %bitcast.23), channel_id=1, source_target_pairs={{0,8},{8,0},{16,24},{24,16},{1,9},{9,1},{17,25},{25,17},{2,10},{10... | collective-permute-start | bytes 1572872 | tf_op jit(solution)/shard_map/cot_core/ppermute | solution.py:18
  22.1 6.9 %collective-permute-start.4 = (bf16[128,256]{1,0:T(8,128)(2,1)}, bf16[128,256]{1,0:T(8,128)(2,1)S(1)}, u32[]{:S(2)}, u32[]{:S(2)}) collective-permute-start(bf16[128,256]{1,0:T(8,128)(2,1)} %get-tuple-element.75), channel_id=1, source_target_pairs={{0,2},{2,0},{4,6},{6,4},{1,3},{3,1},{5,7},{7,5},{8,10},{10,8},{12,... | collective-permute-start | bytes 196616 | tf_op jit(solution)/shard_map/look_near_ends/ppermute | solution.py:18
  23.4 8.8 %collective-permute-start.5 = (bf16[128,256]{1,0:T(8,128)(2,1)S(1)}, bf16[128,256]{1,0:T(8,128)(2,1)S(1)}, u32[]{:S(2)}, u32[]{:S(2)}) collective-permute-start(bf16[128,256]{1,0:T(8,128)(2,1)S(1)} %add_convert_fusion.2), channel_id=1, source_target_pairs={{0,4},{2,6},{4,0},{6,2},{1,5},{3,7},{5,1},{7,3},{8,12},{10,14},{12... | collective-permute-start | bytes 196616 | tf_op jit(solution)/shard_map/look_ends/ppermute | solution.py:18
  25.0 12.7 %collective-permute-start.8 = (bf16[384,256]{1,0:T(8,128)(2,1)S(1)}, bf16[384,256]{1,0:T(8,128)(2,1)S(1)}, u32[]{:S(2)}, u32[]{:S(2)}) collective-permute-start(bf16[384,256]{1,0:T(8,128)(2,1)S(1)} %add_convert_fusion.1), channel_id=1, source_target_pairs={{0,4},{2,6},{4,0},{6,2},{1,5},{3,7},{5,1},{7,3},{8,12},{10,14},{12... | collective-permute-start | bytes 589832 | tf_op jit(solution)/shard_map/look_z2/ppermute | solution.py:18
  25.7 12.0 %collective-permute-start.7 = (bf16[384,256]{1,0:T(8,128)(2,1)}, bf16[384,256]{1,0:T(8,128)(2,1)S(1)}, u32[]{:S(2)}, u32[]{:S(2)}) collective-permute-start(bf16[384,256]{1,0:T(8,128)(2,1)} %get-tuple-element.79), channel_id=1, source_target_pairs={{0,2},{2,0},{4,6},{6,4},{1,3},{3,1},{5,7},{7,5},{8,10},{10,8},{12,... | collective-permute-start | bytes 589832 | tf_op jit(solution)/shard_map/look_near/ppermute | solution.py:18
  26.0 15.0 %copy-start.2 = (bf16[3,3,256,512]{3,2,1,0:T(8,128)(2,1)S(1)}, bf16[3,3,256,512]{3,2,1,0:T(8,128)(2,1)}, u32[]{:S(2)}) copy-start(bf16[3,3,256,512]{3,2,1,0:T(8,128)(2,1)} %kernel.4) | copy-start | bytes 7077892
  26.0 50.1 %slice-start = ((s8[8388608]{0:T(1024)(128)(4,1)}), s8[4194304]{0:T(1024)(128)(4,1)S(1)}, s32[]{:S(2)}) async-start(s8[8388608]{0:T(1024)(128)(4,1)} %bitcast.16), calls=%async_computation | async-start | bytes 8388608
  32.2 5.6 %collective-permute-start.6 = (bf16[64,256]{1,0:T(8,128)(2,1)S(1)}, bf16[64,256]{1,0:T(8,128)(2,1)S(1)}, u32[]{:S(2)}, u32[]{:S(2)}) collective-permute-start(bf16[64,256]{1,0:T(8,128)(2,1)S(1)} %get-tuple-element.119.bottom), channel_id=1, source_target_pairs={{0,2},{2,4},{4,6},{6,8},{8,10},{10,12},{12,14},{14,16},{16,18},{18... | collective-permute-start | bytes 98312 | tf_op jit(solution)/shard_map/embed_edge/ppermute | solution.py:35
  34.2 6.8 %collective-permute-start.9 = (bf16[64,256]{1,0:T(8,128)(2,1)S(1)}, bf16[64,256]{1,0:T(8,128)(2,1)S(1)}, u32[]{:S(2)}, u32[]{:S(2)}) collective-permute-start(bf16[64,256]{1,0:T(8,128)(2,1)S(1)} %get-tuple-element.118.top), channel_id=1, source_target_pairs={{2,0},{4,2},{6,4},{8,6},{10,8},{12,10},{14,12},{16,14},{18,16},{20... | collective-permute-start | bytes 98312 | tf_op jit(solution)/shard_map/embed_edge/ppermute | solution.py:36
  37.8 38.2 %slice-start.1 = ((s8[8388608]{0:T(1024)(128)(4,1)}), s8[4194304]{0:T(1024)(128)(4,1)S(1)}, s32[]{:S(2)}) async-start(s8[8388608]{0:T(1024)(128)(4,1)} %bitcast.16), calls=%async_computation.1 | async-start | bytes 8388608
  45.1 4.7 %collective-permute-start.12 = (bf16[576,512]{1,0:T(8,128)(2,1)S(1)}, bf16[576,512]{1,0:T(8,128)(2,1)S(1)}, u32[]{:S(2)}, u32[]{:S(2)}) collective-permute-start(bf16[576,512]{1,0:T(8,128)(2,1)S(1)} %get-tuple-element.105.refs_2_.hidden), channel_id=1, source_target_pairs={{0,8},{8,0},{16,24},{24,16},{1,9},{9,1},{17,25},{25,17},{2,10},{10... | collective-permute-start | bytes 1769480 | tf_op jit(solution)/shard_map/hidden_core/ppermute | solution.py:18
  47.0 2.8 %collective-permute-start.13 = (bf16[512,512]{1,0:T(8,128)(2,1)S(1)}, bf16[512,512]{1,0:T(8,128)(2,1)S(1)}, u32[]{:S(2)}, u32[]{:S(2)}) collective-permute-start(bf16[512,512]{1,0:T(8,128)(2,1)S(1)} %get-tuple-element.85.refs_4_), channel_id=1, source_target_pairs={{0,8},{8,0},{16,24},{24,16},{1,9},{9,1},{17,25},{25,17},{2,10},{10... | collective-permute-start | bytes 1572872 | tf_op jit(solution)/shard_map/pre_core/ppermute | solution.py:18
  47.1 2.7 %collective-permute-start.14 = (bf16[576,256]{1,0:T(8,128)(2,1)S(1)}, bf16[576,256]{1,0:T(8,128)(2,1)S(1)}, u32[]{:S(2)}, u32[]{:S(2)}) collective-permute-start(bf16[576,256]{1,0:T(8,128)(2,1)S(1)} %get-tuple-element.86.refs_6_), channel_id=1, source_target_pairs={{0,8},{8,0},{16,24},{24,16},{1,9},{9,1},{17,25},{25,17},{2,10},{10... | collective-permute-start | bytes 884744 | tf_op jit(solution)/shard_map/field_core/ppermute | solution.py:18
  55.7 29.2 %collective-permute-start.17 = (bf16[3,3,2,64,384]{4,3,2,1,0:T(8,128)(2,1)S(1)}, bf16[3,3,2,64,384]{4,3,2,1,0:T(8,128)(2,1)S(1)}, u32[]{:S(2)}, u32[]{:S(2)}) collective-permute-start(bf16[3,3,2,64,384]{4,3,2,1,0:T(8,128)(2,1)S(1)} %get-tuple-element.94), channel_id=1, source_target_pairs={{0,1},{1,0},{2,3},{3,2},{4,5},{5,4},{6,7},{7,6},{8,9},{9,8},{10,11... | collective-permute-start | bytes 2654216 | tf_op jit(solution)/shard_map/grads_b1/ppermute | solution.py:18
  57.0 27.9 %collective-permute-start.18 = (bf16[3,3,128,384]{3,2,1,0:T(8,128)(2,1)S(1)}, bf16[3,3,128,384]{3,2,1,0:T(8,128)(2,1)S(1)}, u32[]{:S(2)}, u32[]{:S(2)}) collective-permute-start(bf16[3,3,128,384]{3,2,1,0:T(8,128)(2,1)S(1)} %bitcast.26), channel_id=1, source_target_pairs={{0,16},{8,24},{16,0},{24,8},{1,17},{9,25},{17,1},{25,9},{2,18},{10... | collective-permute-start | bytes 2654216 | tf_op jit(solution)/shard_map/grads_a1/ppermute | solution.py:18
  58.0 15.6 %collective-permute-start.10 = (bf16[512,256]{1,0:T(8,128)(2,1)S(1)}, bf16[512,256]{1,0:T(8,128)(2,1)S(1)}, u32[]{:S(2)}, u32[]{:S(2)}) collective-permute-start(bf16[512,256]{1,0:T(8,128)(2,1)S(1)} %get-tuple-element.82.own), channel_id=1, source_target_pairs={{0,4},{2,6},{4,0},{6,2},{1,5},{3,7},{5,1},{7,3},{8,12},{10,14},{12... | collective-permute-start | bytes 786440 | tf_op jit(solution)/shard_map/ge_z2/ppermute | solution.py:18
  64.2 9.4 %collective-permute-start.11 = (bf16[512,256]{1,0:T(8,128)(2,1)S(1)}, bf16[512,256]{1,0:T(8,128)(2,1)S(1)}, u32[]{:S(2)}, u32[]{:S(2)}) collective-permute-start(bf16[512,256]{1,0:T(8,128)(2,1)S(1)} %get-tuple-element.82.own), channel_id=1, source_target_pairs={{0,2},{2,0},{4,6},{6,4},{1,3},{3,1},{5,7},{7,5},{8,10},{10,8},{12,... | collective-permute-start | bytes 786440 | tf_op jit(solution)/shard_map/ge_z1/ppermute | solution.py:18
  73.6 7.5 %collective-permute-start.15 = (bf16[512,256]{1,0:T(8,128)(2,1)S(1)}, bf16[512,256]{1,0:T(8,128)(2,1)S(1)}, u32[]{:S(2)}, u32[]{:S(2)}) collective-permute-start(bf16[512,256]{1,0:T(8,128)(2,1)S(1)} %collective-permute-done.10.across), channel_id=1, source_target_pairs={{0,2},{2,0},{4,6},{6,4},{1,3},{3,1},{5,7},{7,5},{8,10},{10,8},{12,... | collective-permute-start | bytes 786440 | tf_op jit(solution)/shard_map/ge_z3/ppermute | solution.py:18
  82.6 3.8 %collective-permute-start.16 = (bf16[1024,256]{1,0:T(8,128)(2,1)S(1)}, bf16[1024,256]{1,0:T(8,128)(2,1)S(1)}, u32[]{:S(2)}, u32[]{:S(2)}) collective-permute-start(bf16[1024,256]{1,0:T(8,128)(2,1)S(1)} %get-tuple-element.91), channel_id=1, source_target_pairs={{0,8},{8,0},{16,24},{24,16},{1,9},{9,1},{17,25},{25,17},{2,10},{10... | collective-permute-start | bytes 1572872 | tf_op jit(solution)/shard_map/book_core/ppermute | solution.py:18
  85.3 11.8 %collective-permute-start.19 = (bf16[3,3,64,384]{3,2,1,0:T(8,128)(2,1)S(1)}, bf16[3,3,64,384]{3,2,1,0:T(8,128)(2,1)S(1)}, u32[]{:S(2)}, u32[]{:S(2)}) collective-permute-start(bf16[3,3,64,384]{3,2,1,0:T(8,128)(2,1)S(1)} %get-tuple-element.97), channel_id=1, source_target_pairs={{0,1},{1,0},{2,3},{3,2},{4,5},{5,4},{6,7},{7,6},{8,9},{9,8},{10,11... | collective-permute-start | bytes 1327112 | tf_op jit(solution)/shard_map/grads_a2/ppermute | solution.py:18
  85.6 11.5 %collective-permute-start.20 = (bf16[3,3,64,384]{3,2,1,0:T(8,128)(2,1)S(1)}, bf16[3,3,64,384]{3,2,1,0:T(8,128)(2,1)S(1)}, u32[]{:S(2)}, u32[]{:S(2)}) collective-permute-start(bf16[3,3,64,384]{3,2,1,0:T(8,128)(2,1)S(1)} %bitcast.27), channel_id=1, source_target_pairs={{0,16},{8,24},{16,0},{24,8},{1,17},{9,25},{17,1},{25,9},{2,18},{10... | collective-permute-start | bytes 1327112 | tf_op jit(solution)/shard_map/grads_b2/ppermute | solution.py:18
  86.5 16.1 %collective-permute-start.21 = (bf16[512,256]{1,0:T(8,128)(2,1)S(1)}, bf16[512,256]{1,0:T(8,128)(2,1)S(1)}, u32[]{:S(2)}, u32[]{:S(2)}) collective-permute-start(bf16[512,256]{1,0:T(8,128)(2,1)S(1)} %get-tuple-element.101.refs_0_), channel_id=1, source_target_pairs={{0,16},{8,24},{16,0},{24,8},{1,17},{9,25},{17,1},{25,9},{2,18},{10... | collective-permute-start | bytes 786440 | tf_op jit(solution)/shard_map/book_a/ppermute | solution.py:18
  87.3 15.5 %collective-permute-start.22 = (bf16[512,256]{1,0:T(8,128)(2,1)S(1)}, bf16[512,256]{1,0:T(8,128)(2,1)S(1)}, u32[]{:S(2)}, u32[]{:S(2)}) collective-permute-start(bf16[512,256]{1,0:T(8,128)(2,1)S(1)} %get-tuple-element.102.refs_2_), channel_id=1, source_target_pairs={{0,1},{1,0},{2,3},{3,2},{4,5},{5,4},{6,7},{7,6},{8,9},{9,8},{10,11... | collective-permute-start | bytes 786440 | tf_op jit(solution)/shard_map/book_b/ppermute | solution.py:18
  97.4 14.0 %collective-permute-start.23 = (bf16[3,3,16,768]{3,2,1,0:T(8,128)(2,1)S(1)}, bf16[3,3,16,768]{3,2,1,0:T(8,128)(2,1)S(1)}, u32[]{:S(2)}, u32[]{:S(2)}) collective-permute-start(bf16[3,3,16,768]{3,2,1,0:T(8,128)(2,1)S(1)} %get-tuple-element.106), channel_id=1, source_target_pairs={{0,4},{2,6},{4,0},{6,2},{1,5},{3,7},{5,1},{7,3},{8,12},{10,14},{12... | collective-permute-start | bytes 663560 | tf_op jit(solution)/shard_map/grads_z/ppermute | solution.py:18
  100.2 11.2 %collective-permute-start.24 = (bf16[3,3,16,768]{3,2,1,0:T(8,128)(2,1)S(1)}, bf16[3,3,16,768]{3,2,1,0:T(8,128)(2,1)S(1)}, u32[]{:S(2)}, u32[]{:S(2)}) collective-permute-start(bf16[3,3,16,768]{3,2,1,0:T(8,128)(2,1)S(1)} %get-tuple-element.107), channel_id=1, source_target_pairs={{0,2},{2,0},{4,6},{6,4},{1,3},{3,1},{5,7},{7,5},{8,10},{10,8},{12,... | collective-permute-start | bytes 663560 | tf_op jit(solution)/shard_map/grads_z/ppermute | solution.py:18
  100.5 19.6 %collective-permute-start.25 = (bf16[3,3,16,768]{3,2,1,0:T(8,128)(2,1)S(1)}, bf16[3,3,16,768]{3,2,1,0:T(8,128)(2,1)S(1)}, u32[]{:S(2)}, u32[]{:S(2)}) collective-permute-start(bf16[3,3,16,768]{3,2,1,0:T(8,128)(2,1)S(1)} %get-tuple-element.108), channel_id=1, source_target_pairs={{0,6},{2,4},{4,2},{6,0},{1,7},{3,5},{5,3},{7,1},{8,14},{10,12},{12... | collective-permute-start | bytes 663560 | tf_op jit(solution)/shard_map/grads_z/ppermute | solution.py:18
  102.9 17.4 %collective-permute-start.26 = (bf16[512,256]{1,0:T(8,128)(2,1)S(1)}, bf16[512,256]{1,0:T(8,128)(2,1)S(1)}, u32[]{:S(2)}, u32[]{:S(2)}) collective-permute-start(bf16[512,256]{1,0:T(8,128)(2,1)S(1)} %get-tuple-element.109.refs_0_), channel_id=1, source_target_pairs={{0,1},{1,0},{2,3},{3,2},{4,5},{5,4},{6,7},{7,6},{8,9},{9,8},{10,11... | collective-permute-start | bytes 786440 | tf_op jit(solution)/shard_map/book_a/ppermute | solution.py:18
  104.1 16.2 %collective-permute-start.27 = (bf16[512,256]{1,0:T(8,128)(2,1)S(1)}, bf16[512,256]{1,0:T(8,128)(2,1)S(1)}, u32[]{:S(2)}, u32[]{:S(2)}) collective-permute-start(bf16[512,256]{1,0:T(8,128)(2,1)S(1)} %get-tuple-element.104.refs_2_), channel_id=1, source_target_pairs={{0,16},{8,24},{16,0},{24,8},{1,17},{9,25},{17,1},{25,9},{2,18},{10... | collective-permute-start | bytes 786440 | tf_op jit(solution)/shard_map/book_b/ppermute | solution.py:18
  104.2 2.3 %copy-start = (bf16[3,3,512,512]{3,2,1,0:T(8,128)(2,1)S(1)}, bf16[3,3,512,512]{3,2,1,0:T(8,128)(2,1)}, u32[]{:S(2)}) copy-start(bf16[3,3,512,512]{3,2,1,0:T(8,128)(2,1)} %kernel.5) | copy-start | bytes 14155780
  120.4 2.2 %collective-permute-start.28 = (bf16[1024,256]{1,0:T(8,128)(2,1)S(1)}, bf16[1024,256]{1,0:T(8,128)(2,1)S(1)}, u32[]{:S(2)}, u32[]{:S(2)}) collective-permute-start(bf16[1024,256]{1,0:T(8,128)(2,1)S(1)} %shard_map.96), channel_id=1, source_target_pairs={{0,8},{8,0},{16,24},{24,16},{1,9},{9,1},{17,25},{25,17},{2,10},{10... | collective-permute-start | bytes 1572872 | tf_op jit(solution)/shard_map/book_back/ppermute | solution.py:18

commit v4 on v3

--- a/solution.py
+++ b/solution.py
@@ -112,10 +112,12 @@
 
         @pl.when((step == last) & (shard == k))
         def _():
-            if len(outs) == 1:
+            if len(outs) == count:
+                ends, inner = outs[k].at[: 2 * edge], outs[k].at[2 * edge :]
+            elif k == 0:
                 ends, inner = outs[0].at[: 2 * edge], outs[0].at[2 * edge :]
             else:
-                ends, inner = outs[2 * k], outs[2 * k + 1]
+                ends, inner = outs[2 * k - 1], outs[2 * k]
             ends[:edge] = total[:edge].astype(NARROW)
             ends[edge:] = total[-edge:].astype(NARROW)
             inner[...] = total[edge:-edge].astype(NARROW)
@@ -125,7 +127,7 @@
     codes, inner = codebook.shape
     count = len(places)
     first = places[0]
-    rows = [cells] if count == 1 else [2 * edge, cells - 2 * edge] * count
+    rows = [cells] + [2 * edge, cells - 2 * edge] * (count - 1)
     return pl.pallas_call(
         functools.partial(lookup_body, count, edge),
         grid_spec=pltpu.PrefetchScalarGridSpec(
@@ -192,7 +194,7 @@
         for b in (1, 0, 2)
     )
     row = lax.broadcasted_iota(jnp.int32, pre.shape, 0)
-    inside = ((row >= breadth) | (info[4] > 0)) & ((row < tall - breadth) | (info[5] > 0))
+    inside = ((row >= breadth) | (info[7] > 0)) & ((row < tall - breadth) | (info[8] > 0))
     sigma = 1.0 / (1.0 + jnp.exp(-pre))
     hidden[...] = jnp.where(inside, pre * sigma, 0.0).astype(NARROW)
     slope = grad_hidden[...] * (sigma * (1.0 + pre * (1.0 - sigma)))
@@ -268,7 +270,7 @@
 def book_end_body(info, weights, corner, base, mine, other, total):
     total[...] = base[...] + term_of(info, 0, weights, corner)
     half = mine.shape[0]
-    core = info[6]
+    core = info[9]
     mine[...] = total[pl.ds(pl.multiple_of(core * half, half), half), :].astype(NARROW)
     other[...] = total[pl.ds(pl.multiple_of((1 - core) * half, half), half), :].astype(NARROW)
 
@@ -483,36 +485,35 @@
     place = space * 4 + code
     last = lax.axis_size("space") * 4 - 1
     flat = lambda field: field.reshape(-1, field.shape[2])
-    info = jnp.stack([code ^ 3, code ^ 2, code ^ 1, code, place, last - place, space % 2, 0])
+    info = jnp.stack(
+        [code ^ 3, code ^ 2, code ^ 1, code, code ^ 1, code ^ 2, code, place, last - place, space % 2]
+    )
     info = info.astype(jnp.int32)
 
     edge = 2 * breadth
     (third,) = lookup((0,), info, weights, codebook, cells, edge, 2)
     from_pair = swap(third, "code", 1, "look_z1")
-    upstream = after(own_up, third)
-    cot_low, cot_high = edges(upstream[:edge], upstream[-edge:], "cot_edge")
-    shards = lookup((1, 2, 3), info, weights, after(codebook, third), cells, edge, 1)
+    shards = lookup((4, 5, 6), info, weights, after(codebook, third), cells, edge, 1)
     pick = after(own_channels(width), shards[0])
-    (second_ends, second, beside_ends, beside, own_ends, own), pick, cot_low, cot_high = (
-        lax.optimization_barrier((shards, pick, cot_low, cot_high))
+    (beside, second_ends, second, own_ends, own), pick = lax.optimization_barrier(
+        (shards, pick)
     )
     middle_ends = plus(second_ends, from_pair[: 2 * edge])
     far_ends = swap(middle_ends, "code", 2, "look_ends")
-    near_ends = swap(beside_ends, "code", 1, "look_near_ends")
+    near = swap(beside, "code", 1, "look_near")
     middle = plus(after(second, middle_ends), from_pair[2 * edge :])
     far = swap(middle, "code", 2, "look_z2")
-    near = swap(after(beside, middle), "code", 1, "look_near")
-    grad_hidden = upstream_back(after(own_up, middle), cot_low, cot_high, kernel_two, breadth)
-    far_up = swap(after(own_up, middle), "space", 1, "cot_core")
-    own_ends, own, grad_hidden, far_up = lax.optimization_barrier(
-        (own_ends, own, grad_hidden, far_up)
-    )
+    upstream = after(own_up, middle)
+    cot_low, cot_high = edges(upstream[:edge], upstream[-edge:], "cot_edge")
     part = lambda k: slice(k * edge, (k + 1) * edge)
     top, bottom = [
-        plus(own_ends[part(k)], near_ends[part(k)], far_ends[part(k)]) for k in range(2)
+        plus(own_ends[part(k)], near[part(k)], far_ends[part(k)]) for k in range(2)
     ]
     low, high = edges(top, bottom, "embed_edge")
-    inner = plus(after(own, top, bottom), near, far)
+    upstream = after(own_up, top, bottom)
+    far_up = swap(after(own_up, top), "space", 1, "cot_core")
+    grad_hidden = upstream_back(upstream, cot_low, cot_high, kernel_two, breadth)
+    inner = plus(after(own, top, bottom), near[2 * edge :], far)
     hidden, own_pre, field, grad_embedded = head(
         info, (low, top, inner, bottom, high), kernel_one, grad_hidden, breadth
     )
@@ -533,7 +534,9 @@
     grads = Spread(grads, "grads")
     corner = swap(across, "code", 1, "ge_z3")
     term = book_start(info, weights, grad_embedded, beside, across)
-    ((mine, other),) = fuse(book_end(info, weights, corner, term))
+    (outs,) = fuse(grads.turn())
+    grads.turned(outs)
+    ((mine, other),) = fuse(book_end(info, weights, corner, after(term, grads.first)))
     got = swap(other, "space", 1, "book_core")
     ((first, second),) = fuse(halves(mine, got))
 
@@ -546,14 +549,11 @@
     for k, (way, back) in enumerate(ways):
         got_first, got_second = swap(first, *way, "book_a"), swap(second, *back, "book_b")
         if k == 0:
-            (outs,) = fuse(grads.turn())
-            grads.turned(outs)
+            decoded = decode(after(hidden, first), kernel_two, breadth)
+            grads.second = after(grads.second, decoded)
             (outs,) = fuse(grads.along())
             grads.sent(outs)
             first = after(first, grads.last)
-        elif k == len(ways) - 1:
-            decoded = decode(after(hidden, first, second), kernel_two, breadth)
-            first = after(first, decoded)
         (outs,) = fuse(pair(first, got_first, second, got_second, k == len(ways) - 1))
         if k < len(ways) - 1:
             first, second = outs

time: 125 us -> 119 us (0.952)
  starting transfers between devices: 40 us -> 36.6 us
  local copies, waits for them, and re-layouts: 3.11 us -> 0.76 us
    ppermute x25 -> x24, starting transfers between devices: 28.2 us -> 23.6 us  [swap(): lax.ppermute(value, axis, [(i, i ^ bits) for i in range(lax.axis_size(axi...]
    ppermute x2, waiting for transfers between devices: 3.07 us -> 0.01 us  [edges(): high = lax.ppermute(top, axes, backward)]
    ppermute x25 -> x24, waiting for transfers between devices: 39.3 us -> 41.8 us  [swap(): lax.ppermute(value, axis, [(i, i ^ bits) for i in range(lax.axis_size(axi...]
    unnamed x20 -> x16, local copies, waits for them, and re-layouts: 2.39 us -> 0.05 us
  transfers between devices with their start and end apart: 29 -> 28, of which waited for: 12 -> 10; matrix products, arithmetic and copies ran while one was open for 1% -> 4% of each run, Pallas kernels for 15% -> 14%
where the time goes in v4:
time: 119 us
  waiting for transfers between devices  41.8 us (35%)
  starting transfers between devices  36.6 us (31%)
  Pallas kernels  32.6 us (27%)
  other arithmetic  5.93 us (5%)
    ppermute x24, waiting for transfers between devices, swap(): lax.ppermute(value, axis, [(i, i ^ bits) for i in range(lax.axis_size(axi...  41.8 us
    ppermute x24, starting transfers between devices, swap(): lax.ppermute(value, axis, [(i, i ^ bits) for i in range(lax.axis_size(axi...  23.6 us
    pallas_call x11, Pallas kernels, call(): pl.pallas_call(body, in_specs=[pl.BlockSpec(memory_space=space) for space...  21.8 us
    pallas_call x2, Pallas kernels, lookup(): pl.pallas_call(functools.partial(lookup_body, count, edge), grid_spec=plt...  10.8 us
    ppermute x2, starting transfers between devices, edges(): high = lax.ppermute(top, axes, backward)  6.56 us
    ppermute x2, starting transfers between devices, edges(): low = lax.ppermute(bottom, axes, forward)  6.41 us
    convert_element_type x4, other arithmetic, plus(): return sum((term.astype(WIDE) for term in terms)).astype(NARROW)  2.71 us
  transfers between devices with their start and end apart: 28, of which 10 were waited for; matrix products, arithmetic and copies ran while one was open for 4% of the time, Pallas kernels for 14%

profile of v4, /device:TPU:9, one launch (start us, length us, event | category | flops | bytes accessed | tf_op | source)
XLA Modules:
  0.0 118.6 jit_solution(18312944798035610277)
XLA Ops:
  0.6 0.7 stack.34.order.info.refs_0_
  1.3 3.7 %shard_map.84 = bf16[512,256]{1,0:T(8,128)(2,1)} custom-call(s32[10]{0:T(128)} %stack.34.order.info.refs_0_, bf16[2048,2048]{1,0:T(8,128)(2,1)} %bitcast.14, bf16[2048,256]{1,0:T(8,128)(2,1)} %codebook.2), custom_call_target="tpu_custom_call" | custom-call | flops 67108864 | bytes 1 | tf_op jit(solution)/shard_map/pallas_call | solution.py:131
  5.1 0.0 copy-start
  5.1 0.0 slice-start.3
  5.1 7.1 %shard_map.85 = (bf16[512,256]{1,0:T(8,128)(2,1)}, bf16[128,256]{1,0:T(8,128)(2,1)}, bf16[384,256]{1,0:T(8,128)(2,1)}, bf16[128,256]{1,0:T(8,128)(2,1)}, bf16[384,256]{1,0:T(8,128)(2,1)}) custom-call(s32[10]{0:T(128)} %stack.34.order.info.refs_0_, bf16[2048,2048]{1,0:T(8,128)(2,1)} %bitcast.15, bf16[2048,256]{1,0:T(8,128)(2,1)} %codebook.2), custom_call_target="tpu_custom_call" | custom-call | flops 201326592 | bytes 1 | tf_op jit(solution)/shard_map/pallas_call | solution.py:131
  12.1 0.1 fusion.pick
  12.3 1.5 %collective-permute-start = (bf16[512,256]{1,0:T(8,128)(2,1)}, bf16[512,256]{1,0:T(8,128)(2,1)S(1)}, u32[]{:S(2)}, u32[]{:S(2)}) collective-permute-start(bf16[512,256]{1,0:T(8,128)(2,1)} %get-tuple-element.58), channel_id=1, source_target_pairs={{0,2},{2,0},{4,6},{6,4},{1,3},{3,1},{5,7},{7,5},{8,10},{10,8},{12,... | collective-permute-start | bytes 786440 | tf_op jit(solution)/shard_map/look_near/ppermute | solution.py:18
  13.8 0.9 add_convert_fusion.2
  14.7 2.4 %collective-permute-start.2 = (bf16[128,256]{1,0:T(8,128)(2,1)S(1)}, bf16[128,256]{1,0:T(8,128)(2,1)S(1)}, u32[]{:S(2)}, u32[]{:S(2)}) collective-permute-start(bf16[128,256]{1,0:T(8,128)(2,1)S(1)} %add_convert_fusion.2), channel_id=1, source_target_pairs={{0,4},{2,6},{4,0},{6,2},{1,5},{3,7},{5,1},{7,3},{8,12},{10,14},{12... | collective-permute-start | bytes 196616 | tf_op jit(solution)/shard_map/look_ends/ppermute | solution.py:18
  17.0 1.0 add_convert_fusion.1
  18.0 0.1 collective-permute-start.4
  18.1 3.2 %collective-permute-start.6 = (bf16[64,512]{1,0:T(8,128)(2,1)S(1)}, bf16[64,512]{1,0:T(8,128)(2,1)S(1)}, u32[]{:S(2)}, u32[]{:S(2)}) collective-permute-start(bf16[64,512]{1,0:T(8,128)(2,1)S(1)} %get-tuple-element.99), channel_id=1, source_target_pairs={{0,2},{2,4},{4,6},{6,8},{8,10},{10,12},{12,14},{14,16},{16,18},{18... | collective-permute-start | bytes 196616 | tf_op jit(solution)/shard_map/cot_edge/ppermute | solution.py:35
  21.4 2.1 %collective-permute-start.7 = (bf16[64,512]{1,0:T(8,128)(2,1)S(1)}, bf16[64,512]{1,0:T(8,128)(2,1)S(1)}, u32[]{:S(2)}, u32[]{:S(2)}) collective-permute-start(bf16[64,512]{1,0:T(8,128)(2,1)S(1)} %get-tuple-element.98), channel_id=1, source_target_pairs={{2,0},{4,2},{6,4},{8,6},{10,8},{12,10},{14,12},{16,14},{18,16},{20... | collective-permute-start | bytes 196616 | tf_op jit(solution)/shard_map/cot_edge/ppermute | solution.py:36
  23.5 0.8 add_convert_fusion.3
  24.3 3.2 %collective-permute-start.3 = (bf16[64,256]{1,0:T(8,128)(2,1)S(1)}, bf16[64,256]{1,0:T(8,128)(2,1)S(1)}, u32[]{:S(2)}, u32[]{:S(2)}) collective-permute-start(bf16[64,256]{1,0:T(8,128)(2,1)S(1)} %get-tuple-element.105.bottom), channel_id=1, source_target_pairs={{0,2},{2,4},{4,6},{6,8},{8,10},{10,12},{12,14},{14,16},{16,18},{18... | collective-permute-start | bytes 98312 | tf_op jit(solution)/shard_map/embed_edge/ppermute | solution.py:35
  27.5 0.0 copy-start.1
  27.5 4.5 %collective-permute-start.5 = (bf16[64,256]{1,0:T(8,128)(2,1)S(1)}, bf16[64,256]{1,0:T(8,128)(2,1)S(1)}, u32[]{:S(2)}, u32[]{:S(2)}) collective-permute-start(bf16[64,256]{1,0:T(8,128)(2,1)S(1)} %get-tuple-element.104.top), channel_id=1, source_target_pairs={{2,0},{4,2},{6,4},{8,6},{10,8},{12,10},{14,12},{16,14},{18,16},{20... | collective-permute-start | bytes 98312 | tf_op jit(solution)/shard_map/embed_edge/ppermute | solution.py:36
  32.1 0.0 slice-start
  32.1 2.9 %shard_map.86.grad_hidden = f32[576,512]{1,0:T(8,128)S(1)} custom-call(bf16[512,512]{1,0:T(8,128)(2,1)S(1)} %bitcast.23, bf16[64,512]{1,0:T(8,128)(2,1)S(1)} %collective-permute-done.6.low, bf16[64,512]{1,0:T(8,128)(2,1)S(1)} %collective-permute-done.7.high, bf16[3,3,512,512]{3,2,1,0:T(8,128)(2,1)S(1)} %bitcast.21), custom_call_target="tpu_custom_call" | custom-call | flops 301989888 | bytes 1 | tf_op jit(solution)/shard_map/pallas_call | solution.py:59
  35.0 0.1 add_convert_fusion.inner
  35.1 0.0 slice-start.1
  35.2 4.2 %shard_map.87 = (bf16[576,512]{1,0:T(8,128)(2,1)S(1)}, bf16[512,512]{1,0:T(8,128)(2,1)S(1)}, bf16[576,256]{1,0:T(8,128)(2,1)S(1)}, bf16[512,256]{1,0:T(8,128)(2,1)S(1)}) custom-call(s32[10]{0:T(128)S(1)} %copy-done.2, bf16[64,256]{1,0:T(8,128)(2,1)S(1)} %collective-permute-done.3.low, bf16[64,256]{1,0:T(8,128)(2,1)S(1)} %get-tuple-element.104.top, ...), custom_call_target="tpu_custom_call" | custom-call | flops 301989888 | bytes 1 | tf_op jit(solution)/shard_map/pallas_call | solution.py:59
  39.4 1.9 %collective-permute-start.11 = (bf16[576,512]{1,0:T(8,128)(2,1)S(1)}, bf16[576,512]{1,0:T(8,128)(2,1)S(1)}, u32[]{:S(2)}, u32[]{:S(2)}) collective-permute-start(bf16[576,512]{1,0:T(8,128)(2,1)S(1)} %get-tuple-element.83.refs_2_.hidden), channel_id=1, source_target_pairs={{0,8},{8,0},{16,24},{24,16},{1,9},{9,1},{17,25},{25,17},{2,10},{10... | collective-permute-start | bytes 1769480 | tf_op jit(solution)/shard_map/hidden_core/ppermute | solution.py:18
  41.2 0.1 collective-permute-start.10
  41.3 0.4 collective-permute-start.12
  41.8 0.1 collective-permute-start.13
  41.8 3.0 %collective-permute-done.13.refs_7_ = bf16[576,256]{1,0:T(8,128)(2,1)S(1)} collective-permute-done((bf16[576,256]{1,0:T(8,128)(2,1)S(1)}, bf16[576,256]{1,0:T(8,128)(2,1)S(1)}, u32[]{:S(2)}, u32[]{:S(2)}) %collective-permute-start.13) | collective-permute-done | bytes 294944 | tf_op jit(solution)/shard_map/field_core/ppermute | solution.py:18
  44.8 6.1 %shard_map.88 = (bf16[3,3,128,384]{3,2,1,0:T(8,128)(2,1)S(1)}, bf16[1,3,3,128,384]{4,3,2,1,0:T(8,128)(2,1)S(1)}, bf16[3,3,2,64,384]{4,3,2,1,0:T(8,128)(2,1)S(1)}, bf16[3,3,2,64,384]{4,3,2,1,0:T(8,128)(2,1)S(1)}) custom-call(bf16[256,512]{1,0:T(8,128)(2,1)S(1)} %fusion.pick, bf16[512,512]{1,0:T(8,128)(2,1)S(1)} %bitcast.25, ...), custom_call_target="tpu_custom_call" | custom-call | flops 509607936 | bytes 1 | tf_op jit(solution)/shard_map/pallas_call | solution.py:59
  50.9 1.3 %collective-permute-start.15 = (bf16[3,3,2,64,384]{4,3,2,1,0:T(8,128)(2,1)S(1)}, bf16[3,3,2,64,384]{4,3,2,1,0:T(8,128)(2,1)S(1)}, u32[]{:S(2)}, u32[]{:S(2)}) collective-permute-start(bf16[3,3,2,64,384]{4,3,2,1,0:T(8,128)(2,1)S(1)} %get-tuple-element.76), channel_id=1, source_target_pairs={{0,1},{1,0},{2,3},{3,2},{4,5},{5,4},{6,7},{7,6},{8,9},{9,8},{10,11... | collective-permute-start | bytes 2654216 | tf_op jit(solution)/shard_map/grads_b1/ppermute | solution.py:18
  52.2 0.9 collective-permute-start.16
  53.1 4.6 %collective-permute-start.8 = (bf16[512,256]{1,0:T(8,128)(2,1)S(1)}, bf16[512,256]{1,0:T(8,128)(2,1)S(1)}, u32[]{:S(2)}, u32[]{:S(2)}) collective-permute-start(bf16[512,256]{1,0:T(8,128)(2,1)S(1)} %get-tuple-element.67.own), channel_id=1, source_target_pairs={{0,4},{2,6},{4,0},{6,2},{1,5},{3,7},{5,1},{7,3},{8,12},{10,14},{12... | collective-permute-start | bytes 786440 | tf_op jit(solution)/shard_map/ge_z2/ppermute | solution.py:18
  57.7 11.0 %collective-permute-done.8.across = bf16[512,256]{1,0:T(8,128)(2,1)S(1)} collective-permute-done((bf16[512,256]{1,0:T(8,128)(2,1)S(1)}, bf16[512,256]{1,0:T(8,128)(2,1)S(1)}, u32[]{:S(2)}, u32[]{:S(2)}) %collective-permute-start.8) | collective-permute-done | bytes 262176 | tf_op jit(solution)/shard_map/ge_z2/ppermute | solution.py:18
  68.7 2.7 %collective-permute-start.14 = (bf16[512,256]{1,0:T(8,128)(2,1)S(1)}, bf16[512,256]{1,0:T(8,128)(2,1)S(1)}, u32[]{:S(2)}, u32[]{:S(2)}) collective-permute-start(bf16[512,256]{1,0:T(8,128)(2,1)S(1)} %collective-permute-done.8.across), channel_id=1, source_target_pairs={{0,2},{2,0},{4,6},{6,4},{1,3},{3,1},{5,7},{7,5},{8,10},{10,8},{12,... | collective-permute-start | bytes 786440 | tf_op jit(solution)/shard_map/ge_z3/ppermute | solution.py:18
  71.4 2.6 %shard_map.89.refs_3_ = f32[2048,256]{1,0:T(8,128)S(1)} custom-call(s32[10]{0:T(128)S(1)} %copy-done.2, bf16[2048,2048]{1,0:T(8,128)(2,1)S(1)} %bitcast.18, bf16[512,256]{1,0:T(8,128)(2,1)S(1)} %get-tuple-element.67.own, bf16[512,256]{1,0:T(8,128)(2,1)S(1)} %collective-permute-done.9.beside, bf16[512,256]{1,0:T(8,128)(2,1)S(1)} %collective-permute-done.8.across), custom_call_target="tpu_custom_call" | custom-call | flops 201326592 | bytes 1 | tf_op jit(solution)/shard_map/pallas_call | solution.py:59
  74.0 0.5 shard_map.90
  74.5 2.9 %collective-permute-done.14.refs_2_ = bf16[512,256]{1,0:T(8,128)(2,1)S(1)} collective-permute-done((bf16[512,256]{1,0:T(8,128)(2,1)S(1)}, bf16[512,256]{1,0:T(8,128)(2,1)S(1)}, u32[]{:S(2)}, u32[]{:S(2)}) %collective-permute-start.14) | collective-permute-done | bytes 262176 | tf_op jit(solution)/shard_map/ge_z3/ppermute | solution.py:18
  77.3 1.5 %shard_map.91 = (bf16[1024,256]{1,0:T(8,128)(2,1)S(1)}, bf16[1024,256]{1,0:T(8,128)(2,1)S(1)}) custom-call(s32[10]{0:T(128)S(1)} %copy-done.2, bf16[2048,2048]{1,0:T(8,128)(2,1)S(1)} %bitcast.19, bf16[512,256]{1,0:T(8,128)(2,1)S(1)} %collective-permute-done.14.refs_2_, f32[2048,256]{1,0:T(8,128)S(1)} %shard_map.89.refs_3_), custom_call_target="tpu_custom_call" | custom-call | flops 100000000 | bytes 1 | tf_op jit(solution)/shard_map/pallas_call | solution.py:59
  78.8 1.4 %collective-permute-start.17 = (bf16[1024,256]{1,0:T(8,128)(2,1)S(1)}, bf16[1024,256]{1,0:T(8,128)(2,1)S(1)}, u32[]{:S(2)}, u32[]{:S(2)}) collective-permute-start(bf16[1024,256]{1,0:T(8,128)(2,1)S(1)} %get-tuple-element.81), channel_id=1, source_target_pairs={{0,8},{8,0},{16,24},{24,16},{1,9},{9,1},{17,25},{25,17},{2,10},{10... | collective-permute-start | bytes 1572872 | tf_op jit(solution)/shard_map/book_core/ppermute | solution.py:18
  80.2 0.2 collective-permute-start.18
  80.4 1.3 %collective-permute-done.17.refs_1_ = bf16[1024,256]{1,0:T(8,128)(2,1)S(1)} collective-permute-done((bf16[1024,256]{1,0:T(8,128)(2,1)S(1)}, bf16[1024,256]{1,0:T(8,128)(2,1)S(1)}, u32[]{:S(2)}, u32[]{:S(2)}) %collective-permute-start.17) | collective-permute-done | bytes 524320 | tf_op jit(solution)/shard_map/book_core/ppermute | solution.py:18
  81.7 0.1 shard_map.92
  81.8 0.2 collective-permute-start.23
  82.1 1.2 %collective-permute-start.24 = (bf16[512,256]{1,0:T(8,128)(2,1)S(1)}, bf16[512,256]{1,0:T(8,128)(2,1)S(1)}, u32[]{:S(2)}, u32[]{:S(2)}) collective-permute-start(bf16[512,256]{1,0:T(8,128)(2,1)S(1)} %get-tuple-element.93.refs_2_), channel_id=1, source_target_pairs={{0,1},{1,0},{2,3},{3,2},{4,5},{5,4},{6,7},{7,6},{8,9},{9,8},{10,11... | collective-permute-start | bytes 786440 | tf_op jit(solution)/shard_map/book_b/ppermute | solution.py:18
  83.3 3.4 %shard_map.93 = bf16[512,512]{1,0:T(8,128)(2,1)} custom-call(bf16[576,512]{1,0:T(8,128)(2,1)S(1)} %get-tuple-element.83.refs_2_.hidden, bf16[3,3,512,512]{3,2,1,0:T(8,128)(2,1)S(1)} %bitcast.21), custom_call_target="tpu_custom_call" | custom-call | flops 301989888 | bytes 1 | tf_op jit(solution)/shard_map/pallas_call | solution.py:59
  86.7 5.2 %collective-permute-done.18.refs_1_ = bf16[3,3,64,384]{3,2,1,0:T(8,128)(2,1)S(1)} collective-permute-done((bf16[3,3,64,384]{3,2,1,0:T(8,128)(2,1)S(1)}, bf16[3,3,64,384]{3,2,1,0:T(8,128)(2,1)S(1)}, u32[]{:S(2)}, u32[]{:S(2)}) %collective-permute-start.18) | collective-permute-done | bytes 442400 | tf_op jit(solution)/shard_map/grads_a2/ppermute | solution.py:18
  91.9 0.2 shard_map.94
  92.2 2.0 %collective-permute-start.20 = (bf16[3,3,16,768]{3,2,1,0:T(8,128)(2,1)S(1)}, bf16[3,3,16,768]{3,2,1,0:T(8,128)(2,1)S(1)}, u32[]{:S(2)}, u32[]{:S(2)}) collective-permute-start(bf16[3,3,16,768]{3,2,1,0:T(8,128)(2,1)S(1)} %get-tuple-element.88), channel_id=1, source_target_pairs={{0,4},{2,6},{4,0},{6,2},{1,5},{3,7},{5,1},{7,3},{8,12},{10,14},{12... | collective-permute-start | bytes 663560 | tf_op jit(solution)/shard_map/grads_z/ppermute | solution.py:18
  94.1 0.0 collective-permute-start.21
  94.1 0.7 collective-permute-start.22
  94.9 2.6 %collective-permute-done.23.refs_1_ = bf16[512,256]{1,0:T(8,128)(2,1)S(1)} collective-permute-done((bf16[512,256]{1,0:T(8,128)(2,1)S(1)}, bf16[512,256]{1,0:T(8,128)(2,1)S(1)}, u32[]{:S(2)}, u32[]{:S(2)}) %collective-permute-start.23) | collective-permute-done | bytes 262176 | tf_op jit(solution)/shard_map/book_a/ppermute | solution.py:18
  97.5 0.1 collective-permute-done.24.refs_3_
  97.6 0.1 shard_map.95
  97.7 1.2 %collective-permute-start.25 = (bf16[512,256]{1,0:T(8,128)(2,1)S(1)}, bf16[512,256]{1,0:T(8,128)(2,1)S(1)}, u32[]{:S(2)}, u32[]{:S(2)}) collective-permute-start(bf16[512,256]{1,0:T(8,128)(2,1)S(1)} %get-tuple-element.94.refs_0_), channel_id=1, source_target_pairs={{0,1},{1,0},{2,3},{3,2},{4,5},{5,4},{6,7},{7,6},{8,9},{9,8},{10,11... | collective-permute-start | bytes 786440 | tf_op jit(solution)/shard_map/book_a/ppermute | solution.py:18
  98.9 0.0 collective-permute-start.26
  98.9 6.5 %collective-permute-done.20 = bf16[3,3,16,768]{3,2,1,0:T(8,128)(2,1)S(1)} collective-permute-done((bf16[3,3,16,768]{3,2,1,0:T(8,128)(2,1)S(1)}, bf16[3,3,16,768]{3,2,1,0:T(8,128)(2,1)S(1)}, u32[]{:S(2)}, u32[]{:S(2)}) %collective-permute-start.20) | collective-permute-done | bytes 221216 | tf_op jit(solution)/shard_map/grads_z/ppermute | solution.py:18
  105.4 9.3 %collective-permute-done.22 = bf16[3,3,16,768]{3,2,1,0:T(8,128)(2,1)S(1)} collective-permute-done((bf16[3,3,16,768]{3,2,1,0:T(8,128)(2,1)S(1)}, bf16[3,3,16,768]{3,2,1,0:T(8,128)(2,1)S(1)}, u32[]{:S(2)}, u32[]{:S(2)}) %collective-permute-start.22) | collective-permute-done | bytes 221216 | tf_op jit(solution)/shard_map/grads_z/ppermute | solution.py:18
  114.7 0.1 add_bitcast_fusion
  114.8 0.1 shard_map.96
  114.9 0.6 collective-permute-start.27
  115.5 0.7 pad_maximum_fusion.1
  116.2 0.7 pad_maximum_fusion
  117.0 0.1 collective-permute-done.27
  117.1 0.1 broadcast_select_fusion.1
  117.1 1.5 %maximum_convert_fusion = f32[2048,256]{1,0:T(8,128)} fusion(bf16[1024,256]{1,0:T(8,128)(2,1)S(1)} %get-tuple-element.97, bf16[1024,256]{1,0:T(8,128)(2,1)S(1)} %get-tuple-element.96), kind=kLoop, calls=%fused_computation | loop fusion | flops 2097152 | bytes 3145728 | tf_op jit(solution)/shard_map/convert_element_type | solution.py:565
  (38 shorter events, 0.1 us)
Async XLA Ops:
  5.0 8.7 %collective-permute-start.1 = (bf16[512,256]{1,0:T(8,128)(2,1)}, bf16[512,256]{1,0:T(8,128)(2,1)S(1)}, u32[]{:S(2)}, u32[]{:S(2)}) collective-permute-start(bf16[512,256]{1,0:T(8,128)(2,1)} %shard_map.84), channel_id=1, source_target_pairs={{0,2},{2,0},{4,6},{6,4},{1,3},{3,1},{5,7},{7,5},{8,10},{10,8},{12,... | collective-permute-start | bytes 786440 | tf_op jit(solution)/shard_map/look_z1/ppermute | solution.py:18
  5.1 27.0 %slice-start.2 = ((s8[4718592]{0:T(1024)(128)(4,1)}), s8[4194304]{0:T(1024)(128)(4,1)S(1)}, s32[]{:S(2)}) async-start(s8[4718592]{0:T(1024)(128)(4,1)} %bitcast.20), calls=%async_computation.2 | async-start | bytes 8388608
  5.1 13.1 %copy-start = (bf16[1,16,32,512]{3,2,1,0:T(8,128)(2,1)S(1)}, bf16[1,16,32,512]{3,2,1,0:T(8,128)(2,1)}, u32[]{:S(2)}) copy-start(bf16[1,16,32,512]{3,2,1,0:T(8,128)(2,1)} %param.9) | copy-start | bytes 1572868
  5.1 27.0 %slice-start.3 = ((s8[4718592]{0:T(1024)(128)(4,1)}), s8[524288]{0:T(1024)(128)(4,1)S(1)}, s32[]{:S(2)}) async-start(s8[4718592]{0:T(1024)(128)(4,1)} %bitcast.20), calls=%async_computation.3 | async-start | bytes 1048576
  12.3 11.2 %collective-permute-start = (bf16[512,256]{1,0:T(8,128)(2,1)}, bf16[512,256]{1,0:T(8,128)(2,1)S(1)}, u32[]{:S(2)}, u32[]{:S(2)}) collective-permute-start(bf16[512,256]{1,0:T(8,128)(2,1)} %get-tuple-element.58), channel_id=1, source_target_pairs={{0,2},{2,0},{4,6},{6,4},{1,3},{3,1},{5,7},{7,5},{8,10},{10,8},{12,... | collective-permute-start | bytes 786440 | tf_op jit(solution)/shard_map/look_near/ppermute | solution.py:18
  14.7 8.8 %collective-permute-start.2 = (bf16[128,256]{1,0:T(8,128)(2,1)S(1)}, bf16[128,256]{1,0:T(8,128)(2,1)S(1)}, u32[]{:S(2)}, u32[]{:S(2)}) collective-permute-start(bf16[128,256]{1,0:T(8,128)(2,1)S(1)} %add_convert_fusion.2), channel_id=1, source_target_pairs={{0,4},{2,6},{4,0},{6,2},{1,5},{3,7},{5,1},{7,3},{8,12},{10,14},{12... | collective-permute-start | bytes 196616 | tf_op jit(solution)/shard_map/look_ends/ppermute | solution.py:18
  18.0 17.0 %collective-permute-start.4 = (bf16[384,256]{1,0:T(8,128)(2,1)S(1)}, bf16[384,256]{1,0:T(8,128)(2,1)S(1)}, u32[]{:S(2)}, u32[]{:S(2)}) collective-permute-start(bf16[384,256]{1,0:T(8,128)(2,1)S(1)} %add_convert_fusion.1), channel_id=1, source_target_pairs={{0,4},{2,6},{4,0},{6,2},{1,5},{3,7},{5,1},{7,3},{8,12},{10,14},{12... | collective-permute-start | bytes 589832 | tf_op jit(solution)/shard_map/look_z2/ppermute | solution.py:18
  18.1 13.9 %collective-permute-start.6 = (bf16[64,512]{1,0:T(8,128)(2,1)S(1)}, bf16[64,512]{1,0:T(8,128)(2,1)S(1)}, u32[]{:S(2)}, u32[]{:S(2)}) collective-permute-start(bf16[64,512]{1,0:T(8,128)(2,1)S(1)} %get-tuple-element.99), channel_id=1, source_target_pairs={{0,2},{2,4},{4,6},{6,8},{8,10},{10,12},{12,14},{14,16},{16,18},{18... | collective-permute-start | bytes 196616 | tf_op jit(solution)/shard_map/cot_edge/ppermute | solution.py:35
  21.4 10.7 %collective-permute-start.7 = (bf16[64,512]{1,0:T(8,128)(2,1)S(1)}, bf16[64,512]{1,0:T(8,128)(2,1)S(1)}, u32[]{:S(2)}, u32[]{:S(2)}) collective-permute-start(bf16[64,512]{1,0:T(8,128)(2,1)S(1)} %get-tuple-element.98), channel_id=1, source_target_pairs={{2,0},{4,2},{6,4},{8,6},{10,8},{12,10},{14,12},{16,14},{18,16},{20... | collective-permute-start | bytes 196616 | tf_op jit(solution)/shard_map/cot_edge/ppermute | solution.py:36
  24.3 10.9 %collective-permute-start.3 = (bf16[64,256]{1,0:T(8,128)(2,1)S(1)}, bf16[64,256]{1,0:T(8,128)(2,1)S(1)}, u32[]{:S(2)}, u32[]{:S(2)}) collective-permute-start(bf16[64,256]{1,0:T(8,128)(2,1)S(1)} %get-tuple-element.105.bottom), channel_id=1, source_target_pairs={{0,2},{2,4},{4,6},{6,8},{8,10},{10,12},{12,14},{14,16},{16,18},{18... | collective-permute-start | bytes 98312 | tf_op jit(solution)/shard_map/embed_edge/ppermute | solution.py:35
  27.5 7.6 %copy-start.3 = (bf16[384,256]{1,0:T(8,128)(2,1)S(1)}, bf16[384,256]{1,0:T(8,128)(2,1)}, u32[]{:S(2)}) copy-start(bf16[384,256]{1,0:T(8,128)(2,1)} %get-tuple-element.61) | copy-start | bytes 589828
  27.5 7.7 %copy-start.1 = (bf16[3,3,256,512]{3,2,1,0:T(8,128)(2,1)S(1)}, bf16[3,3,256,512]{3,2,1,0:T(8,128)(2,1)}, u32[]{:S(2)}) copy-start(bf16[3,3,256,512]{3,2,1,0:T(8,128)(2,1)} %kernel.4) | copy-start | bytes 7077892
  27.5 7.7 %copy-start.2 = (s32[10]{0:T(128)S(1)}, s32[10]{0:T(128)}, u32[]{:S(2)}) copy-start(s32[10]{0:T(128)} %stack.34.order.info.refs_0_) | copy-start | bytes 124
  27.5 7.6 %collective-permute-start.5 = (bf16[64,256]{1,0:T(8,128)(2,1)S(1)}, bf16[64,256]{1,0:T(8,128)(2,1)S(1)}, u32[]{:S(2)}, u32[]{:S(2)}) collective-permute-start(bf16[64,256]{1,0:T(8,128)(2,1)S(1)} %get-tuple-element.104.top), channel_id=1, source_target_pairs={{2,0},{4,2},{6,4},{8,6},{10,8},{12,10},{14,12},{16,14},{18,16},{20... | collective-permute-start | bytes 98312 | tf_op jit(solution)/shard_map/embed_edge/ppermute | solution.py:36
  32.1 39.3 %slice-start = ((s8[8388608]{0:T(1024)(128)(4,1)}), s8[4194304]{0:T(1024)(128)(4,1)S(1)}, s32[]{:S(2)}) async-start(s8[8388608]{0:T(1024)(128)(4,1)} %bitcast.16), calls=%async_computation | async-start | bytes 8388608
  35.1 36.2 %slice-start.1 = ((s8[8388608]{0:T(1024)(128)(4,1)}), s8[4194304]{0:T(1024)(128)(4,1)S(1)}, s32[]{:S(2)}) async-start(s8[8388608]{0:T(1024)(128)(4,1)} %bitcast.16), calls=%async_computation.1 | async-start | bytes 8388608
  39.4 5.4 %collective-permute-start.11 = (bf16[576,512]{1,0:T(8,128)(2,1)S(1)}, bf16[576,512]{1,0:T(8,128)(2,1)S(1)}, u32[]{:S(2)}, u32[]{:S(2)}) collective-permute-start(bf16[576,512]{1,0:T(8,128)(2,1)S(1)} %get-tuple-element.83.refs_2_.hidden), channel_id=1, source_target_pairs={{0,8},{8,0},{16,24},{24,16},{1,9},{9,1},{17,25},{25,17},{2,10},{10... | collective-permute-start | bytes 1769480 | tf_op jit(solution)/shard_map/hidden_core/ppermute | solution.py:18
  41.2 3.6 %collective-permute-start.10 = (bf16[512,512]{1,0:T(8,128)(2,1)S(1)}, bf16[512,512]{1,0:T(8,128)(2,1)S(1)}, u32[]{:S(2)}, u32[]{:S(2)}) collective-permute-start(bf16[512,512]{1,0:T(8,128)(2,1)S(1)} %bitcast.24), channel_id=1, source_target_pairs={{0,8},{8,0},{16,24},{24,16},{1,9},{9,1},{17,25},{25,17},{2,10},{10... | collective-permute-start | bytes 1572872 | tf_op jit(solution)/shard_map/cot_core/ppermute | solution.py:18
  41.3 3.5 %collective-permute-start.12 = (bf16[512,512]{1,0:T(8,128)(2,1)S(1)}, bf16[512,512]{1,0:T(8,128)(2,1)S(1)}, u32[]{:S(2)}, u32[]{:S(2)}) collective-permute-start(bf16[512,512]{1,0:T(8,128)(2,1)S(1)} %get-tuple-element.70.refs_4_), channel_id=1, source_target_pairs={{0,8},{8,0},{16,24},{24,16},{1,9},{9,1},{17,25},{25,17},{2,10},{10... | collective-permute-start | bytes 1572872 | tf_op jit(solution)/shard_map/pre_core/ppermute | solution.py:18
  41.8 3.0 %collective-permute-start.13 = (bf16[576,256]{1,0:T(8,128)(2,1)S(1)}, bf16[576,256]{1,0:T(8,128)(2,1)S(1)}, u32[]{:S(2)}, u32[]{:S(2)}) collective-permute-start(bf16[576,256]{1,0:T(8,128)(2,1)S(1)} %get-tuple-element.71.refs_6_), channel_id=1, source_target_pairs={{0,8},{8,0},{16,24},{24,16},{1,9},{9,1},{17,25},{25,17},{2,10},{10... | collective-permute-start | bytes 884744 | tf_op jit(solution)/shard_map/field_core/ppermute | solution.py:18
  50.9 23.1 %collective-permute-start.15 = (bf16[3,3,2,64,384]{4,3,2,1,0:T(8,128)(2,1)S(1)}, bf16[3,3,2,64,384]{4,3,2,1,0:T(8,128)(2,1)S(1)}, u32[]{:S(2)}, u32[]{:S(2)}) collective-permute-start(bf16[3,3,2,64,384]{4,3,2,1,0:T(8,128)(2,1)S(1)} %get-tuple-element.76), channel_id=1, source_target_pairs={{0,1},{1,0},{2,3},{3,2},{4,5},{5,4},{6,7},{7,6},{8,9},{9,8},{10,11... | collective-permute-start | bytes 2654216 | tf_op jit(solution)/shard_map/grads_b1/ppermute | solution.py:18
  52.2 21.8 %collective-permute-start.16 = (bf16[3,3,128,384]{3,2,1,0:T(8,128)(2,1)S(1)}, bf16[3,3,128,384]{3,2,1,0:T(8,128)(2,1)S(1)}, u32[]{:S(2)}, u32[]{:S(2)}) collective-permute-start(bf16[3,3,128,384]{3,2,1,0:T(8,128)(2,1)S(1)} %bitcast.26), channel_id=1, source_target_pairs={{0,16},{8,24},{16,0},{24,8},{1,17},{9,25},{17,1},{25,9},{2,18},{10... | collective-permute-start | bytes 2654216 | tf_op jit(solution)/shard_map/grads_a1/ppermute | solution.py:18
  53.1 15.6 %collective-permute-start.8 = (bf16[512,256]{1,0:T(8,128)(2,1)S(1)}, bf16[512,256]{1,0:T(8,128)(2,1)S(1)}, u32[]{:S(2)}, u32[]{:S(2)}) collective-permute-start(bf16[512,256]{1,0:T(8,128)(2,1)S(1)} %get-tuple-element.67.own), channel_id=1, source_target_pairs={{0,4},{2,6},{4,0},{6,2},{1,5},{3,7},{5,1},{7,3},{8,12},{10,14},{12... | collective-permute-start | bytes 786440 | tf_op jit(solution)/shard_map/ge_z2/ppermute | solution.py:18
  57.7 11.0 %collective-permute-start.9 = (bf16[512,256]{1,0:T(8,128)(2,1)S(1)}, bf16[512,256]{1,0:T(8,128)(2,1)S(1)}, u32[]{:S(2)}, u32[]{:S(2)}) collective-permute-start(bf16[512,256]{1,0:T(8,128)(2,1)S(1)} %get-tuple-element.67.own), channel_id=1, source_target_pairs={{0,2},{2,0},{4,6},{6,4},{1,3},{3,1},{5,7},{7,5},{8,10},{10,8},{12,... | collective-permute-start | bytes 786440 | tf_op jit(solution)/shard_map/ge_z1/ppermute | solution.py:18
  68.7 8.6 %collective-permute-start.14 = (bf16[512,256]{1,0:T(8,128)(2,1)S(1)}, bf16[512,256]{1,0:T(8,128)(2,1)S(1)}, u32[]{:S(2)}, u32[]{:S(2)}) collective-permute-start(bf16[512,256]{1,0:T(8,128)(2,1)S(1)} %collective-permute-done.8.across), channel_id=1, source_target_pairs={{0,2},{2,0},{4,6},{6,4},{1,3},{3,1},{5,7},{7,5},{8,10},{10,8},{12,... | collective-permute-start | bytes 786440 | tf_op jit(solution)/shard_map/ge_z3/ppermute | solution.py:18
  78.8 2.9 %collective-permute-start.17 = (bf16[1024,256]{1,0:T(8,128)(2,1)S(1)}, bf16[1024,256]{1,0:T(8,128)(2,1)S(1)}, u32[]{:S(2)}, u32[]{:S(2)}) collective-permute-start(bf16[1024,256]{1,0:T(8,128)(2,1)S(1)} %get-tuple-element.81), channel_id=1, source_target_pairs={{0,8},{8,0},{16,24},{24,16},{1,9},{9,1},{17,25},{25,17},{2,10},{10... | collective-permute-start | bytes 1572872 | tf_op jit(solution)/shard_map/book_core/ppermute | solution.py:18
  80.2 11.7 %collective-permute-start.18 = (bf16[3,3,64,384]{3,2,1,0:T(8,128)(2,1)S(1)}, bf16[3,3,64,384]{3,2,1,0:T(8,128)(2,1)S(1)}, u32[]{:S(2)}, u32[]{:S(2)}) collective-permute-start(bf16[3,3,64,384]{3,2,1,0:T(8,128)(2,1)S(1)} %get-tuple-element.84), channel_id=1, source_target_pairs={{0,1},{1,0},{2,3},{3,2},{4,5},{5,4},{6,7},{7,6},{8,9},{9,8},{10,11... | collective-permute-start | bytes 1327112 | tf_op jit(solution)/shard_map/grads_a2/ppermute | solution.py:18
  80.4 11.5 %collective-permute-start.19 = (bf16[3,3,64,384]{3,2,1,0:T(8,128)(2,1)S(1)}, bf16[3,3,64,384]{3,2,1,0:T(8,128)(2,1)S(1)}, u32[]{:S(2)}, u32[]{:S(2)}) collective-permute-start(bf16[3,3,64,384]{3,2,1,0:T(8,128)(2,1)S(1)} %bitcast.27), channel_id=1, source_target_pairs={{0,16},{8,24},{16,0},{24,8},{1,17},{9,25},{17,1},{25,9},{2,18},{10... | collective-permute-start | bytes 1327112 | tf_op jit(solution)/shard_map/grads_b2/ppermute | solution.py:18
  81.8 15.6 %collective-permute-start.23 = (bf16[512,256]{1,0:T(8,128)(2,1)S(1)}, bf16[512,256]{1,0:T(8,128)(2,1)S(1)}, u32[]{:S(2)}, u32[]{:S(2)}) collective-permute-start(bf16[512,256]{1,0:T(8,128)(2,1)S(1)} %get-tuple-element.92.refs_0_), channel_id=1, source_target_pairs={{0,16},{8,24},{16,0},{24,8},{1,17},{9,25},{17,1},{25,9},{2,18},{10... | collective-permute-start | bytes 786440 | tf_op jit(solution)/shard_map/book_a/ppermute | solution.py:18
  82.1 15.5 %collective-permute-start.24 = (bf16[512,256]{1,0:T(8,128)(2,1)S(1)}, bf16[512,256]{1,0:T(8,128)(2,1)S(1)}, u32[]{:S(2)}, u32[]{:S(2)}) collective-permute-start(bf16[512,256]{1,0:T(8,128)(2,1)S(1)} %get-tuple-element.93.refs_2_), channel_id=1, source_target_pairs={{0,1},{1,0},{2,3},{3,2},{4,5},{5,4},{6,7},{7,6},{8,9},{9,8},{10,11... | collective-permute-start | bytes 786440 | tf_op jit(solution)/shard_map/book_b/ppermute | solution.py:18
  92.2 13.3 %collective-permute-start.20 = (bf16[3,3,16,768]{3,2,1,0:T(8,128)(2,1)S(1)}, bf16[3,3,16,768]{3,2,1,0:T(8,128)(2,1)S(1)}, u32[]{:S(2)}, u32[]{:S(2)}) collective-permute-start(bf16[3,3,16,768]{3,2,1,0:T(8,128)(2,1)S(1)} %get-tuple-element.88), channel_id=1, source_target_pairs={{0,4},{2,6},{4,0},{6,2},{1,5},{3,7},{5,1},{7,3},{8,12},{10,14},{12... | collective-permute-start | bytes 663560 | tf_op jit(solution)/shard_map/grads_z/ppermute | solution.py:18
  94.1 11.3 %collective-permute-start.21 = (bf16[3,3,16,768]{3,2,1,0:T(8,128)(2,1)S(1)}, bf16[3,3,16,768]{3,2,1,0:T(8,128)(2,1)S(1)}, u32[]{:S(2)}, u32[]{:S(2)}) collective-permute-start(bf16[3,3,16,768]{3,2,1,0:T(8,128)(2,1)S(1)} %get-tuple-element.89), channel_id=1, source_target_pairs={{0,2},{2,0},{4,6},{6,4},{1,3},{3,1},{5,7},{7,5},{8,10},{10,8},{12,... | collective-permute-start | bytes 663560 | tf_op jit(solution)/shard_map/grads_z/ppermute | solution.py:18
  94.1 20.5 %collective-permute-start.22 = (bf16[3,3,16,768]{3,2,1,0:T(8,128)(2,1)S(1)}, bf16[3,3,16,768]{3,2,1,0:T(8,128)(2,1)S(1)}, u32[]{:S(2)}, u32[]{:S(2)}) collective-permute-start(bf16[3,3,16,768]{3,2,1,0:T(8,128)(2,1)S(1)} %get-tuple-element.90), channel_id=1, source_target_pairs={{0,6},{2,4},{4,2},{6,0},{1,7},{3,5},{5,3},{7,1},{8,14},{10,12},{12... | collective-permute-start | bytes 663560 | tf_op jit(solution)/shard_map/grads_z/ppermute | solution.py:18
  97.7 17.1 %collective-permute-start.25 = (bf16[512,256]{1,0:T(8,128)(2,1)S(1)}, bf16[512,256]{1,0:T(8,128)(2,1)S(1)}, u32[]{:S(2)}, u32[]{:S(2)}) collective-permute-start(bf16[512,256]{1,0:T(8,128)(2,1)S(1)} %get-tuple-element.94.refs_0_), channel_id=1, source_target_pairs={{0,1},{1,0},{2,3},{3,2},{4,5},{5,4},{6,7},{7,6},{8,9},{9,8},{10,11... | collective-permute-start | bytes 786440 | tf_op jit(solution)/shard_map/book_a/ppermute | solution.py:18
  98.9 15.9 %collective-permute-start.26 = (bf16[512,256]{1,0:T(8,128)(2,1)S(1)}, bf16[512,256]{1,0:T(8,128)(2,1)S(1)}, u32[]{:S(2)}, u32[]{:S(2)}) collective-permute-start(bf16[512,256]{1,0:T(8,128)(2,1)S(1)} %get-tuple-element.95.refs_2_), channel_id=1, source_target_pairs={{0,16},{8,24},{16,0},{24,8},{1,17},{9,25},{17,1},{25,9},{2,18},{10... | collective-permute-start | bytes 786440 | tf_op jit(solution)/shard_map/book_b/ppermute | solution.py:18
  114.9 2.1 %collective-permute-start.27 = (bf16[1024,256]{1,0:T(8,128)(2,1)S(1)}, bf16[1024,256]{1,0:T(8,128)(2,1)S(1)}, u32[]{:S(2)}, u32[]{:S(2)}) collective-permute-start(bf16[1024,256]{1,0:T(8,128)(2,1)S(1)} %shard_map.96), channel_id=1, source_target_pairs={{0,8},{8,0},{16,24},{24,16},{1,9},{9,1},{17,25},{25,17},{2,10},{10... | collective-permute-start | bytes 1572872 | tf_op jit(solution)/shard_map/book_back/ppermute | solution.py:18

commit v5 on v4

--- a/solution.py
+++ b/solution.py
@@ -323,63 +323,83 @@
     return pair_body, (first, got_first, second, got_second), outs, []
 
 
-def kernel_grad_part(breadth, at, pick, own_up, far_up, own_field, far_field, outs, turned):
-    keep_a, send_a, keep_b, send_b = outs
-    cells = own_up.shape[0]
+def lay_out(breadth, pick, up, turned):
+    half, cells = pick.shape[0], up.shape[0]
+    across = matmul_turned(pick[...], up[...])
+    column = lax.broadcasted_iota(jnp.int32, across.shape, 1) % breadth
+    later = jnp.where(column == breadth - 1, 0.0, pltpu.roll(across, cells - 1, 1))
+    sooner = jnp.where(column == 0, 0.0, pltpu.roll(across, 1, 1))
+    for b, value in enumerate((later, across, sooner)):
+        turned[b * half : (b + 1) * half, :] = value.astype(NARROW)
+
+
+def own_grads_body(breadth, pick, up, pre, hidden, field, out, turned):
+    width, cells = hidden.shape[1], up.shape[0]
+    lay_out(breadth, pick, up, turned.at[0])
+    lay_out(breadth, pick, pre, turned.at[1])
+
+    @pl.loop(0, 3)
+    def _(a):
+        rows = pl.ds(pl.multiple_of(a * breadth, breadth), cells)
+        out[a, :, :width] = matmul(turned[0], hidden[rows, :])
+        out[a, :, width:] = matmul(turned[1], field[rows, :])
+
+
+def far_grads_body(
+    breadth, pick, up, pre, hidden, field, base, keep_a, send_a, keep_b, send_b, turned
+):
+    width, cells = hidden.shape[1], up.shape[0]
     half = pick.shape[0]
-    lanes = own_field.shape[1] // 2
     parts = send_a.shape[0] + 1
     tall = half // parts
     short = tall // 2
-    for source, ref in enumerate((own_up, far_up)):
-        across = matmul_turned(pick[...], ref[...])
-        column = lax.broadcasted_iota(jnp.int32, across.shape, 1) % breadth
-        later = jnp.where(column == breadth - 1, 0.0, pltpu.roll(across, cells - 1, 1))
-        sooner = jnp.where(column == 0, 0.0, pltpu.roll(across, 1, 1))
-        for b, value in enumerate((later, across, sooner)):
-            turned[source, b * half : (b + 1) * half, :] = value.astype(NARROW)
+    lay_out(breadth, pick, up, turned.at[0])
+    lay_out(breadth, pick, pre, turned.at[1])
 
     @pl.loop(0, 3)
     def _(a):
         rows = pl.ds(pl.multiple_of(a * breadth, breadth), cells)
-        total = matmul(turned[0], own_field[rows, :]) + matmul(turned[1], far_field[rows, :])
-        total = total.astype(NARROW)
-        for b in range(3):
-            for k in range(parts):
-                base = b * half + k * tall
-                block = total[base : base + tall]
-                if k == 0:
-                    keep_a[a, b, :, at : at + lanes] = block[:, :lanes]
-                else:
-                    send_a[k - 1, a, b, :, at : at + lanes] = block[:, :lanes]
-                keep_b[a, b, k, :, at : at + lanes] = block[:short, lanes:]
-                send_b[a, b, k, :, at : at + lanes] = block[short:, lanes:]
-
-
-def kernel_grads_body(breadth, pick, *refs):
-    outs, turned = refs[8:12], refs[-1]
-    kernel_grad_part(breadth, 0, pick, *refs[:4], outs, turned)
-    kernel_grad_part(breadth, refs[2].shape[1] // 2, pick, *refs[4:8], outs, turned)
-
-
-def kernel_grads(pick, two, one, breadth, parts):
-    half = pick.shape[0]
-    cells = two[0].shape[0]
+        for which, (array, start) in enumerate(((hidden, 0), (field, width))):
+            inputs = array.shape[1]
+            lanes = inputs // 2
+            at = start // 2
+            total = base[a, :, start : start + inputs] + matmul(turned[which], array[rows, :])
+            total = total.astype(NARROW)
+            for b in range(3):
+                for k in range(parts):
+                    block = total[b * half + k * tall : b * half + (k + 1) * tall]
+                    if k == 0:
+                        keep_a[a, b, :, at : at + lanes] = block[:, :lanes]
+                    else:
+                        send_a[k - 1, a, b, :, at : at + lanes] = block[:, :lanes]
+                    keep_b[a, b, k, :, at : at + lanes] = block[:short, lanes:]
+                    send_b[a, b, k, :, at : at + lanes] = block[short:, lanes:]
+
+
+def kernel_grads(pick, own, far, breadth, parts):
+    half, cells = pick.shape[0], own[0].shape[0]
     tall = half // parts
-    lanes = (two[2].shape[1] + one[2].shape[1]) // 2
+    inputs = own[2].shape[1] + own[3].shape[1]
+    scratch = [pltpu.VMEM((2, 3 * half, cells), NARROW)]
+    (base,) = call(
+        functools.partial(own_grads_body, breadth),
+        (pick, *own),
+        [((3, 3 * half, inputs), WIDE)],
+        18 * half * cells * inputs,
+        scratch,
+    )
     shapes = [
-        (3, 3, tall, lanes),
-        (parts - 1, 3, 3, tall, lanes),
-        (3, 3, parts, tall // 2, lanes),
-        (3, 3, parts, tall // 2, lanes),
+        (3, 3, tall, inputs // 2),
+        (parts - 1, 3, 3, tall, inputs // 2),
+        (3, 3, parts, tall // 2, inputs // 2),
+        (3, 3, parts, tall // 2, inputs // 2),
     ]
     return call(
-        functools.partial(kernel_grads_body, breadth),
-        (pick, *two, *one),
+        functools.partial(far_grads_body, breadth),
+        (pick, *far, base),
         [(shape, NARROW) for shape in shapes],
-        36 * half * (two[2].size + one[2].size),
-        [pltpu.VMEM((2, 3 * half, cells), NARROW)],
-        limit=LARGE,
+        18 * half * cells * inputs,
+        scratch,
     )
 
 
@@ -525,8 +545,8 @@
     far_field = swap(field, "space", 1, "field_core")
     grads = kernel_grads(
         pick,
-        (own_up, far_up, hidden, far_hidden),
-        (own_pre, far_pre, field, far_field),
+        (own_up, own_pre, hidden, field),
+        (far_up, far_pre, far_hidden, far_field),
         breadth,
         parts,
     )

time: 119 us -> 116 us (0.975)
  waiting for transfers between devices: 41.8 us -> 38.6 us
    ppermute x24, waiting for transfers between devices: 41.8 us -> 38.6 us  [swap(): lax.ppermute(value, axis, [(i, i ^ bits) for i in range(lax.axis_size(axi...]
    pallas_call x11 -> x12, Pallas kernels: 21.8 us -> 21.9 us  [call(): pl.pallas_call(body, in_specs=[pl.BlockSpec(memory_space=space) for space...]
  transfers between devices with their start and end apart: 28 -> 28, of which waited for: 10 -> 9; matrix products, arithmetic and copies ran while one was open for 4% -> 4% of each run, Pallas kernels for 14% -> 17%
where the time goes in v5:
time: 116 us
  waiting for transfers between devices  38.6 us (33%)
  starting transfers between devices  36.9 us (32%)
  Pallas kernels  32.7 us (28%)
  other arithmetic  5.94 us (5%)
    ppermute x24, waiting for transfers between devices, swap(): lax.ppermute(value, axis, [(i, i ^ bits) for i in range(lax.axis_size(axi...  38.6 us
    ppermute x24, starting transfers between devices, swap(): lax.ppermute(value, axis, [(i, i ^ bits) for i in range(lax.axis_size(axi...  23.9 us
    pallas_call x12, Pallas kernels, call(): pl.pallas_call(body, in_specs=[pl.BlockSpec(memory_space=space) for space...  21.9 us
    pallas_call x2, Pallas kernels, lookup(): pl.pallas_call(functools.partial(lookup_body, count, edge), grid_spec=plt...  10.8 us
    ppermute x2, starting transfers between devices, edges(): high = lax.ppermute(top, axes, backward)  6.56 us
    ppermute x2, starting transfers between devices, edges(): low = lax.ppermute(bottom, axes, forward)  6.41 us
    convert_element_type x4, other arithmetic, plus(): return sum((term.astype(WIDE) for term in terms)).astype(NARROW)  2.72 us
  transfers between devices with their start and end apart: 28, of which 9 were waited for; matrix products, arithmetic and copies ran while one was open for 4% of the time, Pallas kernels for 17%

profile of v5, /device:TPU:9, one launch (start us, length us, event | category | flops | bytes accessed | tf_op | source)
XLA Modules:
  0.0 115.9 jit_solution(17214248929514757118)
XLA Ops:
  0.6 0.7 stack.34.order.info.refs_0_
  1.3 3.7 %shard_map.84 = bf16[512,256]{1,0:T(8,128)(2,1)} custom-call(s32[10]{0:T(128)} %stack.34.order.info.refs_0_, bf16[2048,2048]{1,0:T(8,128)(2,1)} %bitcast.14, bf16[2048,256]{1,0:T(8,128)(2,1)} %codebook.2), custom_call_target="tpu_custom_call" | custom-call | flops 67108864 | bytes 1 | tf_op jit(solution)/shard_map/pallas_call | solution.py:131
  5.1 0.0 copy-start
  5.1 0.0 slice-start.3
  5.1 7.1 %shard_map.85 = (bf16[512,256]{1,0:T(8,128)(2,1)}, bf16[128,256]{1,0:T(8,128)(2,1)}, bf16[384,256]{1,0:T(8,128)(2,1)}, bf16[128,256]{1,0:T(8,128)(2,1)}, bf16[384,256]{1,0:T(8,128)(2,1)}) custom-call(s32[10]{0:T(128)} %stack.34.order.info.refs_0_, bf16[2048,2048]{1,0:T(8,128)(2,1)} %bitcast.15, bf16[2048,256]{1,0:T(8,128)(2,1)} %codebook.2), custom_call_target="tpu_custom_call" | custom-call | flops 201326592 | bytes 1 | tf_op jit(solution)/shard_map/pallas_call | solution.py:131
  12.1 0.1 fusion.pick
  12.3 1.5 %collective-permute-start = (bf16[512,256]{1,0:T(8,128)(2,1)}, bf16[512,256]{1,0:T(8,128)(2,1)S(1)}, u32[]{:S(2)}, u32[]{:S(2)}) collective-permute-start(bf16[512,256]{1,0:T(8,128)(2,1)} %get-tuple-element.58), channel_id=1, source_target_pairs={{0,2},{2,0},{4,6},{6,4},{1,3},{3,1},{5,7},{7,5},{8,10},{10,8},{12,... | collective-permute-start | bytes 786440 | tf_op jit(solution)/shard_map/look_near/ppermute | solution.py:18
  13.8 0.0 collective-permute-done.1
  13.8 0.9 add_convert_fusion.2
  14.7 2.4 %collective-permute-start.2 = (bf16[128,256]{1,0:T(8,128)(2,1)S(1)}, bf16[128,256]{1,0:T(8,128)(2,1)S(1)}, u32[]{:S(2)}, u32[]{:S(2)}) collective-permute-start(bf16[128,256]{1,0:T(8,128)(2,1)S(1)} %add_convert_fusion.2), channel_id=1, source_target_pairs={{0,4},{2,6},{4,0},{6,2},{1,5},{3,7},{5,1},{7,3},{8,12},{10,14},{12... | collective-permute-start | bytes 196616 | tf_op jit(solution)/shard_map/look_ends/ppermute | solution.py:18
  17.0 1.0 add_convert_fusion.1
  18.0 0.1 collective-permute-start.4
  18.1 3.2 %collective-permute-start.6 = (bf16[64,512]{1,0:T(8,128)(2,1)S(1)}, bf16[64,512]{1,0:T(8,128)(2,1)S(1)}, u32[]{:S(2)}, u32[]{:S(2)}) collective-permute-start(bf16[64,512]{1,0:T(8,128)(2,1)S(1)} %get-tuple-element.99), channel_id=1, source_target_pairs={{0,2},{2,4},{4,6},{6,8},{8,10},{10,12},{12,14},{14,16},{16,18},{18... | collective-permute-start | bytes 196616 | tf_op jit(solution)/shard_map/cot_edge/ppermute | solution.py:35
  21.4 2.1 %collective-permute-start.7 = (bf16[64,512]{1,0:T(8,128)(2,1)S(1)}, bf16[64,512]{1,0:T(8,128)(2,1)S(1)}, u32[]{:S(2)}, u32[]{:S(2)}) collective-permute-start(bf16[64,512]{1,0:T(8,128)(2,1)S(1)} %get-tuple-element.98), channel_id=1, source_target_pairs={{2,0},{4,2},{6,4},{8,6},{10,8},{12,10},{14,12},{16,14},{18,16},{20... | collective-permute-start | bytes 196616 | tf_op jit(solution)/shard_map/cot_edge/ppermute | solution.py:36
  23.5 0.8 add_convert_fusion.3
  24.3 3.2 %collective-permute-start.3 = (bf16[64,256]{1,0:T(8,128)(2,1)S(1)}, bf16[64,256]{1,0:T(8,128)(2,1)S(1)}, u32[]{:S(2)}, u32[]{:S(2)}) collective-permute-start(bf16[64,256]{1,0:T(8,128)(2,1)S(1)} %get-tuple-element.105.bottom), channel_id=1, source_target_pairs={{0,2},{2,4},{4,6},{6,8},{8,10},{10,12},{12,14},{14,16},{16,18},{18... | collective-permute-start | bytes 98312 | tf_op jit(solution)/shard_map/embed_edge/ppermute | solution.py:35
  27.5 0.0 copy-start.1
  27.5 4.5 %collective-permute-start.5 = (bf16[64,256]{1,0:T(8,128)(2,1)S(1)}, bf16[64,256]{1,0:T(8,128)(2,1)S(1)}, u32[]{:S(2)}, u32[]{:S(2)}) collective-permute-start(bf16[64,256]{1,0:T(8,128)(2,1)S(1)} %get-tuple-element.104.top), channel_id=1, source_target_pairs={{2,0},{4,2},{6,4},{8,6},{10,8},{12,10},{14,12},{16,14},{18,16},{20... | collective-permute-start | bytes 98312 | tf_op jit(solution)/shard_map/embed_edge/ppermute | solution.py:36
  32.1 3.0 %shard_map.86.grad_hidden = f32[576,512]{1,0:T(8,128)S(1)} custom-call(bf16[512,512]{1,0:T(8,128)(2,1)S(1)} %bitcast.23, bf16[64,512]{1,0:T(8,128)(2,1)S(1)} %collective-permute-done.6.low, bf16[64,512]{1,0:T(8,128)(2,1)S(1)} %collective-permute-done.7.high, bf16[3,3,512,512]{3,2,1,0:T(8,128)(2,1)S(1)} %bitcast.21), custom_call_target="tpu_custom_call" | custom-call | flops 301989888 | bytes 1 | tf_op jit(solution)/shard_map/pallas_call | solution.py:59
  35.0 0.1 add_convert_fusion.inner
  35.2 4.2 %shard_map.87 = (bf16[576,512]{1,0:T(8,128)(2,1)S(1)}, bf16[512,512]{1,0:T(8,128)(2,1)S(1)}, bf16[576,256]{1,0:T(8,128)(2,1)S(1)}, bf16[512,256]{1,0:T(8,128)(2,1)S(1)}) custom-call(s32[10]{0:T(128)S(1)} %copy-done.2, bf16[64,256]{1,0:T(8,128)(2,1)S(1)} %collective-permute-done.3.low, bf16[64,256]{1,0:T(8,128)(2,1)S(1)} %get-tuple-element.104.top, ...), custom_call_target="tpu_custom_call" | custom-call | flops 301989888 | bytes 1 | tf_op jit(solution)/shard_map/pallas_call | solution.py:59
  39.4 1.9 %collective-permute-start.12 = (bf16[576,512]{1,0:T(8,128)(2,1)S(1)}, bf16[576,512]{1,0:T(8,128)(2,1)S(1)}, u32[]{:S(2)}, u32[]{:S(2)}) collective-permute-start(bf16[576,512]{1,0:T(8,128)(2,1)S(1)} %get-tuple-element.83.hidden), channel_id=1, source_target_pairs={{0,8},{8,0},{16,24},{24,16},{1,9},{9,1},{17,25},{25,17},{2,10},{10... | collective-permute-start | bytes 1769480 | tf_op jit(solution)/shard_map/hidden_core/ppermute | solution.py:18
  41.2 0.1 collective-permute-start.10
  41.3 0.4 collective-permute-start.11
  41.8 0.1 collective-permute-start.13
  41.8 3.1 %shard_map.88.base = f32[3,768,768]{2,1,0:T(8,128)S(1)} custom-call(bf16[256,512]{1,0:T(8,128)(2,1)S(1)} %fusion.pick, bf16[512,512]{1,0:T(8,128)(2,1)S(1)} %bitcast.25, bf16[512,512]{1,0:T(8,128)(2,1)S(1)} %get-tuple-element.70.pre, bf16[576,512]{1,0:T(8,128)(2,1)S(1)} %get-tuple-element.83.hidden, bf16[576,256]{1,0:T(8,128)(2,1)S(1)} %get-tuple-element.71.field), custom_call_target="tpu_custom_call" | custom-call | flops 226492416 | bytes 1 | tf_op jit(solution)/shard_map/pallas_call | solution.py:59
  45.0 0.0 slice-start.1
  45.0 3.1 %shard_map.89 = (bf16[3,3,128,384]{3,2,1,0:T(8,128)(2,1)S(1)}, bf16[1,3,3,128,384]{4,3,2,1,0:T(8,128)(2,1)S(1)}, bf16[3,3,2,64,384]{4,3,2,1,0:T(8,128)(2,1)S(1)}, bf16[3,3,2,64,384]{4,3,2,1,0:T(8,128)(2,1)S(1)}) custom-call(bf16[256,512]{1,0:T(8,128)(2,1)S(1)} %fusion.pick, bf16[512,512]{1,0:T(8,128)(2,1)S(1)} %collective-permute-done.10.up, ...), custom_call_target="tpu_custom_call" | custom-call | flops 226492416 | bytes 1 | tf_op jit(solution)/shard_map/pallas_call | solution.py:59
  48.1 1.3 %collective-permute-start.15 = (bf16[3,3,2,64,384]{4,3,2,1,0:T(8,128)(2,1)S(1)}, bf16[3,3,2,64,384]{4,3,2,1,0:T(8,128)(2,1)S(1)}, u32[]{:S(2)}, u32[]{:S(2)}) collective-permute-start(bf16[3,3,2,64,384]{4,3,2,1,0:T(8,128)(2,1)S(1)} %get-tuple-element.76), channel_id=1, source_target_pairs={{0,1},{1,0},{2,3},{3,2},{4,5},{5,4},{6,7},{7,6},{8,9},{9,8},{10,11... | collective-permute-start | bytes 2654216 | tf_op jit(solution)/shard_map/grads_b1/ppermute | solution.py:18
  49.4 0.9 collective-permute-start.16
  50.3 4.7 %collective-permute-start.8 = (bf16[512,256]{1,0:T(8,128)(2,1)S(1)}, bf16[512,256]{1,0:T(8,128)(2,1)S(1)}, u32[]{:S(2)}, u32[]{:S(2)}) collective-permute-start(bf16[512,256]{1,0:T(8,128)(2,1)S(1)} %get-tuple-element.67.own), channel_id=1, source_target_pairs={{0,4},{2,6},{4,0},{6,2},{1,5},{3,7},{5,1},{7,3},{8,12},{10,14},{12... | collective-permute-start | bytes 786440 | tf_op jit(solution)/shard_map/ge_z2/ppermute | solution.py:18
  55.0 10.9 %collective-permute-done.8.across = bf16[512,256]{1,0:T(8,128)(2,1)S(1)} collective-permute-done((bf16[512,256]{1,0:T(8,128)(2,1)S(1)}, bf16[512,256]{1,0:T(8,128)(2,1)S(1)}, u32[]{:S(2)}, u32[]{:S(2)}) %collective-permute-start.8) | collective-permute-done | bytes 262176 | tf_op jit(solution)/shard_map/ge_z2/ppermute | solution.py:18
  65.9 2.7 %collective-permute-start.14 = (bf16[512,256]{1,0:T(8,128)(2,1)S(1)}, bf16[512,256]{1,0:T(8,128)(2,1)S(1)}, u32[]{:S(2)}, u32[]{:S(2)}) collective-permute-start(bf16[512,256]{1,0:T(8,128)(2,1)S(1)} %collective-permute-done.8.across), channel_id=1, source_target_pairs={{0,2},{2,0},{4,6},{6,4},{1,3},{3,1},{5,7},{7,5},{8,10},{10,8},{12,... | collective-permute-start | bytes 786440 | tf_op jit(solution)/shard_map/ge_z3/ppermute | solution.py:18
  68.7 2.6 %shard_map.90.refs_3_ = f32[2048,256]{1,0:T(8,128)S(1)} custom-call(s32[10]{0:T(128)S(1)} %copy-done.2, bf16[2048,2048]{1,0:T(8,128)(2,1)S(1)} %bitcast.18, bf16[512,256]{1,0:T(8,128)(2,1)S(1)} %get-tuple-element.67.own, bf16[512,256]{1,0:T(8,128)(2,1)S(1)} %collective-permute-done.9.beside, bf16[512,256]{1,0:T(8,128)(2,1)S(1)} %collective-permute-done.8.across), custom_call_target="tpu_custom_call" | custom-call | flops 201326592 | bytes 1 | tf_op jit(solution)/shard_map/pallas_call | solution.py:59
  71.3 0.4 shard_map.91
  71.7 2.9 %collective-permute-done.14.refs_2_ = bf16[512,256]{1,0:T(8,128)(2,1)S(1)} collective-permute-done((bf16[512,256]{1,0:T(8,128)(2,1)S(1)}, bf16[512,256]{1,0:T(8,128)(2,1)S(1)}, u32[]{:S(2)}, u32[]{:S(2)}) %collective-permute-start.14) | collective-permute-done | bytes 262176 | tf_op jit(solution)/shard_map/ge_z3/ppermute | solution.py:18
  74.6 1.5 %shard_map.92 = (bf16[1024,256]{1,0:T(8,128)(2,1)S(1)}, bf16[1024,256]{1,0:T(8,128)(2,1)S(1)}) custom-call(s32[10]{0:T(128)S(1)} %copy-done.2, bf16[2048,2048]{1,0:T(8,128)(2,1)S(1)} %bitcast.19, bf16[512,256]{1,0:T(8,128)(2,1)S(1)} %collective-permute-done.14.refs_2_, f32[2048,256]{1,0:T(8,128)S(1)} %shard_map.90.refs_3_), custom_call_target="tpu_custom_call" | custom-call | flops 100000000 | bytes 1 | tf_op jit(solution)/shard_map/pallas_call | solution.py:59
  76.1 1.4 %collective-permute-start.17 = (bf16[1024,256]{1,0:T(8,128)(2,1)S(1)}, bf16[1024,256]{1,0:T(8,128)(2,1)S(1)}, u32[]{:S(2)}, u32[]{:S(2)}) collective-permute-start(bf16[1024,256]{1,0:T(8,128)(2,1)S(1)} %get-tuple-element.81), channel_id=1, source_target_pairs={{0,8},{8,0},{16,24},{24,16},{1,9},{9,1},{17,25},{25,17},{2,10},{10... | collective-permute-start | bytes 1572872 | tf_op jit(solution)/shard_map/book_core/ppermute | solution.py:18
  77.5 0.2 collective-permute-start.18
  77.7 1.3 %collective-permute-done.17.refs_1_ = bf16[1024,256]{1,0:T(8,128)(2,1)S(1)} collective-permute-done((bf16[1024,256]{1,0:T(8,128)(2,1)S(1)}, bf16[1024,256]{1,0:T(8,128)(2,1)S(1)}, u32[]{:S(2)}, u32[]{:S(2)}) %collective-permute-start.17) | collective-permute-done | bytes 524320 | tf_op jit(solution)/shard_map/book_core/ppermute | solution.py:18
  79.0 0.1 shard_map.93
  79.2 0.2 collective-permute-start.23
  79.4 1.2 %collective-permute-start.24 = (bf16[512,256]{1,0:T(8,128)(2,1)S(1)}, bf16[512,256]{1,0:T(8,128)(2,1)S(1)}, u32[]{:S(2)}, u32[]{:S(2)}) collective-permute-start(bf16[512,256]{1,0:T(8,128)(2,1)S(1)} %get-tuple-element.93.refs_2_), channel_id=1, source_target_pairs={{0,1},{1,0},{2,3},{3,2},{4,5},{5,4},{6,7},{7,6},{8,9},{9,8},{10,11... | collective-permute-start | bytes 786440 | tf_op jit(solution)/shard_map/book_b/ppermute | solution.py:18
  80.6 3.4 %shard_map.94 = bf16[512,512]{1,0:T(8,128)(2,1)} custom-call(bf16[576,512]{1,0:T(8,128)(2,1)S(1)} %get-tuple-element.83.hidden, bf16[3,3,512,512]{3,2,1,0:T(8,128)(2,1)S(1)} %bitcast.21), custom_call_target="tpu_custom_call" | custom-call | flops 301989888 | bytes 1 | tf_op jit(solution)/shard_map/pallas_call | solution.py:59
  84.0 5.2 %collective-permute-done.18.refs_1_ = bf16[3,3,64,384]{3,2,1,0:T(8,128)(2,1)S(1)} collective-permute-done((bf16[3,3,64,384]{3,2,1,0:T(8,128)(2,1)S(1)}, bf16[3,3,64,384]{3,2,1,0:T(8,128)(2,1)S(1)}, u32[]{:S(2)}, u32[]{:S(2)}) %collective-permute-start.18) | collective-permute-done | bytes 442400 | tf_op jit(solution)/shard_map/grads_a2/ppermute | solution.py:18
  89.2 0.2 shard_map.95
  89.5 1.9 %collective-permute-start.20 = (bf16[3,3,16,768]{3,2,1,0:T(8,128)(2,1)S(1)}, bf16[3,3,16,768]{3,2,1,0:T(8,128)(2,1)S(1)}, u32[]{:S(2)}, u32[]{:S(2)}) collective-permute-start(bf16[3,3,16,768]{3,2,1,0:T(8,128)(2,1)S(1)} %get-tuple-element.88), channel_id=1, source_target_pairs={{0,4},{2,6},{4,0},{6,2},{1,5},{3,7},{5,1},{7,3},{8,12},{10,14},{12... | collective-permute-start | bytes 663560 | tf_op jit(solution)/shard_map/grads_z/ppermute | solution.py:18
  91.4 0.0 collective-permute-start.21
  91.4 0.8 collective-permute-start.22
  92.2 2.6 %collective-permute-done.23.refs_1_ = bf16[512,256]{1,0:T(8,128)(2,1)S(1)} collective-permute-done((bf16[512,256]{1,0:T(8,128)(2,1)S(1)}, bf16[512,256]{1,0:T(8,128)(2,1)S(1)}, u32[]{:S(2)}, u32[]{:S(2)}) %collective-permute-start.23) | collective-permute-done | bytes 262176 | tf_op jit(solution)/shard_map/book_a/ppermute | solution.py:18
  94.8 0.1 collective-permute-done.24.refs_3_
  94.9 0.1 shard_map.96
  95.0 1.2 %collective-permute-start.25 = (bf16[512,256]{1,0:T(8,128)(2,1)S(1)}, bf16[512,256]{1,0:T(8,128)(2,1)S(1)}, u32[]{:S(2)}, u32[]{:S(2)}) collective-permute-start(bf16[512,256]{1,0:T(8,128)(2,1)S(1)} %get-tuple-element.94.refs_0_), channel_id=1, source_target_pairs={{0,1},{1,0},{2,3},{3,2},{4,5},{5,4},{6,7},{7,6},{8,9},{9,8},{10,11... | collective-permute-start | bytes 786440 | tf_op jit(solution)/shard_map/book_a/ppermute | solution.py:18
  96.2 0.2 collective-permute-start.26
  96.4 6.2 %collective-permute-done.20 = bf16[3,3,16,768]{3,2,1,0:T(8,128)(2,1)S(1)} collective-permute-done((bf16[3,3,16,768]{3,2,1,0:T(8,128)(2,1)S(1)}, bf16[3,3,16,768]{3,2,1,0:T(8,128)(2,1)S(1)}, u32[]{:S(2)}, u32[]{:S(2)}) %collective-permute-start.20) | collective-permute-done | bytes 221216 | tf_op jit(solution)/shard_map/grads_z/ppermute | solution.py:18
  102.7 9.3 %collective-permute-done.22 = bf16[3,3,16,768]{3,2,1,0:T(8,128)(2,1)S(1)} collective-permute-done((bf16[3,3,16,768]{3,2,1,0:T(8,128)(2,1)S(1)}, bf16[3,3,16,768]{3,2,1,0:T(8,128)(2,1)S(1)}, u32[]{:S(2)}, u32[]{:S(2)}) %collective-permute-start.22) | collective-permute-done | bytes 221216 | tf_op jit(solution)/shard_map/grads_z/ppermute | solution.py:18
  112.0 0.1 add_bitcast_fusion
  112.1 0.1 shard_map.97
  112.3 0.6 collective-permute-start.27
  112.9 0.7 pad_maximum_fusion.1
  113.6 0.7 pad_maximum_fusion
  114.3 0.1 collective-permute-done.27
  114.4 0.1 broadcast_select_fusion.1
  114.5 1.5 %maximum_convert_fusion = f32[2048,256]{1,0:T(8,128)} fusion(bf16[1024,256]{1,0:T(8,128)(2,1)S(1)} %get-tuple-element.97, bf16[1024,256]{1,0:T(8,128)(2,1)S(1)} %get-tuple-element.96), kind=kLoop, calls=%fused_computation | loop fusion | flops 2097152 | bytes 3145728 | tf_op jit(solution)/shard_map/convert_element_type | solution.py:585
  (39 shorter events, 0.1 us)
Async XLA Ops:
  5.0 8.7 %collective-permute-start.1 = (bf16[512,256]{1,0:T(8,128)(2,1)}, bf16[512,256]{1,0:T(8,128)(2,1)S(1)}, u32[]{:S(2)}, u32[]{:S(2)}) collective-permute-start(bf16[512,256]{1,0:T(8,128)(2,1)} %shard_map.84), channel_id=1, source_target_pairs={{0,2},{2,0},{4,6},{6,4},{1,3},{3,1},{5,7},{7,5},{8,10},{10,8},{12,... | collective-permute-start | bytes 786440 | tf_op jit(solution)/shard_map/look_z1/ppermute | solution.py:18
  5.1 27.0 %slice-start.2 = ((s8[4718592]{0:T(1024)(128)(4,1)}), s8[4194304]{0:T(1024)(128)(4,1)S(1)}, s32[]{:S(2)}) async-start(s8[4718592]{0:T(1024)(128)(4,1)} %bitcast.20), calls=%async_computation.2 | async-start | bytes 8388608
  5.1 13.1 %copy-start = (bf16[1,16,32,512]{3,2,1,0:T(8,128)(2,1)S(1)}, bf16[1,16,32,512]{3,2,1,0:T(8,128)(2,1)}, u32[]{:S(2)}) copy-start(bf16[1,16,32,512]{3,2,1,0:T(8,128)(2,1)} %param.9) | copy-start | bytes 1572868
  5.1 27.0 %slice-start.3 = ((s8[4718592]{0:T(1024)(128)(4,1)}), s8[524288]{0:T(1024)(128)(4,1)S(1)}, s32[]{:S(2)}) async-start(s8[4718592]{0:T(1024)(128)(4,1)} %bitcast.20), calls=%async_computation.3 | async-start | bytes 1048576
  12.3 11.2 %collective-permute-start = (bf16[512,256]{1,0:T(8,128)(2,1)}, bf16[512,256]{1,0:T(8,128)(2,1)S(1)}, u32[]{:S(2)}, u32[]{:S(2)}) collective-permute-start(bf16[512,256]{1,0:T(8,128)(2,1)} %get-tuple-element.58), channel_id=1, source_target_pairs={{0,2},{2,0},{4,6},{6,4},{1,3},{3,1},{5,7},{7,5},{8,10},{10,8},{12,... | collective-permute-start | bytes 786440 | tf_op jit(solution)/shard_map/look_near/ppermute | solution.py:18
  14.7 8.8 %collective-permute-start.2 = (bf16[128,256]{1,0:T(8,128)(2,1)S(1)}, bf16[128,256]{1,0:T(8,128)(2,1)S(1)}, u32[]{:S(2)}, u32[]{:S(2)}) collective-permute-start(bf16[128,256]{1,0:T(8,128)(2,1)S(1)} %add_convert_fusion.2), channel_id=1, source_target_pairs={{0,4},{2,6},{4,0},{6,2},{1,5},{3,7},{5,1},{7,3},{8,12},{10,14},{12... | collective-permute-start | bytes 196616 | tf_op jit(solution)/shard_map/look_ends/ppermute | solution.py:18
  18.0 17.0 %collective-permute-start.4 = (bf16[384,256]{1,0:T(8,128)(2,1)S(1)}, bf16[384,256]{1,0:T(8,128)(2,1)S(1)}, u32[]{:S(2)}, u32[]{:S(2)}) collective-permute-start(bf16[384,256]{1,0:T(8,128)(2,1)S(1)} %add_convert_fusion.1), channel_id=1, source_target_pairs={{0,4},{2,6},{4,0},{6,2},{1,5},{3,7},{5,1},{7,3},{8,12},{10,14},{12... | collective-permute-start | bytes 589832 | tf_op jit(solution)/shard_map/look_z2/ppermute | solution.py:18
  18.1 13.9 %collective-permute-start.6 = (bf16[64,512]{1,0:T(8,128)(2,1)S(1)}, bf16[64,512]{1,0:T(8,128)(2,1)S(1)}, u32[]{:S(2)}, u32[]{:S(2)}) collective-permute-start(bf16[64,512]{1,0:T(8,128)(2,1)S(1)} %get-tuple-element.99), channel_id=1, source_target_pairs={{0,2},{2,4},{4,6},{6,8},{8,10},{10,12},{12,14},{14,16},{16,18},{18... | collective-permute-start | bytes 196616 | tf_op jit(solution)/shard_map/cot_edge/ppermute | solution.py:35
  21.4 10.7 %collective-permute-start.7 = (bf16[64,512]{1,0:T(8,128)(2,1)S(1)}, bf16[64,512]{1,0:T(8,128)(2,1)S(1)}, u32[]{:S(2)}, u32[]{:S(2)}) collective-permute-start(bf16[64,512]{1,0:T(8,128)(2,1)S(1)} %get-tuple-element.98), channel_id=1, source_target_pairs={{2,0},{4,2},{6,4},{8,6},{10,8},{12,10},{14,12},{16,14},{18,16},{20... | collective-permute-start | bytes 196616 | tf_op jit(solution)/shard_map/cot_edge/ppermute | solution.py:36
  24.3 10.9 %collective-permute-start.3 = (bf16[64,256]{1,0:T(8,128)(2,1)S(1)}, bf16[64,256]{1,0:T(8,128)(2,1)S(1)}, u32[]{:S(2)}, u32[]{:S(2)}) collective-permute-start(bf16[64,256]{1,0:T(8,128)(2,1)S(1)} %get-tuple-element.105.bottom), channel_id=1, source_target_pairs={{0,2},{2,4},{4,6},{6,8},{8,10},{10,12},{12,14},{14,16},{16,18},{18... | collective-permute-start | bytes 98312 | tf_op jit(solution)/shard_map/embed_edge/ppermute | solution.py:35
  27.5 7.6 %copy-start.3 = (bf16[384,256]{1,0:T(8,128)(2,1)S(1)}, bf16[384,256]{1,0:T(8,128)(2,1)}, u32[]{:S(2)}) copy-start(bf16[384,256]{1,0:T(8,128)(2,1)} %get-tuple-element.61) | copy-start | bytes 589828
  27.5 7.7 %copy-start.1 = (bf16[3,3,256,512]{3,2,1,0:T(8,128)(2,1)S(1)}, bf16[3,3,256,512]{3,2,1,0:T(8,128)(2,1)}, u32[]{:S(2)}) copy-start(bf16[3,3,256,512]{3,2,1,0:T(8,128)(2,1)} %kernel.4) | copy-start | bytes 7077892
  27.5 7.7 %copy-start.2 = (s32[10]{0:T(128)S(1)}, s32[10]{0:T(128)}, u32[]{:S(2)}) copy-start(s32[10]{0:T(128)} %stack.34.order.info.refs_0_) | copy-start | bytes 124
  27.5 7.6 %collective-permute-start.5 = (bf16[64,256]{1,0:T(8,128)(2,1)S(1)}, bf16[64,256]{1,0:T(8,128)(2,1)S(1)}, u32[]{:S(2)}, u32[]{:S(2)}) collective-permute-start(bf16[64,256]{1,0:T(8,128)(2,1)S(1)} %get-tuple-element.104.top), channel_id=1, source_target_pairs={{2,0},{4,2},{6,4},{8,6},{10,8},{12,10},{14,12},{16,14},{18,16},{20... | collective-permute-start | bytes 98312 | tf_op jit(solution)/shard_map/embed_edge/ppermute | solution.py:36
  39.4 5.6 %collective-permute-start.12 = (bf16[576,512]{1,0:T(8,128)(2,1)S(1)}, bf16[576,512]{1,0:T(8,128)(2,1)S(1)}, u32[]{:S(2)}, u32[]{:S(2)}) collective-permute-start(bf16[576,512]{1,0:T(8,128)(2,1)S(1)} %get-tuple-element.83.hidden), channel_id=1, source_target_pairs={{0,8},{8,0},{16,24},{24,16},{1,9},{9,1},{17,25},{25,17},{2,10},{10... | collective-permute-start | bytes 1769480 | tf_op jit(solution)/shard_map/hidden_core/ppermute | solution.py:18
  41.2 3.8 %collective-permute-start.10 = (bf16[512,512]{1,0:T(8,128)(2,1)S(1)}, bf16[512,512]{1,0:T(8,128)(2,1)S(1)}, u32[]{:S(2)}, u32[]{:S(2)}) collective-permute-start(bf16[512,512]{1,0:T(8,128)(2,1)S(1)} %bitcast.24), channel_id=1, source_target_pairs={{0,8},{8,0},{16,24},{24,16},{1,9},{9,1},{17,25},{25,17},{2,10},{10... | collective-permute-start | bytes 1572872 | tf_op jit(solution)/shard_map/cot_core/ppermute | solution.py:18
  41.3 3.7 %collective-permute-start.11 = (bf16[512,512]{1,0:T(8,128)(2,1)S(1)}, bf16[512,512]{1,0:T(8,128)(2,1)S(1)}, u32[]{:S(2)}, u32[]{:S(2)}) collective-permute-start(bf16[512,512]{1,0:T(8,128)(2,1)S(1)} %get-tuple-element.70.pre), channel_id=1, source_target_pairs={{0,8},{8,0},{16,24},{24,16},{1,9},{9,1},{17,25},{25,17},{2,10},{10... | collective-permute-start | bytes 1572872 | tf_op jit(solution)/shard_map/pre_core/ppermute | solution.py:18
  41.8 3.2 %collective-permute-start.13 = (bf16[576,256]{1,0:T(8,128)(2,1)S(1)}, bf16[576,256]{1,0:T(8,128)(2,1)S(1)}, u32[]{:S(2)}, u32[]{:S(2)}) collective-permute-start(bf16[576,256]{1,0:T(8,128)(2,1)S(1)} %get-tuple-element.71.field), channel_id=1, source_target_pairs={{0,8},{8,0},{16,24},{24,16},{1,9},{9,1},{17,25},{25,17},{2,10},{10... | collective-permute-start | bytes 884744 | tf_op jit(solution)/shard_map/field_core/ppermute | solution.py:18
  41.8 26.8 %slice-start = ((s8[8388608]{0:T(1024)(128)(4,1)}), s8[4194304]{0:T(1024)(128)(4,1)S(1)}, s32[]{:S(2)}) async-start(s8[8388608]{0:T(1024)(128)(4,1)} %bitcast.16), calls=%async_computation | async-start | bytes 8388608
  45.0 23.7 %slice-start.1 = ((s8[8388608]{0:T(1024)(128)(4,1)}), s8[4194304]{0:T(1024)(128)(4,1)S(1)}, s32[]{:S(2)}) async-start(s8[8388608]{0:T(1024)(128)(4,1)} %bitcast.16), calls=%async_computation.1 | async-start | bytes 8388608
  48.1 23.1 %collective-permute-start.15 = (bf16[3,3,2,64,384]{4,3,2,1,0:T(8,128)(2,1)S(1)}, bf16[3,3,2,64,384]{4,3,2,1,0:T(8,128)(2,1)S(1)}, u32[]{:S(2)}, u32[]{:S(2)}) collective-permute-start(bf16[3,3,2,64,384]{4,3,2,1,0:T(8,128)(2,1)S(1)} %get-tuple-element.76), channel_id=1, source_target_pairs={{0,1},{1,0},{2,3},{3,2},{4,5},{5,4},{6,7},{7,6},{8,9},{9,8},{10,11... | collective-permute-start | bytes 2654216 | tf_op jit(solution)/shard_map/grads_b1/ppermute | solution.py:18
  49.4 21.9 %collective-permute-start.16 = (bf16[3,3,128,384]{3,2,1,0:T(8,128)(2,1)S(1)}, bf16[3,3,128,384]{3,2,1,0:T(8,128)(2,1)S(1)}, u32[]{:S(2)}, u32[]{:S(2)}) collective-permute-start(bf16[3,3,128,384]{3,2,1,0:T(8,128)(2,1)S(1)} %bitcast.26), channel_id=1, source_target_pairs={{0,16},{8,24},{16,0},{24,8},{1,17},{9,25},{17,1},{25,9},{2,18},{10... | collective-permute-start | bytes 2654216 | tf_op jit(solution)/shard_map/grads_a1/ppermute | solution.py:18
  50.3 15.6 %collective-permute-start.8 = (bf16[512,256]{1,0:T(8,128)(2,1)S(1)}, bf16[512,256]{1,0:T(8,128)(2,1)S(1)}, u32[]{:S(2)}, u32[]{:S(2)}) collective-permute-start(bf16[512,256]{1,0:T(8,128)(2,1)S(1)} %get-tuple-element.67.own), channel_id=1, source_target_pairs={{0,4},{2,6},{4,0},{6,2},{1,5},{3,7},{5,1},{7,3},{8,12},{10,14},{12... | collective-permute-start | bytes 786440 | tf_op jit(solution)/shard_map/ge_z2/ppermute | solution.py:18
  55.0 10.9 %collective-permute-start.9 = (bf16[512,256]{1,0:T(8,128)(2,1)S(1)}, bf16[512,256]{1,0:T(8,128)(2,1)S(1)}, u32[]{:S(2)}, u32[]{:S(2)}) collective-permute-start(bf16[512,256]{1,0:T(8,128)(2,1)S(1)} %get-tuple-element.67.own), channel_id=1, source_target_pairs={{0,2},{2,0},{4,6},{6,4},{1,3},{3,1},{5,7},{7,5},{8,10},{10,8},{12,... | collective-permute-start | bytes 786440 | tf_op jit(solution)/shard_map/ge_z1/ppermute | solution.py:18
  65.9 8.7 %collective-permute-start.14 = (bf16[512,256]{1,0:T(8,128)(2,1)S(1)}, bf16[512,256]{1,0:T(8,128)(2,1)S(1)}, u32[]{:S(2)}, u32[]{:S(2)}) collective-permute-start(bf16[512,256]{1,0:T(8,128)(2,1)S(1)} %collective-permute-done.8.across), channel_id=1, source_target_pairs={{0,2},{2,0},{4,6},{6,4},{1,3},{3,1},{5,7},{7,5},{8,10},{10,8},{12,... | collective-permute-start | bytes 786440 | tf_op jit(solution)/shard_map/ge_z3/ppermute | solution.py:18
  76.1 2.9 %collective-permute-start.17 = (bf16[1024,256]{1,0:T(8,128)(2,1)S(1)}, bf16[1024,256]{1,0:T(8,128)(2,1)S(1)}, u32[]{:S(2)}, u32[]{:S(2)}) collective-permute-start(bf16[1024,256]{1,0:T(8,128)(2,1)S(1)} %get-tuple-element.81), channel_id=1, source_target_pairs={{0,8},{8,0},{16,24},{24,16},{1,9},{9,1},{17,25},{25,17},{2,10},{10... | collective-permute-start | bytes 1572872 | tf_op jit(solution)/shard_map/book_core/ppermute | solution.py:18
  77.5 11.7 %collective-permute-start.18 = (bf16[3,3,64,384]{3,2,1,0:T(8,128)(2,1)S(1)}, bf16[3,3,64,384]{3,2,1,0:T(8,128)(2,1)S(1)}, u32[]{:S(2)}, u32[]{:S(2)}) collective-permute-start(bf16[3,3,64,384]{3,2,1,0:T(8,128)(2,1)S(1)} %get-tuple-element.84), channel_id=1, source_target_pairs={{0,1},{1,0},{2,3},{3,2},{4,5},{5,4},{6,7},{7,6},{8,9},{9,8},{10,11... | collective-permute-start | bytes 1327112 | tf_op jit(solution)/shard_map/grads_a2/ppermute | solution.py:18
  77.7 11.5 %collective-permute-start.19 = (bf16[3,3,64,384]{3,2,1,0:T(8,128)(2,1)S(1)}, bf16[3,3,64,384]{3,2,1,0:T(8,128)(2,1)S(1)}, u32[]{:S(2)}, u32[]{:S(2)}) collective-permute-start(bf16[3,3,64,384]{3,2,1,0:T(8,128)(2,1)S(1)} %bitcast.27), channel_id=1, source_target_pairs={{0,16},{8,24},{16,0},{24,8},{1,17},{9,25},{17,1},{25,9},{2,18},{10... | collective-permute-start | bytes 1327112 | tf_op jit(solution)/shard_map/grads_b2/ppermute | solution.py:18
  79.2 15.6 %collective-permute-start.23 = (bf16[512,256]{1,0:T(8,128)(2,1)S(1)}, bf16[512,256]{1,0:T(8,128)(2,1)S(1)}, u32[]{:S(2)}, u32[]{:S(2)}) collective-permute-start(bf16[512,256]{1,0:T(8,128)(2,1)S(1)} %get-tuple-element.92.refs_0_), channel_id=1, source_target_pairs={{0,16},{8,24},{16,0},{24,8},{1,17},{9,25},{17,1},{25,9},{2,18},{10... | collective-permute-start | bytes 786440 | tf_op jit(solution)/shard_map/book_a/ppermute | solution.py:18
  79.4 15.5 %collective-permute-start.24 = (bf16[512,256]{1,0:T(8,128)(2,1)S(1)}, bf16[512,256]{1,0:T(8,128)(2,1)S(1)}, u32[]{:S(2)}, u32[]{:S(2)}) collective-permute-start(bf16[512,256]{1,0:T(8,128)(2,1)S(1)} %get-tuple-element.93.refs_2_), channel_id=1, source_target_pairs={{0,1},{1,0},{2,3},{3,2},{4,5},{5,4},{6,7},{7,6},{8,9},{9,8},{10,11... | collective-permute-start | bytes 786440 | tf_op jit(solution)/shard_map/book_b/ppermute | solution.py:18
  89.5 13.2 %collective-permute-start.20 = (bf16[3,3,16,768]{3,2,1,0:T(8,128)(2,1)S(1)}, bf16[3,3,16,768]{3,2,1,0:T(8,128)(2,1)S(1)}, u32[]{:S(2)}, u32[]{:S(2)}) collective-permute-start(bf16[3,3,16,768]{3,2,1,0:T(8,128)(2,1)S(1)} %get-tuple-element.88), channel_id=1, source_target_pairs={{0,4},{2,6},{4,0},{6,2},{1,5},{3,7},{5,1},{7,3},{8,12},{10,14},{12... | collective-permute-start | bytes 663560 | tf_op jit(solution)/shard_map/grads_z/ppermute | solution.py:18
  91.4 11.3 %collective-permute-start.21 = (bf16[3,3,16,768]{3,2,1,0:T(8,128)(2,1)S(1)}, bf16[3,3,16,768]{3,2,1,0:T(8,128)(2,1)S(1)}, u32[]{:S(2)}, u32[]{:S(2)}) collective-permute-start(bf16[3,3,16,768]{3,2,1,0:T(8,128)(2,1)S(1)} %get-tuple-element.89), channel_id=1, source_target_pairs={{0,2},{2,0},{4,6},{6,4},{1,3},{3,1},{5,7},{7,5},{8,10},{10,8},{12,... | collective-permute-start | bytes 663560 | tf_op jit(solution)/shard_map/grads_z/ppermute | solution.py:18
  91.4 20.6 %collective-permute-start.22 = (bf16[3,3,16,768]{3,2,1,0:T(8,128)(2,1)S(1)}, bf16[3,3,16,768]{3,2,1,0:T(8,128)(2,1)S(1)}, u32[]{:S(2)}, u32[]{:S(2)}) collective-permute-start(bf16[3,3,16,768]{3,2,1,0:T(8,128)(2,1)S(1)} %get-tuple-element.90), channel_id=1, source_target_pairs={{0,6},{2,4},{4,2},{6,0},{1,7},{3,5},{5,3},{7,1},{8,14},{10,12},{12... | collective-permute-start | bytes 663560 | tf_op jit(solution)/shard_map/grads_z/ppermute | solution.py:18
  95.0 17.1 %collective-permute-start.25 = (bf16[512,256]{1,0:T(8,128)(2,1)S(1)}, bf16[512,256]{1,0:T(8,128)(2,1)S(1)}, u32[]{:S(2)}, u32[]{:S(2)}) collective-permute-start(bf16[512,256]{1,0:T(8,128)(2,1)S(1)} %get-tuple-element.94.refs_0_), channel_id=1, source_target_pairs={{0,1},{1,0},{2,3},{3,2},{4,5},{5,4},{6,7},{7,6},{8,9},{9,8},{10,11... | collective-permute-start | bytes 786440 | tf_op jit(solution)/shard_map/book_a/ppermute | solution.py:18
  96.2 15.9 %collective-permute-start.26 = (bf16[512,256]{1,0:T(8,128)(2,1)S(1)}, bf16[512,256]{1,0:T(8,128)(2,1)S(1)}, u32[]{:S(2)}, u32[]{:S(2)}) collective-permute-start(bf16[512,256]{1,0:T(8,128)(2,1)S(1)} %get-tuple-element.95.refs_2_), channel_id=1, source_target_pairs={{0,16},{8,24},{16,0},{24,8},{1,17},{9,25},{17,1},{25,9},{2,18},{10... | collective-permute-start | bytes 786440 | tf_op jit(solution)/shard_map/book_b/ppermute | solution.py:18
  112.3 2.1 %collective-permute-start.27 = (bf16[1024,256]{1,0:T(8,128)(2,1)S(1)}, bf16[1024,256]{1,0:T(8,128)(2,1)S(1)}, u32[]{:S(2)}, u32[]{:S(2)}) collective-permute-start(bf16[1024,256]{1,0:T(8,128)(2,1)S(1)} %shard_map.97), channel_id=1, source_target_pairs={{0,8},{8,0},{16,24},{24,16},{1,9},{9,1},{17,25},{25,17},{2,10},{10... | collective-permute-start | bytes 1572872 | tf_op jit(solution)/shard_map/book_back/ppermute | solution.py:18

commit v6 on v5

--- a/solution.py
+++ b/solution.py
@@ -176,9 +176,9 @@
 
 
 def head_body(
-    breadth, info, low, top, inner, bottom, high, kernel, grad_hidden, hidden, own_pre, field, grad, padded, grad_pre
+    breadth, info, low, top, inner, bottom, high, kernel, grad_hidden, hidden, own_pre, field, grad_pre, padded
 ):
-    cells = grad.shape[0]
+    cells = own_pre.shape[0]
     tall = hidden.shape[0]
     at = 0
     for part in (low, top, inner, bottom, high):
@@ -200,6 +200,10 @@
     slope = grad_hidden[...] * (sigma * (1.0 + pre * (1.0 - sigma)))
     grad_pre[...] = jnp.where(inside, slope, 0.0).astype(NARROW)
     own_pre[...] = grad_pre[breadth : breadth + cells]
+
+
+def embedded_body(breadth, grad_pre, kernel, grad):
+    cells = grad.shape[0]
     total = sum(
         step_columns(
             sum(
@@ -216,6 +220,16 @@
     grad[...] = total.astype(NARROW)
 
 
+def embedded_grad(grad_pre, kernel, breadth):
+    cells = grad_pre.shape[0] - 2 * breadth
+    return call(
+        functools.partial(embedded_body, breadth),
+        (grad_pre, kernel),
+        [((cells, kernel.shape[2]), NARROW)],
+        2 * cells * kernel.size,
+    )[0]
+
+
 def head(info, parts, kernel, grad_hidden, breadth):
     inputs = parts[0].shape[1]
     tall, width = grad_hidden.shape
@@ -223,9 +237,9 @@
     return call(
         functools.partial(head_body, breadth),
         (info, *parts, kernel, grad_hidden),
-        [((tall, width), NARROW), ((cells, width), NARROW), ((tall, inputs), NARROW), ((cells, inputs), NARROW)],
+        [((tall, width), NARROW), ((cells, width), NARROW), ((tall, inputs), NARROW), ((tall, width), NARROW)],
         4 * cells * kernel.size,
-        [pltpu.VMEM((tall + 2 * breadth, inputs), NARROW), pltpu.VMEM((tall, width), NARROW)],
+        [pltpu.VMEM((tall + 2 * breadth, inputs), NARROW)],
         spaces=(pltpu.SMEM,) + (pltpu.VMEM,) * 7,
     )
 
@@ -534,12 +548,10 @@
     far_up = swap(after(own_up, top), "space", 1, "cot_core")
     grad_hidden = upstream_back(upstream, cot_low, cot_high, kernel_two, breadth)
     inner = plus(after(own, top, bottom), near[2 * edge :], far)
-    hidden, own_pre, field, grad_embedded = head(
+    hidden, own_pre, field, grad_pre = head(
         info, (low, top, inner, bottom, high), kernel_one, grad_hidden, breadth
     )
 
-    across = swap(grad_embedded, "code", 2, "ge_z2")
-    beside = swap(grad_embedded, "code", 1, "ge_z1")
     far_hidden = swap(hidden, "space", 1, "hidden_core")
     far_pre = swap(own_pre, "space", 1, "pre_core")
     far_field = swap(field, "space", 1, "field_core")
@@ -550,7 +562,9 @@
         breadth,
         parts,
     )
-    across, beside = after((across, beside), grads[0])
+    grad_embedded = embedded_grad(after(grad_pre, grads[0]), kernel_one, breadth)
+    across = swap(grad_embedded, "code", 2, "ge_z2")
+    beside = swap(grad_embedded, "code", 1, "ge_z1")
     grads = Spread(grads, "grads")
     corner = swap(across, "code", 1, "ge_z3")
     term = book_start(info, weights, grad_embedded, beside, across)

time: 116 us -> 116 us (level)
    pallas_call x12 -> x13, Pallas kernels: 21.9 us -> 21.7 us  [call(): pl.pallas_call(body, in_specs=[pl.BlockSpec(memory_space=space) for space...]
  transfers between devices with their start and end apart: 28 -> 28, of which waited for: 9 -> 8; matrix products, arithmetic and copies ran while one was open for 4% -> 4% of each run, Pallas kernels for 17% -> 19%
where the time goes in v6:
time: 116 us
  waiting for transfers between devices  39.4 us (34%)
  starting transfers between devices  36.2 us (31%)
  Pallas kernels  32.5 us (28%)
  other arithmetic  5.94 us (5%)
    ppermute x24, waiting for transfers between devices, swap(): lax.ppermute(value, axis, [(i, i ^ bits) for i in range(lax.axis_size(axi...  39.4 us
    ppermute x24, starting transfers between devices, swap(): lax.ppermute(value, axis, [(i, i ^ bits) for i in range(lax.axis_size(axi...  23.2 us
    pallas_call x13, Pallas kernels, call(): pl.pallas_call(body, in_specs=[pl.BlockSpec(memory_space=space) for space...  21.7 us
    pallas_call x2, Pallas kernels, lookup(): pl.pallas_call(functools.partial(lookup_body, count, edge), grid_spec=plt...  10.8 us
    ppermute x2, starting transfers between devices, edges(): high = lax.ppermute(top, axes, backward)  6.54 us
    ppermute x2, starting transfers between devices, edges(): low = lax.ppermute(bottom, axes, forward)  6.44 us
    convert_element_type x4, other arithmetic, plus(): return sum((term.astype(WIDE) for term in terms)).astype(NARROW)  2.72 us
  transfers between devices with their start and end apart: 28, of which 8 were waited for; matrix products, arithmetic and copies ran while one was open for 4% of the time, Pallas kernels for 19%

profile of v6, /device:TPU:9, one launch (start us, length us, event | category | flops | bytes accessed | tf_op | source)
XLA Modules:
  0.0 115.8 jit_solution(9326254820008044756)
XLA Ops:
  0.6 0.7 stack.34.order.info.refs_0_
  1.3 3.7 %shard_map.84 = bf16[512,256]{1,0:T(8,128)(2,1)} custom-call(s32[10]{0:T(128)} %stack.34.order.info.refs_0_, bf16[2048,2048]{1,0:T(8,128)(2,1)} %bitcast.14, bf16[2048,256]{1,0:T(8,128)(2,1)} %codebook.2), custom_call_target="tpu_custom_call" | custom-call | flops 67108864 | bytes 1 | tf_op jit(solution)/shard_map/pallas_call | solution.py:131
  5.1 0.0 copy-start.1
  5.1 0.0 slice-start.3
  5.1 7.1 %shard_map.85 = (bf16[512,256]{1,0:T(8,128)(2,1)}, bf16[128,256]{1,0:T(8,128)(2,1)}, bf16[384,256]{1,0:T(8,128)(2,1)}, bf16[128,256]{1,0:T(8,128)(2,1)}, bf16[384,256]{1,0:T(8,128)(2,1)}) custom-call(s32[10]{0:T(128)} %stack.34.order.info.refs_0_, bf16[2048,2048]{1,0:T(8,128)(2,1)} %bitcast.15, bf16[2048,256]{1,0:T(8,128)(2,1)} %codebook.2), custom_call_target="tpu_custom_call" | custom-call | flops 201326592 | bytes 1 | tf_op jit(solution)/shard_map/pallas_call | solution.py:131
  12.1 0.1 fusion.pick
  12.3 1.5 %collective-permute-start = (bf16[512,256]{1,0:T(8,128)(2,1)}, bf16[512,256]{1,0:T(8,128)(2,1)S(1)}, u32[]{:S(2)}, u32[]{:S(2)}) collective-permute-start(bf16[512,256]{1,0:T(8,128)(2,1)} %get-tuple-element.57), channel_id=1, source_target_pairs={{0,2},{2,0},{4,6},{6,4},{1,3},{3,1},{5,7},{7,5},{8,10},{10,8},{12,... | collective-permute-start | bytes 786440 | tf_op jit(solution)/shard_map/look_near/ppermute | solution.py:18
  13.8 0.9 add_convert_fusion.2
  14.7 2.4 %collective-permute-start.2 = (bf16[128,256]{1,0:T(8,128)(2,1)S(1)}, bf16[128,256]{1,0:T(8,128)(2,1)S(1)}, u32[]{:S(2)}, u32[]{:S(2)}) collective-permute-start(bf16[128,256]{1,0:T(8,128)(2,1)S(1)} %add_convert_fusion.2), channel_id=1, source_target_pairs={{0,4},{2,6},{4,0},{6,2},{1,5},{3,7},{5,1},{7,3},{8,12},{10,14},{12... | collective-permute-start | bytes 196616 | tf_op jit(solution)/shard_map/look_ends/ppermute | solution.py:18
  17.0 1.0 add_convert_fusion.1
  18.0 0.1 collective-permute-start.4
  18.1 2.0 %collective-permute-start.7 = (bf16[64,512]{1,0:T(8,128)(2,1)S(1)}, bf16[64,512]{1,0:T(8,128)(2,1)S(1)}, u32[]{:S(2)}, u32[]{:S(2)}) collective-permute-start(bf16[64,512]{1,0:T(8,128)(2,1)S(1)} %get-tuple-element.96), channel_id=1, source_target_pairs={{2,0},{4,2},{6,4},{8,6},{10,8},{12,10},{14,12},{16,14},{18,16},{20... | collective-permute-start | bytes 196616 | tf_op jit(solution)/shard_map/cot_edge/ppermute | solution.py:36
  20.2 3.2 %collective-permute-start.6 = (bf16[64,512]{1,0:T(8,128)(2,1)S(1)}, bf16[64,512]{1,0:T(8,128)(2,1)S(1)}, u32[]{:S(2)}, u32[]{:S(2)}) collective-permute-start(bf16[64,512]{1,0:T(8,128)(2,1)S(1)} %get-tuple-element.97), channel_id=1, source_target_pairs={{0,2},{2,4},{4,6},{6,8},{8,10},{10,12},{12,14},{14,16},{16,18},{18... | collective-permute-start | bytes 196616 | tf_op jit(solution)/shard_map/cot_edge/ppermute | solution.py:35
  23.5 0.8 add_convert_fusion.3
  24.3 3.2 %collective-permute-start.3 = (bf16[64,256]{1,0:T(8,128)(2,1)S(1)}, bf16[64,256]{1,0:T(8,128)(2,1)S(1)}, u32[]{:S(2)}, u32[]{:S(2)}) collective-permute-start(bf16[64,256]{1,0:T(8,128)(2,1)S(1)} %get-tuple-element.103.bottom), channel_id=1, source_target_pairs={{0,2},{2,4},{4,6},{6,8},{8,10},{10,12},{12,14},{14,16},{16,18},{18... | collective-permute-start | bytes 98312 | tf_op jit(solution)/shard_map/embed_edge/ppermute | solution.py:35
  27.5 0.0 copy-start
  27.5 4.5 %collective-permute-start.5 = (bf16[64,256]{1,0:T(8,128)(2,1)S(1)}, bf16[64,256]{1,0:T(8,128)(2,1)S(1)}, u32[]{:S(2)}, u32[]{:S(2)}) collective-permute-start(bf16[64,256]{1,0:T(8,128)(2,1)S(1)} %get-tuple-element.102.top), channel_id=1, source_target_pairs={{2,0},{4,2},{6,4},{8,6},{10,8},{12,10},{14,12},{16,14},{18,16},{20... | collective-permute-start | bytes 98312 | tf_op jit(solution)/shard_map/embed_edge/ppermute | solution.py:36
  32.1 3.0 %shard_map.86.grad_hidden = f32[576,512]{1,0:T(8,128)S(1)} custom-call(bf16[512,512]{1,0:T(8,128)(2,1)S(1)} %bitcast.23, bf16[64,512]{1,0:T(8,128)(2,1)S(1)} %collective-permute-done.6.low, bf16[64,512]{1,0:T(8,128)(2,1)S(1)} %collective-permute-done.7.high, bf16[3,3,512,512]{3,2,1,0:T(8,128)(2,1)S(1)} %bitcast.21), custom_call_target="tpu_custom_call" | custom-call | flops 301989888 | bytes 1 | tf_op jit(solution)/shard_map/pallas_call | solution.py:59
  35.0 0.1 add_convert_fusion.inner
  35.2 2.6 %shard_map.87 = (bf16[576,512]{1,0:T(8,128)(2,1)S(1)}, bf16[512,512]{1,0:T(8,128)(2,1)S(1)}, bf16[576,256]{1,0:T(8,128)(2,1)S(1)}, bf16[576,512]{1,0:T(8,128)(2,1)S(1)}) custom-call(s32[10]{0:T(128)S(1)} %copy-done.2, bf16[64,256]{1,0:T(8,128)(2,1)S(1)} %collective-permute-done.3.low, bf16[64,256]{1,0:T(8,128)(2,1)S(1)} %get-tuple-element.102.top, ...), custom_call_target="tpu_custom_call" | custom-call | flops 301989888 | bytes 1 | tf_op jit(solution)/shard_map/pallas_call | solution.py:59
  37.8 2.6 %collective-permute-start.10 = (bf16[576,512]{1,0:T(8,128)(2,1)S(1)}, bf16[576,512]{1,0:T(8,128)(2,1)S(1)}, u32[]{:S(2)}, u32[]{:S(2)}) collective-permute-start(bf16[576,512]{1,0:T(8,128)(2,1)S(1)} %get-tuple-element.81.hidden), channel_id=1, source_target_pairs={{0,8},{8,0},{16,24},{24,16},{1,9},{9,1},{17,25},{25,17},{2,10},{10... | collective-permute-start | bytes 1769480 | tf_op jit(solution)/shard_map/hidden_core/ppermute | solution.py:18
  40.4 0.1 collective-permute-start.8
  40.5 0.4 collective-permute-start.9
  40.9 0.1 collective-permute-start.11
  41.0 3.1 %shard_map.88.base = f32[3,768,768]{2,1,0:T(8,128)S(1)} custom-call(bf16[256,512]{1,0:T(8,128)(2,1)S(1)} %fusion.pick, bf16[512,512]{1,0:T(8,128)(2,1)S(1)} %bitcast.25, bf16[512,512]{1,0:T(8,128)(2,1)S(1)} %get-tuple-element.69.pre, bf16[576,512]{1,0:T(8,128)(2,1)S(1)} %get-tuple-element.81.hidden, bf16[576,256]{1,0:T(8,128)(2,1)S(1)} %get-tuple-element.70.field), custom_call_target="tpu_custom_call" | custom-call | flops 226492416 | bytes 1 | tf_op jit(solution)/shard_map/pallas_call | solution.py:59
  44.1 0.0 slice-start.1
  44.2 3.1 %shard_map.89 = (bf16[3,3,128,384]{3,2,1,0:T(8,128)(2,1)S(1)}, bf16[1,3,3,128,384]{4,3,2,1,0:T(8,128)(2,1)S(1)}, bf16[3,3,2,64,384]{4,3,2,1,0:T(8,128)(2,1)S(1)}, bf16[3,3,2,64,384]{4,3,2,1,0:T(8,128)(2,1)S(1)}) custom-call(bf16[256,512]{1,0:T(8,128)(2,1)S(1)} %fusion.pick, bf16[512,512]{1,0:T(8,128)(2,1)S(1)} %collective-permute-done.8.up, ...), custom_call_target="tpu_custom_call" | custom-call | flops 226492416 | bytes 1 | tf_op jit(solution)/shard_map/pallas_call | solution.py:59
  47.3 1.2 %collective-permute-start.15 = (bf16[3,3,2,64,384]{4,3,2,1,0:T(8,128)(2,1)S(1)}, bf16[3,3,2,64,384]{4,3,2,1,0:T(8,128)(2,1)S(1)}, u32[]{:S(2)}, u32[]{:S(2)}) collective-permute-start(bf16[3,3,2,64,384]{4,3,2,1,0:T(8,128)(2,1)S(1)} %get-tuple-element.74), channel_id=1, source_target_pairs={{0,1},{1,0},{2,3},{3,2},{4,5},{5,4},{6,7},{7,6},{8,9},{9,8},{10,11... | collective-permute-start | bytes 2654216 | tf_op jit(solution)/shard_map/grads_b1/ppermute | solution.py:18
  48.5 2.0 %collective-permute-start.16 = (bf16[3,3,128,384]{3,2,1,0:T(8,128)(2,1)S(1)}, bf16[3,3,128,384]{3,2,1,0:T(8,128)(2,1)S(1)}, u32[]{:S(2)}, u32[]{:S(2)}) collective-permute-start(bf16[3,3,128,384]{3,2,1,0:T(8,128)(2,1)S(1)} %bitcast.26), channel_id=1, source_target_pairs={{0,16},{8,24},{16,0},{24,8},{1,17},{9,25},{17,1},{25,9},{2,18},{10... | collective-permute-start | bytes 2654216 | tf_op jit(solution)/shard_map/grads_a1/ppermute | solution.py:18
  50.5 1.4 %shard_map.90.own = bf16[512,256]{1,0:T(8,128)(2,1)S(1)} custom-call(bf16[576,512]{1,0:T(8,128)(2,1)S(1)} %get-tuple-element.72.grad_pre, bf16[3,3,256,512]{3,2,1,0:T(8,128)(2,1)S(1)} %copy-done), custom_call_target="tpu_custom_call" | custom-call | flops 150994944 | bytes 1 | tf_op jit(solution)/shard_map/pallas_call | solution.py:59
  51.9 2.8 %collective-permute-start.12 = (bf16[512,256]{1,0:T(8,128)(2,1)S(1)}, bf16[512,256]{1,0:T(8,128)(2,1)S(1)}, u32[]{:S(2)}, u32[]{:S(2)}) collective-permute-start(bf16[512,256]{1,0:T(8,128)(2,1)S(1)} %shard_map.90.own), channel_id=1, source_target_pairs={{0,4},{2,6},{4,0},{6,2},{1,5},{3,7},{5,1},{7,3},{8,12},{10,14},{12... | collective-permute-start | bytes 786440 | tf_op jit(solution)/shard_map/ge_z2/ppermute | solution.py:18
  54.7 0.2 collective-permute-start.14
  54.9 11.4 %collective-permute-done.12.across = bf16[512,256]{1,0:T(8,128)(2,1)S(1)} collective-permute-done((bf16[512,256]{1,0:T(8,128)(2,1)S(1)}, bf16[512,256]{1,0:T(8,128)(2,1)S(1)}, u32[]{:S(2)}, u32[]{:S(2)}) %collective-permute-start.12) | collective-permute-done | bytes 262176 | tf_op jit(solution)/shard_map/ge_z2/ppermute | solution.py:18
  66.2 2.0 %collective-permute-start.13 = (bf16[512,256]{1,0:T(8,128)(2,1)S(1)}, bf16[512,256]{1,0:T(8,128)(2,1)S(1)}, u32[]{:S(2)}, u32[]{:S(2)}) collective-permute-start(bf16[512,256]{1,0:T(8,128)(2,1)S(1)} %collective-permute-done.12.across), channel_id=1, source_target_pairs={{0,2},{2,0},{4,6},{6,4},{1,3},{3,1},{5,7},{7,5},{8,10},{10,8},{12,... | collective-permute-start | bytes 786440 | tf_op jit(solution)/shard_map/ge_z3/ppermute | solution.py:18
  68.3 2.6 %shard_map.91.refs_3_ = f32[2048,256]{1,0:T(8,128)S(1)} custom-call(s32[10]{0:T(128)S(1)} %copy-done.2, bf16[2048,2048]{1,0:T(8,128)(2,1)S(1)} %bitcast.18, bf16[512,256]{1,0:T(8,128)(2,1)S(1)} %shard_map.90.own, bf16[512,256]{1,0:T(8,128)(2,1)S(1)} %collective-permute-done.14.beside, bf16[512,256]{1,0:T(8,128)(2,1)S(1)} %collective-permute-done.12.across), custom_call_target="tpu_custom_call" | custom-call | flops 201326592 | bytes 1 | tf_op jit(solution)/shard_map/pallas_call | solution.py:59
  70.9 0.4 shard_map.92
  71.4 3.1 %collective-permute-done.13.refs_2_ = bf16[512,256]{1,0:T(8,128)(2,1)S(1)} collective-permute-done((bf16[512,256]{1,0:T(8,128)(2,1)S(1)}, bf16[512,256]{1,0:T(8,128)(2,1)S(1)}, u32[]{:S(2)}, u32[]{:S(2)}) %collective-permute-start.13) | collective-permute-done | bytes 262176 | tf_op jit(solution)/shard_map/ge_z3/ppermute | solution.py:18
  74.5 1.5 %shard_map.93 = (bf16[1024,256]{1,0:T(8,128)(2,1)S(1)}, bf16[1024,256]{1,0:T(8,128)(2,1)S(1)}) custom-call(s32[10]{0:T(128)S(1)} %copy-done.2, bf16[2048,2048]{1,0:T(8,128)(2,1)S(1)} %bitcast.19, bf16[512,256]{1,0:T(8,128)(2,1)S(1)} %collective-permute-done.13.refs_2_, f32[2048,256]{1,0:T(8,128)S(1)} %shard_map.91.refs_3_), custom_call_target="tpu_custom_call" | custom-call | flops 100000000 | bytes 1 | tf_op jit(solution)/shard_map/pallas_call | solution.py:59
  76.0 1.2 %collective-permute-start.17 = (bf16[1024,256]{1,0:T(8,128)(2,1)S(1)}, bf16[1024,256]{1,0:T(8,128)(2,1)S(1)}, u32[]{:S(2)}, u32[]{:S(2)}) collective-permute-start(bf16[1024,256]{1,0:T(8,128)(2,1)S(1)} %get-tuple-element.79), channel_id=1, source_target_pairs={{0,8},{8,0},{16,24},{24,16},{1,9},{9,1},{17,25},{25,17},{2,10},{10... | collective-permute-start | bytes 1572872 | tf_op jit(solution)/shard_map/book_core/ppermute | solution.py:18
  77.1 0.2 collective-permute-start.18
  77.4 1.3 %collective-permute-done.17.refs_1_ = bf16[1024,256]{1,0:T(8,128)(2,1)S(1)} collective-permute-done((bf16[1024,256]{1,0:T(8,128)(2,1)S(1)}, bf16[1024,256]{1,0:T(8,128)(2,1)S(1)}, u32[]{:S(2)}, u32[]{:S(2)}) %collective-permute-start.17) | collective-permute-done | bytes 524320 | tf_op jit(solution)/shard_map/book_core/ppermute | solution.py:18
  78.7 0.1 shard_map.94
  78.8 0.3 collective-permute-start.24
  79.1 1.2 %collective-permute-start.23 = (bf16[512,256]{1,0:T(8,128)(2,1)S(1)}, bf16[512,256]{1,0:T(8,128)(2,1)S(1)}, u32[]{:S(2)}, u32[]{:S(2)}) collective-permute-start(bf16[512,256]{1,0:T(8,128)(2,1)S(1)} %get-tuple-element.90.refs_0_), channel_id=1, source_target_pairs={{0,16},{8,24},{16,0},{24,8},{1,17},{9,25},{17,1},{25,9},{2,18},{10... | collective-permute-start | bytes 786440 | tf_op jit(solution)/shard_map/book_a/ppermute | solution.py:18
  80.3 3.4 %shard_map.95 = bf16[512,512]{1,0:T(8,128)(2,1)} custom-call(bf16[576,512]{1,0:T(8,128)(2,1)S(1)} %get-tuple-element.81.hidden, bf16[3,3,512,512]{3,2,1,0:T(8,128)(2,1)S(1)} %bitcast.21), custom_call_target="tpu_custom_call" | custom-call | flops 301989888 | bytes 1 | tf_op jit(solution)/shard_map/pallas_call | solution.py:59
  83.7 5.2 %collective-permute-done.18.refs_1_ = bf16[3,3,64,384]{3,2,1,0:T(8,128)(2,1)S(1)} collective-permute-done((bf16[3,3,64,384]{3,2,1,0:T(8,128)(2,1)S(1)}, bf16[3,3,64,384]{3,2,1,0:T(8,128)(2,1)S(1)}, u32[]{:S(2)}, u32[]{:S(2)}) %collective-permute-start.18) | collective-permute-done | bytes 442400 | tf_op jit(solution)/shard_map/grads_a2/ppermute | solution.py:18
  88.9 0.2 shard_map.96
  89.1 2.6 %collective-permute-start.20 = (bf16[3,3,16,768]{3,2,1,0:T(8,128)(2,1)S(1)}, bf16[3,3,16,768]{3,2,1,0:T(8,128)(2,1)S(1)}, u32[]{:S(2)}, u32[]{:S(2)}) collective-permute-start(bf16[3,3,16,768]{3,2,1,0:T(8,128)(2,1)S(1)} %get-tuple-element.86), channel_id=1, source_target_pairs={{0,4},{2,6},{4,0},{6,2},{1,5},{3,7},{5,1},{7,3},{8,12},{10,14},{12... | collective-permute-start | bytes 663560 | tf_op jit(solution)/shard_map/grads_z/ppermute | solution.py:18
  91.7 0.0 collective-permute-start.21
  91.7 0.4 collective-permute-start.22
  92.0 2.5 %collective-permute-done.24.refs_3_ = bf16[512,256]{1,0:T(8,128)(2,1)S(1)} collective-permute-done((bf16[512,256]{1,0:T(8,128)(2,1)S(1)}, bf16[512,256]{1,0:T(8,128)(2,1)S(1)}, u32[]{:S(2)}, u32[]{:S(2)}) %collective-permute-start.24) | collective-permute-done | bytes 262176 | tf_op jit(solution)/shard_map/book_b/ppermute | solution.py:18
  94.5 0.1 shard_map.97
  94.6 1.2 %collective-permute-start.25 = (bf16[512,256]{1,0:T(8,128)(2,1)S(1)}, bf16[512,256]{1,0:T(8,128)(2,1)S(1)}, u32[]{:S(2)}, u32[]{:S(2)}) collective-permute-start(bf16[512,256]{1,0:T(8,128)(2,1)S(1)} %get-tuple-element.92.refs_0_), channel_id=1, source_target_pairs={{0,1},{1,0},{2,3},{3,2},{4,5},{5,4},{6,7},{7,6},{8,9},{9,8},{10,11... | collective-permute-start | bytes 786440 | tf_op jit(solution)/shard_map/book_a/ppermute | solution.py:18
  95.8 0.1 collective-permute-start.26
  96.0 7.0 %collective-permute-done.20 = bf16[3,3,16,768]{3,2,1,0:T(8,128)(2,1)S(1)} collective-permute-done((bf16[3,3,16,768]{3,2,1,0:T(8,128)(2,1)S(1)}, bf16[3,3,16,768]{3,2,1,0:T(8,128)(2,1)S(1)}, u32[]{:S(2)}, u32[]{:S(2)}) %collective-permute-start.20) | collective-permute-done | bytes 221216 | tf_op jit(solution)/shard_map/grads_z/ppermute | solution.py:18
  103.0 8.9 %collective-permute-done.22 = bf16[3,3,16,768]{3,2,1,0:T(8,128)(2,1)S(1)} collective-permute-done((bf16[3,3,16,768]{3,2,1,0:T(8,128)(2,1)S(1)}, bf16[3,3,16,768]{3,2,1,0:T(8,128)(2,1)S(1)}, u32[]{:S(2)}, u32[]{:S(2)}) %collective-permute-start.22) | collective-permute-done | bytes 221216 | tf_op jit(solution)/shard_map/grads_z/ppermute | solution.py:18
  111.8 0.1 add_bitcast_fusion
  112.0 0.1 shard_map.98
  112.1 0.6 collective-permute-start.27
  112.7 0.7 pad_maximum_fusion.1
  113.4 0.7 pad_maximum_fusion
  114.1 0.1 collective-permute-done.27
  114.2 0.1 broadcast_select_fusion.1
  114.3 1.5 %maximum_convert_fusion = f32[2048,256]{1,0:T(8,128)} fusion(bf16[1024,256]{1,0:T(8,128)(2,1)S(1)} %get-tuple-element.95, bf16[1024,256]{1,0:T(8,128)(2,1)S(1)} %get-tuple-element.94), kind=kLoop, calls=%fused_computation | loop fusion | flops 2097152 | bytes 3145728 | tf_op jit(solution)/shard_map/convert_element_type | solution.py:599
  (40 shorter events, 0.1 us)
Async XLA Ops:
  5.0 8.7 %collective-permute-start.1 = (bf16[512,256]{1,0:T(8,128)(2,1)}, bf16[512,256]{1,0:T(8,128)(2,1)S(1)}, u32[]{:S(2)}, u32[]{:S(2)}) collective-permute-start(bf16[512,256]{1,0:T(8,128)(2,1)} %shard_map.84), channel_id=1, source_target_pairs={{0,2},{2,0},{4,6},{6,4},{1,3},{3,1},{5,7},{7,5},{8,10},{10,8},{12,... | collective-permute-start | bytes 786440 | tf_op jit(solution)/shard_map/look_z1/ppermute | solution.py:18
  5.1 27.0 %slice-start.2 = ((s8[4718592]{0:T(1024)(128)(4,1)}), s8[4194304]{0:T(1024)(128)(4,1)S(1)}, s32[]{:S(2)}) async-start(s8[4718592]{0:T(1024)(128)(4,1)} %bitcast.20), calls=%async_computation.2 | async-start | bytes 8388608
  5.1 13.1 %copy-start.1 = (bf16[1,16,32,512]{3,2,1,0:T(8,128)(2,1)S(1)}, bf16[1,16,32,512]{3,2,1,0:T(8,128)(2,1)}, u32[]{:S(2)}) copy-start(bf16[1,16,32,512]{3,2,1,0:T(8,128)(2,1)} %param.9) | copy-start | bytes 1572868
  5.1 27.0 %slice-start.3 = ((s8[4718592]{0:T(1024)(128)(4,1)}), s8[524288]{0:T(1024)(128)(4,1)S(1)}, s32[]{:S(2)}) async-start(s8[4718592]{0:T(1024)(128)(4,1)} %bitcast.20), calls=%async_computation.3 | async-start | bytes 1048576
  12.3 11.2 %collective-permute-start = (bf16[512,256]{1,0:T(8,128)(2,1)}, bf16[512,256]{1,0:T(8,128)(2,1)S(1)}, u32[]{:S(2)}, u32[]{:S(2)}) collective-permute-start(bf16[512,256]{1,0:T(8,128)(2,1)} %get-tuple-element.57), channel_id=1, source_target_pairs={{0,2},{2,0},{4,6},{6,4},{1,3},{3,1},{5,7},{7,5},{8,10},{10,8},{12,... | collective-permute-start | bytes 786440 | tf_op jit(solution)/shard_map/look_near/ppermute | solution.py:18
  14.7 8.8 %collective-permute-start.2 = (bf16[128,256]{1,0:T(8,128)(2,1)S(1)}, bf16[128,256]{1,0:T(8,128)(2,1)S(1)}, u32[]{:S(2)}, u32[]{:S(2)}) collective-permute-start(bf16[128,256]{1,0:T(8,128)(2,1)S(1)} %add_convert_fusion.2), channel_id=1, source_target_pairs={{0,4},{2,6},{4,0},{6,2},{1,5},{3,7},{5,1},{7,3},{8,12},{10,14},{12... | collective-permute-start | bytes 196616 | tf_op jit(solution)/shard_map/look_ends/ppermute | solution.py:18
  18.0 17.0 %collective-permute-start.4 = (bf16[384,256]{1,0:T(8,128)(2,1)S(1)}, bf16[384,256]{1,0:T(8,128)(2,1)S(1)}, u32[]{:S(2)}, u32[]{:S(2)}) collective-permute-start(bf16[384,256]{1,0:T(8,128)(2,1)S(1)} %add_convert_fusion.1), channel_id=1, source_target_pairs={{0,4},{2,6},{4,0},{6,2},{1,5},{3,7},{5,1},{7,3},{8,12},{10,14},{12... | collective-permute-start | bytes 589832 | tf_op jit(solution)/shard_map/look_z2/ppermute | solution.py:18
  18.1 13.9 %collective-permute-start.7 = (bf16[64,512]{1,0:T(8,128)(2,1)S(1)}, bf16[64,512]{1,0:T(8,128)(2,1)S(1)}, u32[]{:S(2)}, u32[]{:S(2)}) collective-permute-start(bf16[64,512]{1,0:T(8,128)(2,1)S(1)} %get-tuple-element.96), channel_id=1, source_target_pairs={{2,0},{4,2},{6,4},{8,6},{10,8},{12,10},{14,12},{16,14},{18,16},{20... | collective-permute-start | bytes 196616 | tf_op jit(solution)/shard_map/cot_edge/ppermute | solution.py:36
  20.2 11.8 %collective-permute-start.6 = (bf16[64,512]{1,0:T(8,128)(2,1)S(1)}, bf16[64,512]{1,0:T(8,128)(2,1)S(1)}, u32[]{:S(2)}, u32[]{:S(2)}) collective-permute-start(bf16[64,512]{1,0:T(8,128)(2,1)S(1)} %get-tuple-element.97), channel_id=1, source_target_pairs={{0,2},{2,4},{4,6},{6,8},{8,10},{10,12},{12,14},{14,16},{16,18},{18... | collective-permute-start | bytes 196616 | tf_op jit(solution)/shard_map/cot_edge/ppermute | solution.py:35
  24.3 10.9 %collective-permute-start.3 = (bf16[64,256]{1,0:T(8,128)(2,1)S(1)}, bf16[64,256]{1,0:T(8,128)(2,1)S(1)}, u32[]{:S(2)}, u32[]{:S(2)}) collective-permute-start(bf16[64,256]{1,0:T(8,128)(2,1)S(1)} %get-tuple-element.103.bottom), channel_id=1, source_target_pairs={{0,2},{2,4},{4,6},{6,8},{8,10},{10,12},{12,14},{14,16},{16,18},{18... | collective-permute-start | bytes 98312 | tf_op jit(solution)/shard_map/embed_edge/ppermute | solution.py:35
  27.5 7.6 %copy-start.3 = (bf16[384,256]{1,0:T(8,128)(2,1)S(1)}, bf16[384,256]{1,0:T(8,128)(2,1)}, u32[]{:S(2)}) copy-start(bf16[384,256]{1,0:T(8,128)(2,1)} %get-tuple-element.60) | copy-start | bytes 589828
  27.5 7.7 %copy-start = (bf16[3,3,256,512]{3,2,1,0:T(8,128)(2,1)S(1)}, bf16[3,3,256,512]{3,2,1,0:T(8,128)(2,1)}, u32[]{:S(2)}) copy-start(bf16[3,3,256,512]{3,2,1,0:T(8,128)(2,1)} %kernel.6) | copy-start | bytes 7077892
  27.5 7.7 %copy-start.2 = (s32[10]{0:T(128)S(1)}, s32[10]{0:T(128)}, u32[]{:S(2)}) copy-start(s32[10]{0:T(128)} %stack.34.order.info.refs_0_) | copy-start | bytes 124
  27.5 7.6 %collective-permute-start.5 = (bf16[64,256]{1,0:T(8,128)(2,1)S(1)}, bf16[64,256]{1,0:T(8,128)(2,1)S(1)}, u32[]{:S(2)}, u32[]{:S(2)}) collective-permute-start(bf16[64,256]{1,0:T(8,128)(2,1)S(1)} %get-tuple-element.102.top), channel_id=1, source_target_pairs={{2,0},{4,2},{6,4},{8,6},{10,8},{12,10},{14,12},{16,14},{18,16},{20... | collective-permute-start | bytes 98312 | tf_op jit(solution)/shard_map/embed_edge/ppermute | solution.py:36
  37.8 6.4 %collective-permute-start.10 = (bf16[576,512]{1,0:T(8,128)(2,1)S(1)}, bf16[576,512]{1,0:T(8,128)(2,1)S(1)}, u32[]{:S(2)}, u32[]{:S(2)}) collective-permute-start(bf16[576,512]{1,0:T(8,128)(2,1)S(1)} %get-tuple-element.81.hidden), channel_id=1, source_target_pairs={{0,8},{8,0},{16,24},{24,16},{1,9},{9,1},{17,25},{25,17},{2,10},{10... | collective-permute-start | bytes 1769480 | tf_op jit(solution)/shard_map/hidden_core/ppermute | solution.py:18
  40.4 3.8 %collective-permute-start.8 = (bf16[512,512]{1,0:T(8,128)(2,1)S(1)}, bf16[512,512]{1,0:T(8,128)(2,1)S(1)}, u32[]{:S(2)}, u32[]{:S(2)}) collective-permute-start(bf16[512,512]{1,0:T(8,128)(2,1)S(1)} %bitcast.24), channel_id=1, source_target_pairs={{0,8},{8,0},{16,24},{24,16},{1,9},{9,1},{17,25},{25,17},{2,10},{10... | collective-permute-start | bytes 1572872 | tf_op jit(solution)/shard_map/cot_core/ppermute | solution.py:18
  40.5 3.7 %collective-permute-start.9 = (bf16[512,512]{1,0:T(8,128)(2,1)S(1)}, bf16[512,512]{1,0:T(8,128)(2,1)S(1)}, u32[]{:S(2)}, u32[]{:S(2)}) collective-permute-start(bf16[512,512]{1,0:T(8,128)(2,1)S(1)} %get-tuple-element.69.pre), channel_id=1, source_target_pairs={{0,8},{8,0},{16,24},{24,16},{1,9},{9,1},{17,25},{25,17},{2,10},{10... | collective-permute-start | bytes 1572872 | tf_op jit(solution)/shard_map/pre_core/ppermute | solution.py:18
  40.9 3.2 %collective-permute-start.11 = (bf16[576,256]{1,0:T(8,128)(2,1)S(1)}, bf16[576,256]{1,0:T(8,128)(2,1)S(1)}, u32[]{:S(2)}, u32[]{:S(2)}) collective-permute-start(bf16[576,256]{1,0:T(8,128)(2,1)S(1)} %get-tuple-element.70.field), channel_id=1, source_target_pairs={{0,8},{8,0},{16,24},{24,16},{1,9},{9,1},{17,25},{25,17},{2,10},{10... | collective-permute-start | bytes 884744 | tf_op jit(solution)/shard_map/field_core/ppermute | solution.py:18
  41.0 27.3 %slice-start = ((s8[8388608]{0:T(1024)(128)(4,1)}), s8[4194304]{0:T(1024)(128)(4,1)S(1)}, s32[]{:S(2)}) async-start(s8[8388608]{0:T(1024)(128)(4,1)} %bitcast.16), calls=%async_computation | async-start | bytes 8388608
  44.1 24.2 %slice-start.1 = ((s8[8388608]{0:T(1024)(128)(4,1)}), s8[4194304]{0:T(1024)(128)(4,1)S(1)}, s32[]{:S(2)}) async-start(s8[8388608]{0:T(1024)(128)(4,1)} %bitcast.16), calls=%async_computation.1 | async-start | bytes 8388608
  47.3 23.7 %collective-permute-start.15 = (bf16[3,3,2,64,384]{4,3,2,1,0:T(8,128)(2,1)S(1)}, bf16[3,3,2,64,384]{4,3,2,1,0:T(8,128)(2,1)S(1)}, u32[]{:S(2)}, u32[]{:S(2)}) collective-permute-start(bf16[3,3,2,64,384]{4,3,2,1,0:T(8,128)(2,1)S(1)} %get-tuple-element.74), channel_id=1, source_target_pairs={{0,1},{1,0},{2,3},{3,2},{4,5},{5,4},{6,7},{7,6},{8,9},{9,8},{10,11... | collective-permute-start | bytes 2654216 | tf_op jit(solution)/shard_map/grads_b1/ppermute | solution.py:18
  48.5 22.4 %collective-permute-start.16 = (bf16[3,3,128,384]{3,2,1,0:T(8,128)(2,1)S(1)}, bf16[3,3,128,384]{3,2,1,0:T(8,128)(2,1)S(1)}, u32[]{:S(2)}, u32[]{:S(2)}) collective-permute-start(bf16[3,3,128,384]{3,2,1,0:T(8,128)(2,1)S(1)} %bitcast.26), channel_id=1, source_target_pairs={{0,16},{8,24},{16,0},{24,8},{1,17},{9,25},{17,1},{25,9},{2,18},{10... | collective-permute-start | bytes 2654216 | tf_op jit(solution)/shard_map/grads_a1/ppermute | solution.py:18
  51.9 14.3 %collective-permute-start.12 = (bf16[512,256]{1,0:T(8,128)(2,1)S(1)}, bf16[512,256]{1,0:T(8,128)(2,1)S(1)}, u32[]{:S(2)}, u32[]{:S(2)}) collective-permute-start(bf16[512,256]{1,0:T(8,128)(2,1)S(1)} %shard_map.90.own), channel_id=1, source_target_pairs={{0,4},{2,6},{4,0},{6,2},{1,5},{3,7},{5,1},{7,3},{8,12},{10,14},{12... | collective-permute-start | bytes 786440 | tf_op jit(solution)/shard_map/ge_z2/ppermute | solution.py:18
  54.7 13.6 %collective-permute-start.14 = (bf16[512,256]{1,0:T(8,128)(2,1)S(1)}, bf16[512,256]{1,0:T(8,128)(2,1)S(1)}, u32[]{:S(2)}, u32[]{:S(2)}) collective-permute-start(bf16[512,256]{1,0:T(8,128)(2,1)S(1)} %shard_map.90.own), channel_id=1, source_target_pairs={{0,2},{2,0},{4,6},{6,4},{1,3},{3,1},{5,7},{7,5},{8,10},{10,8},{12,... | collective-permute-start | bytes 786440 | tf_op jit(solution)/shard_map/ge_z1/ppermute | solution.py:18
  66.2 8.2 %collective-permute-start.13 = (bf16[512,256]{1,0:T(8,128)(2,1)S(1)}, bf16[512,256]{1,0:T(8,128)(2,1)S(1)}, u32[]{:S(2)}, u32[]{:S(2)}) collective-permute-start(bf16[512,256]{1,0:T(8,128)(2,1)S(1)} %collective-permute-done.12.across), channel_id=1, source_target_pairs={{0,2},{2,0},{4,6},{6,4},{1,3},{3,1},{5,7},{7,5},{8,10},{10,8},{12,... | collective-permute-start | bytes 786440 | tf_op jit(solution)/shard_map/ge_z3/ppermute | solution.py:18
  76.0 2.7 %collective-permute-start.17 = (bf16[1024,256]{1,0:T(8,128)(2,1)S(1)}, bf16[1024,256]{1,0:T(8,128)(2,1)S(1)}, u32[]{:S(2)}, u32[]{:S(2)}) collective-permute-start(bf16[1024,256]{1,0:T(8,128)(2,1)S(1)} %get-tuple-element.79), channel_id=1, source_target_pairs={{0,8},{8,0},{16,24},{24,16},{1,9},{9,1},{17,25},{25,17},{2,10},{10... | collective-permute-start | bytes 1572872 | tf_op jit(solution)/shard_map/book_core/ppermute | solution.py:18
  77.1 11.7 %collective-permute-start.18 = (bf16[3,3,64,384]{3,2,1,0:T(8,128)(2,1)S(1)}, bf16[3,3,64,384]{3,2,1,0:T(8,128)(2,1)S(1)}, u32[]{:S(2)}, u32[]{:S(2)}) collective-permute-start(bf16[3,3,64,384]{3,2,1,0:T(8,128)(2,1)S(1)} %get-tuple-element.82), channel_id=1, source_target_pairs={{0,1},{1,0},{2,3},{3,2},{4,5},{5,4},{6,7},{7,6},{8,9},{9,8},{10,11... | collective-permute-start | bytes 1327112 | tf_op jit(solution)/shard_map/grads_a2/ppermute | solution.py:18
  77.4 11.5 %collective-permute-start.19 = (bf16[3,3,64,384]{3,2,1,0:T(8,128)(2,1)S(1)}, bf16[3,3,64,384]{3,2,1,0:T(8,128)(2,1)S(1)}, u32[]{:S(2)}, u32[]{:S(2)}) collective-permute-start(bf16[3,3,64,384]{3,2,1,0:T(8,128)(2,1)S(1)} %bitcast.27), channel_id=1, source_target_pairs={{0,16},{8,24},{16,0},{24,8},{1,17},{9,25},{17,1},{25,9},{2,18},{10... | collective-permute-start | bytes 1327112 | tf_op jit(solution)/shard_map/grads_b2/ppermute | solution.py:18
  78.8 15.7 %collective-permute-start.24 = (bf16[512,256]{1,0:T(8,128)(2,1)S(1)}, bf16[512,256]{1,0:T(8,128)(2,1)S(1)}, u32[]{:S(2)}, u32[]{:S(2)}) collective-permute-start(bf16[512,256]{1,0:T(8,128)(2,1)S(1)} %get-tuple-element.91.refs_2_), channel_id=1, source_target_pairs={{0,1},{1,0},{2,3},{3,2},{4,5},{5,4},{6,7},{7,6},{8,9},{9,8},{10,11... | collective-permute-start | bytes 786440 | tf_op jit(solution)/shard_map/book_b/ppermute | solution.py:18
  79.1 15.4 %collective-permute-start.23 = (bf16[512,256]{1,0:T(8,128)(2,1)S(1)}, bf16[512,256]{1,0:T(8,128)(2,1)S(1)}, u32[]{:S(2)}, u32[]{:S(2)}) collective-permute-start(bf16[512,256]{1,0:T(8,128)(2,1)S(1)} %get-tuple-element.90.refs_0_), channel_id=1, source_target_pairs={{0,16},{8,24},{16,0},{24,8},{1,17},{9,25},{17,1},{25,9},{2,18},{10... | collective-permute-start | bytes 786440 | tf_op jit(solution)/shard_map/book_a/ppermute | solution.py:18
  89.1 13.9 %collective-permute-start.20 = (bf16[3,3,16,768]{3,2,1,0:T(8,128)(2,1)S(1)}, bf16[3,3,16,768]{3,2,1,0:T(8,128)(2,1)S(1)}, u32[]{:S(2)}, u32[]{:S(2)}) collective-permute-start(bf16[3,3,16,768]{3,2,1,0:T(8,128)(2,1)S(1)} %get-tuple-element.86), channel_id=1, source_target_pairs={{0,4},{2,6},{4,0},{6,2},{1,5},{3,7},{5,1},{7,3},{8,12},{10,14},{12... | collective-permute-start | bytes 663560 | tf_op jit(solution)/shard_map/grads_z/ppermute | solution.py:18
  91.7 11.3 %collective-permute-start.21 = (bf16[3,3,16,768]{3,2,1,0:T(8,128)(2,1)S(1)}, bf16[3,3,16,768]{3,2,1,0:T(8,128)(2,1)S(1)}, u32[]{:S(2)}, u32[]{:S(2)}) collective-permute-start(bf16[3,3,16,768]{3,2,1,0:T(8,128)(2,1)S(1)} %get-tuple-element.87), channel_id=1, source_target_pairs={{0,2},{2,0},{4,6},{6,4},{1,3},{3,1},{5,7},{7,5},{8,10},{10,8},{12,... | collective-permute-start | bytes 663560 | tf_op jit(solution)/shard_map/grads_z/ppermute | solution.py:18
  91.7 20.1 %collective-permute-start.22 = (bf16[3,3,16,768]{3,2,1,0:T(8,128)(2,1)S(1)}, bf16[3,3,16,768]{3,2,1,0:T(8,128)(2,1)S(1)}, u32[]{:S(2)}, u32[]{:S(2)}) collective-permute-start(bf16[3,3,16,768]{3,2,1,0:T(8,128)(2,1)S(1)} %get-tuple-element.88), channel_id=1, source_target_pairs={{0,6},{2,4},{4,2},{6,0},{1,7},{3,5},{5,3},{7,1},{8,14},{10,12},{12... | collective-permute-start | bytes 663560 | tf_op jit(solution)/shard_map/grads_z/ppermute | solution.py:18
  94.6 17.3 %collective-permute-start.25 = (bf16[512,256]{1,0:T(8,128)(2,1)S(1)}, bf16[512,256]{1,0:T(8,128)(2,1)S(1)}, u32[]{:S(2)}, u32[]{:S(2)}) collective-permute-start(bf16[512,256]{1,0:T(8,128)(2,1)S(1)} %get-tuple-element.92.refs_0_), channel_id=1, source_target_pairs={{0,1},{1,0},{2,3},{3,2},{4,5},{5,4},{6,7},{7,6},{8,9},{9,8},{10,11... | collective-permute-start | bytes 786440 | tf_op jit(solution)/shard_map/book_a/ppermute | solution.py:18
  95.8 16.1 %collective-permute-start.26 = (bf16[512,256]{1,0:T(8,128)(2,1)S(1)}, bf16[512,256]{1,0:T(8,128)(2,1)S(1)}, u32[]{:S(2)}, u32[]{:S(2)}) collective-permute-start(bf16[512,256]{1,0:T(8,128)(2,1)S(1)} %get-tuple-element.93.refs_2_), channel_id=1, source_target_pairs={{0,16},{8,24},{16,0},{24,8},{1,17},{9,25},{17,1},{25,9},{2,18},{10... | collective-permute-start | bytes 786440 | tf_op jit(solution)/shard_map/book_b/ppermute | solution.py:18
  112.1 2.1 %collective-permute-start.27 = (bf16[1024,256]{1,0:T(8,128)(2,1)S(1)}, bf16[1024,256]{1,0:T(8,128)(2,1)S(1)}, u32[]{:S(2)}, u32[]{:S(2)}) collective-permute-start(bf16[1024,256]{1,0:T(8,128)(2,1)S(1)} %shard_map.98), channel_id=1, source_target_pairs={{0,8},{8,0},{16,24},{24,16},{1,9},{9,1},{17,25},{25,17},{2,10},{10... | collective-permute-start | bytes 1572872 | tf_op jit(solution)/shard_map/book_back/ppermute | solution.py:18
